TPU v7x, 256 devices: a whole 4x4x8 slice. The times are simulated.
256 devices in a mesh: dp: 4 (over y), ctx: 64 (over x, z, core).
Axes of the slice: x: 4, y: 4, z: 8, core: 2. Of those that a mesh axis runs over, the one named last changes fastest.
Arguments:
- incoming_embeddings: float32 [4, 65536, 384], P('dp', 'ctx'), may hold values from -58 to 58
- stacked_projector: float32 [384, 1152], replicated, may hold values from -0.3125 to 0.3125
- final_projector: float32 [384, 384], replicated, may hold values from -0.3125 to 0.3125
- sharpness_per_view: float32 [8], replicated, may hold values from 0.5 to 3
- upstream_sensitivity: float32 [4, 65536, 384], P('dp', 'ctx'), may hold values from -6 to 6
Outputs:
- input_grad: float32 [4, 65536, 384], P('dp', 'ctx')
- mixer_grad: float32 [384, 1152], P('ctx')
- output_grad: float32 [384, 384], P('ctx')
- sharpness_sensitivity: float32 [8], replicated
All inputs are finite; a program needn't handle non-finite values.
Results may differ from a plain program's by a relative error of at most 0.000088.
Values sent between devices are 32-bit elements; how exact they have to be, the bound alone decides.
No kernel may reach another device: no remote copies, remote signals or barrier semaphores. Data moves between devices by JAX's collectives and lax.ppermute only.
A program may use at most 64 MiB of HBM per device.

v0:
```python
import math

import jax
import jax.numpy as jnp
from jax import lax
from jax.sharding import PartitionSpec as P

precise = lax.Precision.HIGHEST
epsilon = 1e-06


def body(
    incoming_embeddings,
    stacked_projector,
    final_projector,
    sharpness_per_view,
    upstream_sensitivity,
):
    patch_lines = incoming_embeddings[0]
    incoming = upstream_sensitivity[0]
    tokens_here = patch_lines.shape[0]
    features = patch_lines.shape[1]
    view_total = sharpness_per_view.shape[0]

    def split_heads(array):
        return array.reshape(tokens_here, view_total, -1)

    projected = jnp.dot(patch_lines, stacked_projector, precision=precise)
    queries = projected[:, :features]
    keys_part = projected[:, features : 2 * features]
    values_part = projected[:, 2 * features :]
    mixed_grad = jnp.dot(incoming, final_projector.T, precision=precise)
    local_attn = jnp.einsum(
        "nhi,nhj->hij", split_heads(mixed_grad), split_heads(values_part), precision=precise
    )
    query_square = jnp.sum(queries * queries, axis=0)
    key_square = jnp.sum(keys_part * keys_part, axis=0)
    query_total, key_total = lax.psum((query_square, key_square), "ctx")
    query_norm = jnp.sqrt(query_total + epsilon)
    key_norm = jnp.sqrt(key_total + epsilon)
    query_hat = queries / query_norm
    key_hat = keys_part / key_norm
    local_cov = jnp.einsum(
        "nhi,nhj->hij", split_heads(query_hat), split_heads(key_hat), precision=precise
    )
    feature_crosscorr, attention_grad = lax.psum((local_cov, local_attn), "ctx")
    logit_table = jnp.exp(sharpness_per_view[:, None, None] * feature_crosscorr)
    attention = logit_table / jnp.sum(logit_table, axis=-1, keepdims=True)
    mixed = jnp.einsum(
        "hij,nhj->nhi", attention, split_heads(values_part), precision=precise
    ).reshape(tokens_here, features)
    values_grad = jnp.einsum(
        "hij,nhi->nhj", attention, split_heads(mixed_grad), precision=precise
    ).reshape(tokens_here, features)
    logit_sensitivity = attention * (
        attention_grad - jnp.sum(attention * attention_grad, axis=-1, keepdims=True)
    )
    specimen_sharpness = jnp.sum(logit_sensitivity * feature_crosscorr, axis=(1, 2))
    crosscorr_sensitivity = sharpness_per_view[:, None, None] * logit_sensitivity
    qhat_grad = jnp.einsum(
        "hij,nhj->nhi", crosscorr_sensitivity, split_heads(key_hat), precision=precise
    ).reshape(tokens_here, features)
    khat_grad = jnp.einsum(
        "hij,nhi->nhj", crosscorr_sensitivity, split_heads(query_hat), precision=precise
    ).reshape(tokens_here, features)
    query_inner, key_inner = lax.psum(
        (jnp.sum(query_hat * qhat_grad, axis=0), jnp.sum(key_hat * khat_grad, axis=0)), "ctx"
    )
    queries_grad = (qhat_grad - query_hat * query_inner) / query_norm
    keys_grad = (khat_grad - key_hat * key_inner) / key_norm
    projected_grad = jnp.concatenate([queries_grad, keys_grad, values_grad], axis=1)
    input_grad = jnp.dot(projected_grad, stacked_projector.T, precision=precise)
    logit_multiplier = 1.0 / math.sqrt(lax.axis_size("dp") * lax.axis_size("ctx") * tokens_here)
    mixer_part = jnp.dot(patch_lines.T, projected_grad, precision=precise)
    output_part = jnp.dot(mixed.T, incoming, precision=precise)
    device_patch_lines = lax.psum_scatter(
        jnp.concatenate([mixer_part, output_part], axis=1) * logit_multiplier,
        "ctx",
        scatter_dimension=0,
        tiled=True,
    )
    device_patch_lines, sharpness_sensitivity = lax.psum(
        (device_patch_lines, specimen_sharpness * logit_multiplier), "dp"
    )
    return (
        input_grad[None],
        device_patch_lines[:, : 3 * features],
        device_patch_lines[:, 3 * features :],
        sharpness_sensitivity,
    )


def solution(mesh):
    return jax.shard_map(
        body,
        mesh=mesh,
        in_specs=(P("dp", "ctx", None), P(), P(), P(), P("dp", "ctx", None)),
        out_specs=(P("dp", "ctx", None), P("ctx", None), P("ctx", None), P()),
        check_vma=False,
    )
```

profile of v0, /device:TPU:4, one launch (start us, length us, event | category | flops | bytes accessed | tf_op | source)
XLA Modules:
  0.0 741.2 jit_solution(7265601830931782079)
XLA Ops:
  8.6 9.8 %fusion.8 = f32[1024,1152]{1,0:T(8,128)S(1)} fusion(f32[384,1152]{1,0:T(8,128)S(1)} %copy-done, f32[1,1024,384]{2,1,0:T(8,128)} %param.5), kind=kOutput, calls=%fused_computation.10 | convolution fusion | flops 5435817984 | bytes 8060928 | tf_op jit(solution)/shard_map/dot_general | solution.py:28
  20.9 110.5 %all-reduce.2 = (f32[384]{0:T(512)S(1)}, f32[384]{0:T(512)S(1)}) all-reduce(f32[384]{0:T(512)S(1)} %get-tuple-element.17, f32[384]{0:T(512)S(1)} %get-tuple-element.16), channel_id=1, replica_groups=mesh['dp'=4,'ctx'=64] {'ctx'}, use_global_device_ids=true, to_apply=%region_3.0 | all-reduce | flops 768 | bytes 6144 | tf_op jit(solution)/shard_map/psum | solution.py:38
  131.3 4.4 fusion.25
  135.7 3.0 copy.36
  138.7 3.0 copy.35
  143.4 4.3 fusion.3
  147.8 2.2 fusion.27
  150.2 2.2 fusion.26
  152.7 195.3 %all-reduce.10.cloned.1.call-done = (f32[8,48,48]{2,1,0:T(8,128)}, f32[8,48,48]{2,1,0:T(8,128)}) async-done(((f32[8,48,48]{2,1,0:T(8,128)}, f32[8,48,48]{2,1,0:T(8,128)}), (f32[8,48,48]{2,1,0:T(8,128)}, f32[8,48,48]{2,1,0:T(8,128)})) %all-reduce.10.cloned.1.call-update) | async-done | bytes 147472 | tf_op jit(solution)/shard_map/psum | solution.py:46
  349.1 4.4 fusion.23
  353.6 2.7 fusion.21
  356.5 2.9 fusion.11
  359.4 2.7 fusion.13
  362.1 3.0 copy.43
  365.1 5.4 fusion.5
  370.5 3.0 copy.41
  373.6 3.0 copy.38
  376.6 2.8 multiply_reduce_fusion.1
  380.3 107.4 %all-reduce.1 = (f32[384]{0:T(512)}, f32[384]{0:T(512)}) all-reduce(f32[384]{0:T(512)} %multiply_reduce_fusion, f32[384]{0:T(512)} %multiply_reduce_fusion.1), channel_id=1, replica_groups=mesh['dp'=4,'ctx'=64] {'ctx'}, use_global_device_ids=true, to_apply=%region_11.0 | all-reduce | flops 768 | bytes 6144 | tf_op jit(solution)/shard_map/psum | solution.py:66
  487.7 2.2 subtract_divide_fusion.1
  492.3 7.5 %fusion.2 = f32[384,1152]{0,1:T(8,128)S(1)} fusion(f32[1024,384]{1,0:T(8,128)S(1)} %copy-done.15, f32[1024,384]{1,0:T(8,128)S(1)} %subtract_divide_fusion, f32[1024,384]{1,0:T(8,128)S(1)} %subtract_divide_fusion.1, f32[1,1024,384]{2,1,0:T(8,128)S(1)} %copy-done.18), kind=kOutput, calls=%fused_computation.3 | convolution fusion | flops 5438177280 | bytes 8060928 | tf_op jit(solution)/shard_map/dot_general | solution.py:74
  503.6 10.9 %fusion.10 = f32[1,1024,384]{2,1,0:T(8,128)} fusion(f32[384,1152]{1,0:T(8,128)S(1)} %copy-done, f32[1024,384]{1,0:T(8,128)} %copy.43, f32[1024,384]{1,0:T(8,128)} %copy-done.17, f32[1024,384]{1,0:T(8,128)} %copy-done.16), kind=kOutput, calls=%fused_computation.18 | convolution fusion | flops 5438177280 | bytes 8060928 | tf_op jit(solution)/shard_map/dot_general | solution.py:72
  514.6 191.4 %all-reduce.8.cloned.1.call-done = f32[384,1536]{0,1:T(8,128)} async-done(((f32[384,1536]{0,1:T(8,128)}), f32[384,1536]{0,1:T(8,128)}) %all-reduce.8.cloned.1.call-update) | async-done | bytes 2359312
  707.6 24.8 %all-reduce.4 = (f32[6,1536]{0,1:T(8,128)S(1)}, f32[8]{0:T(128)}) all-reduce(f32[6,1536]{0,1:T(8,128)S(1)} %constant_dynamic-slice_fusion, f32[8]{0:T(128)S(1)} %broadcast_multiply_fusion), channel_id=1, replica_groups=mesh['dp'=4,'ctx'=64] {'dp'}, use_global_device_ids=true, to_apply=%region_13.0 | all-reduce | flops 9224 | bytes 73792 | tf_op jit(solution)/shard_map/psum | solution.py:82
  (66 shorter events, 17.0 us)
Async XLA Ops:
  7.2 1.5 copy-start
  7.2 340.8 %all-reduce.10.cloned.1.call-start = ((), (), s32[]{:S(2)}) async-start(), calls=%async_computation.1 | async-start | bytes 786432 | tf_op jit(solution)/shard_map/psum | solution.py:46
  18.5 2.1 copy-start.1
  131.3 4.4 copy-start.20
  143.4 4.4 copy-start.7
  147.7 2.3 copy-start.2
  147.8 2.3 copy-start.3
  147.8 2.4 copy-start.5
  150.2 197.7 %copy-start.19 = (f32[8]{0:T(128)S(1)}, f32[8]{0:T(128)}, u32[]{:S(2)}) copy-start(f32[8]{0:T(128)} %param.8) | copy-start | bytes 100
  152.5 553.5 %all-reduce.8.cloned.1.call-start = ((), (), s32[]{:S(2)}) async-start(), calls=%async_computation | async-start | bytes 4718592
  349.1 4.5 copy-start.8
  349.1 4.5 copy-start.11
  353.5 2.7 copy-start.12
  353.6 2.9 copy-start.4
  356.5 2.9 copy-start.6
  376.6 2.8 copy-start.9
  487.7 2.4 copy-start.10
  487.7 2.4 copy-start.21
  489.9 1.2 copy-start.16
  490.0 1.8 copy-start.15
  490.0 2.3 copy-start.18
  492.3 7.5 %copy-start.17 = (f32[1024,384]{1,0:T(8,128)}, f32[1024,384]{1,0:T(8,128)S(1)}, u32[]{:S(2)}) copy-start(f32[1024,384]{1,0:T(8,128)S(1)} %subtract_divide_fusion) | copy-start | bytes 4718596
  492.3 7.5 %copy-start.14 = (f32[384,384]{0,1:T(8,128)S(1)}, f32[384,384]{0,1:T(8,128)}, u32[]{:S(2)}) copy-start(f32[384,384]{0,1:T(8,128)} %fusion.5) | copy-start | bytes 1769476
  501.4 1.9 copy-start.13
  (1 other events, 0.7 us)
Sparse Core Ops, SparseCore 0:
  152.6 195.3 all-reduce.9
  501.6 204.3 all-reduce.7
where the time goes:
time: 748 us; the launch traced here: 741 us
  waiting for transfers between devices  387 us (52%)
  blocking collectives  243 us (32%)
  matrix products  55.2 us (7%)
  local copies, waits for them, and re-layouts  27.2 us (4%)
  between operations  15.2 us (2%)
  other arithmetic  14 us (2%)
    psum x1, waiting for transfers between devices, body(): feature_crosscorr, attention_grad = lax.psum((local_cov, local_attn), 'ctx')  195 us
    unnamed x3, waiting for transfers between devices  191 us
    psum x1, blocking collectives, body(): query_total, key_total = lax.psum((query_square, key_square), 'ctx')  110 us
    psum x1, blocking collectives, body(): lax.psum((jnp.sum(query_hat * qhat_grad, axis=0), jnp.sum(key_hat * khat_...  107 us
    psum x1, blocking collectives, body(): lax.psum((device_patch_lines, specimen_sharpness * logit_multiplier), 'dp')  24.8 us
  transfers between devices with their start and end apart: 2, of which 2 were waited for; matrix products, arithmetic and copies ran while one was open for 2% of the time, Pallas kernels for 0%

commit v1 on v0

v1 whole, which is shorter than its diff:
```python
import functools
import math

import jax
import jax.numpy as jnp
from jax import lax
from jax.experimental import pallas as pl
from jax.experimental.pallas import tpu as pltpu
from jax.sharding import Mesh, PartitionSpec as P

epsilon = 1e-06
D = 384
VIEWS = 8
HEAD = D // VIEWS
T = 128
X_CHIPS, Z_CHIPS, CORES = 4, 8, 2
SHARES = X_CHIPS * Z_CHIPS
ROWS = D // (SHARES * CORES)
A_BLOCKS = [(0, 0), (0, 1), (0, 2), (1, 1), (1, 2), (2, 2)]
B_BLOCKS = [(i, j) for i in range(3) for j in range(3)]
HALF = 8 * T
f32, bf16 = jnp.float32, jnp.bfloat16


def split(a):
    high = a.astype(bf16)
    return high, (a - high.astype(f32)).astype(bf16)


def dot3(a, b, dims):
    d = functools.partial(
        lax.dot_general, dimension_numbers=(dims, ((), ())), preferred_element_type=f32
    )
    return d(a[0], b[0]) + (d(a[0], b[1]) + d(a[1], b[0]))


NN = ((1,), (0,))
NT = ((1,), (1,))
TN = ((0,), (0,))


def gram_kernel(core_ref, x_ref, u_ref, keep_ref, send_ref, acc_ref, pay_ref):
    step = pl.program_id(0)
    xh, xl = split(x_ref[...])
    uh, ul = split(u_ref[...])
    d = functools.partial(
        lax.dot_general, dimension_numbers=(TN, ((), ())), preferred_element_type=f32
    )
    whole = d(xh, xh)
    cross = d(xh, xl)
    mixed = d(xh, uh) + (d(xh, ul) + d(xl, uh))

    @pl.when(step == 0)
    def _():
        acc_ref[0] = whole
        acc_ref[1] = cross
        acc_ref[2] = mixed

    @pl.when(step > 0)
    def _():
        acc_ref[0] += whole
        acc_ref[1] += cross
        acc_ref[2] += mixed

    @pl.when(step == pl.num_programs(0) - 1)
    def _():
        a = acc_ref[0] + acc_ref[1] + acc_ref[1].T
        at = 0
        for i, j in A_BLOCKS:
            pay_ref[at // 8, at % 8] = a[i * T : (i + 1) * T, j * T : (j + 1) * T]
            at += 1
        for i, j in B_BLOCKS:
            pay_ref[at // 8, at % 8] = acc_ref[2, i * T : (i + 1) * T, j * T : (j + 1) * T]
            at += 1
        pay_ref[1, 7] = jnp.zeros((T, T), f32)
        core = core_ref[0]
        keep_ref[...] = pay_ref[core].reshape(HALF, T)
        send_ref[...] = pay_ref[1 - core].reshape(HALF, T)


def solve_kernel(
    place_ref,
    sharp_ref,
    mine_ref,
    other_ref,
    w_ref,
    f_ref,
    ph_ref,
    pl_ref,
    rows_ref,
    a_ref,
    b_ref,
):
    core = place_ref[0]
    first = place_ref[1]
    mine = mine_ref[...].reshape(8, T, T)
    other = other_ref[...].reshape(8, T, T)
    low = jnp.where(core == 0, mine, other)
    high = jnp.where(core == 0, other, mine)
    at = 0
    for i, j in A_BLOCKS:
        block = low[at]
        a_ref[i * T : (i + 1) * T, j * T : (j + 1) * T] = block
        if i != j:
            a_ref[j * T : (j + 1) * T, i * T : (i + 1) * T] = block.T
        at += 1
    for i, j in B_BLOCKS:
        block = low[at] if at < 8 else high[at - 8]
        b_ref[i * T : (i + 1) * T, j * T : (j + 1) * T] = block
        at += 1

    wq, wk, wv = w_ref[:, :D], w_ref[:, D : 2 * D], w_ref[:, 2 * D :]
    wqs, wks, wvs, fs = split(wq), split(wk), split(wv), split(f_ref[...])
    a_s = split(a_ref[...])
    b_s = split(b_ref[...])

    row = lax.broadcasted_iota(jnp.int32, (D, D), 0)
    col = lax.broadcasted_iota(jnp.int32, (D, D), 1)
    eye = row == col
    same = jnp.zeros((D, D), jnp.bool_)
    sharp = jnp.zeros((D, 1), f32)
    for h in range(VIEWS):
        lo, hi = h * HEAD, (h + 1) * HEAD
        same = same | ((row >= lo) & (row < hi) & (col >= lo) & (col < hi))
        r = row[:, :1]
        sharp = jnp.where((r >= lo) & (r < hi), sharp_ref[h], sharp)

    def to_col(v):
        return jnp.sum(jnp.where(eye, v, 0.0), axis=1, keepdims=True)

    def to_row(v):
        return jnp.sum(jnp.where(eye, v, 0.0), axis=0, keepdims=True)

    tq = dot3(a_s, wqs, NN)
    tk = dot3(a_s, wks, NN)
    q_square = jnp.maximum(jnp.sum(wq * tq, axis=0, keepdims=True), 0.0) + epsilon
    k_square = jnp.maximum(jnp.sum(wk * tk, axis=0, keepdims=True), 0.0) + epsilon
    q_inv = lax.rsqrt(q_square)
    k_inv = lax.rsqrt(k_square)
    q_inv_col = to_col(q_inv)
    cov = dot3(wqs, split(tk), TN) * q_inv_col * k_inv
    c = dot3(wvs, b_s, TN)
    c_s = split(c)
    attention_grad = dot3(fs, c_s, NT)

    table = jnp.where(same, jnp.exp(jnp.where(same, sharp * cov, 0.0)), 0.0)
    attention = table / jnp.sum(table, axis=1, keepdims=True)
    inner = jnp.sum(attention * attention_grad, axis=1, keepdims=True)
    score_grad = attention * (attention_grad - inner)
    weighed = score_grad * cov
    cov_grad = sharp * score_grad
    inner_grad = sharp * weighed
    c_q = to_row(jnp.sum(inner_grad, axis=1, keepdims=True))
    c_k = jnp.sum(inner_grad, axis=0, keepdims=True)
    m_s = split(cov_grad * q_inv_col * k_inv)
    att_s = split(attention)

    gq = dot3(wks, m_s, NT) - wq * (c_q * q_inv * q_inv)
    gk = dot3(wqs, m_s, NN) - wk * (c_k * k_inv * k_inv)
    gv = dot3(fs, att_s, TN)
    gq_s, gk_s, gv_s = split(gq), split(gk), split(gv)
    p = dot3(gq_s, wqs, NT) + dot3(gk_s, wks, NT)
    r = dot3(gv_s, wvs, NT)
    ph, plo = split(p)
    rh, rlo = split(r)
    ph_ref[:D] = ph
    ph_ref[D:] = rh
    pl_ref[:D] = plo
    pl_ref[D:] = rlo

    pick_row = lax.broadcasted_iota(jnp.int32, (16, D), 0)
    pick_col = lax.broadcasted_iota(jnp.int32, (16, D), 1)
    pick = jnp.where(pick_row + first == pick_col, 1.0, 0.0).astype(bf16)

    def rows_of(pair):
        return tuple(jnp.dot(pick, one, preferred_element_type=f32).astype(bf16) for one in pair)

    a_rows, b_rows, att_rows = rows_of(a_s), rows_of(b_s), rows_of(att_s)
    scale = place_scale
    rows_ref[:, :D] = dot3(a_rows, gq_s, NN)[:8] * scale
    rows_ref[:, D : 2 * D] = dot3(a_rows, gk_s, NN)[:8] * scale
    rows_ref[:, 2 * D : 3 * D] = dot3(b_rows, gv_s, NN)[:8] * scale
    rows_ref[:, 3 * D : 4 * D] = dot3(att_rows, c_s, NN)[:8] * scale
    by_feature = jnp.sum(weighed, axis=1, keepdims=True) * scale
    lane = lax.broadcasted_iota(jnp.int32, (D, T), 1)
    feature = lax.broadcasted_iota(jnp.int32, (D, T), 0)
    chosen = (feature >= lane * HEAD) & (feature < (lane + 1) * HEAD)
    temp = jnp.sum(jnp.where(chosen, by_feature, 0.0), axis=0, keepdims=True)
    rows_ref[:, 4 * D :] = jnp.broadcast_to(temp, (8, T))


place_scale = 1.0 / math.sqrt(262144)


def output_kernel(x_ref, u_ref, ph_ref, pl_ref, out_ref):
    xh, xl = split(x_ref[...])
    uh, ul = split(u_ref[...])
    high = jnp.concatenate([xh, uh], axis=1)
    low = jnp.concatenate([xl, ul], axis=1)
    out_ref[...] = dot3((high, low), (ph_ref[...], pl_ref[...]), NN)


def body(
    incoming_embeddings,
    stacked_projector,
    final_projector,
    sharpness_per_view,
    upstream_sensitivity,
):
    x = incoming_embeddings[0]
    u = upstream_sensitivity[0]
    tokens = x.shape[0]
    core = lax.axis_index("core")
    ctx = (lax.axis_index("x") * Z_CHIPS + lax.axis_index("z")) * CORES + core
    place = jnp.stack([core, ctx * ROWS]).astype(jnp.int32)
    smem = pl.BlockSpec(memory_space=pltpu.SMEM)
    params = pltpu.CompilerParams(vmem_limit_bytes=48 * 1024 * 1024)

    block = tokens // 2
    token_spec = pl.BlockSpec((block, D), lambda i: (i, 0))
    half_spec = pl.BlockSpec((HALF, T), lambda i: (0, 0))
    half_shape = jax.ShapeDtypeStruct((HALF, T), f32)
    keep, send = pl.pallas_call(
        gram_kernel,
        grid=(tokens // block,),
        in_specs=[smem, token_spec, token_spec],
        out_specs=[half_spec, half_spec],
        out_shape=[half_shape, half_shape],
        scratch_shapes=[pltpu.VMEM((3, D, D), f32), pltpu.VMEM((2, 8, T, T), f32)],
        compiler_params=params,
    )(place, x, u)

    swap = [(0, 1), (1, 0)]
    part = (keep + lax.ppermute(send, "core", swap)).reshape(SHARES, -1, T)
    arrived = lax.all_to_all(part, ("x", "z"), 0, 0, tiled=True)
    summed = jnp.sum(arrived, axis=0)
    spread = jnp.broadcast_to(summed, (SHARES,) + summed.shape)
    mine = lax.all_to_all(spread, ("x", "z"), 0, 0, tiled=True).reshape(HALF, T)
    other = lax.ppermute(mine, "core", swap)

    vmem = pl.BlockSpec(memory_space=pltpu.VMEM)
    ph, plo, rows = pl.pallas_call(
        solve_kernel,
        in_specs=[smem, smem, vmem, vmem, vmem, vmem],
        out_specs=[vmem, vmem, vmem],
        out_shape=[
            jax.ShapeDtypeStruct((2 * D, D), bf16),
            jax.ShapeDtypeStruct((2 * D, D), bf16),
            jax.ShapeDtypeStruct((8, 4 * D + T), f32),
        ],
        scratch_shapes=[
            pltpu.VMEM((D, D), f32),
            pltpu.VMEM((D, D), f32),
        ],
        compiler_params=params,
    )(place, sharpness_per_view, mine, other, stacked_projector, final_projector)

    slides = lax.axis_size("dp")
    others = [
        lax.ppermute(rows, "dp", [(i, (i + k) % slides) for i in range(slides)])
        for k in range(1, slides)
    ]

    whole_spec = pl.BlockSpec((2 * D, D), lambda i: (0, 0))
    input_grad = pl.pallas_call(
        output_kernel,
        grid=(tokens // block,),
        in_specs=[token_spec, token_spec, whole_spec, whole_spec],
        out_specs=token_spec,
        out_shape=jax.ShapeDtypeStruct((tokens, D), f32),
        compiler_params=params,
        cost_estimate=pl.CostEstimate(
            flops=2 * 3 * tokens * 2 * D * D, bytes_accessed=3 * tokens * D * 4, transcendentals=0
        ),
    )(x, u, ph, plo)

    total = (rows + others[1]) + (others[0] + others[2])
    return (
        input_grad[None],
        total[:ROWS, : 3 * D],
        total[:ROWS, 3 * D : 4 * D],
        total[0, 4 * D : 4 * D + VIEWS],
    )


def solution(mesh):
    slides = mesh.shape["dp"]
    fine = Mesh(
        mesh.devices.reshape(slides, X_CHIPS, Z_CHIPS, CORES), ("dp", "x", "z", "core")
    )
    ctx = ("x", "z", "core")
    return jax.shard_map(
        body,
        mesh=fine,
        in_specs=(P("dp", ctx, None), P(), P(), P(), P("dp", ctx, None)),
        out_specs=(P("dp", ctx, None), P(ctx, None), P(ctx, None), P()),
        check_vma=False,
    )
```

time: 748 us -> 81.8 us (0.11)
  the two profiles are of different devices: /device:TPU:4 before, /device:TPU:40 now
where the time goes in v1:
time: 81.8 us; the launch traced here: 81.5 us
  blocking collectives  51.1 us (62%)
  Pallas kernels  15.4 us (19%)
  starting transfers between devices  5.71 us (7%)
  local copies, waits for them, and re-layouts  4.63 us (6%)
  waiting for transfers between devices  3.81 us (5%)
    all_to_all x1, blocking collectives, body(): arrived = lax.all_to_all(part, ('x', 'z'), 0, 0, tiled=True)  29 us
    all_to_all x1, blocking collectives, body(): mine = lax.all_to_all(spread, ('x', 'z'), 0, 0, tiled=True).reshape(HALF, T)  22.1 us
    pallas_call x1, Pallas kernels, body(): pl.pallas_call(solve_kernel, in_specs=[smem, smem, vmem, vmem, vmem, vmem...  8.14 us
    ppermute x3, starting transfers between devices, body(): lax.ppermute(rows, 'dp', [(i, (i + k) % slides) for i in range(slides)])  5.62 us
    pallas_call x1, Pallas kernels, body(): pl.pallas_call(output_kernel, grid=(tokens // block,), in_specs=[token_sp...  3.66 us
    pallas_call x1, Pallas kernels, body(): pl.pallas_call(gram_kernel, grid=(tokens // block,), in_specs=[smem, toke...  3.57 us
    unnamed x14, local copies, waits for them, and re-layouts  2.84 us
    ppermute x1, waiting for transfers between devices, body(): other = lax.ppermute(mine, 'core', swap)  1.91 us
  transfers between devices with their start and end apart: 5, of which 2 were waited for; matrix products, arithmetic and copies ran while one was open for 0% of the time, Pallas kernels for 4%

profile of v1, /device:TPU:40, one launch (start us, length us, event | category | flops | bytes accessed | tf_op | source)
XLA Modules:
  0.0 81.5 jit_solution(6389353733269237589)
XLA Ops:
  0.6 0.1 pad_add_fusion.core_ref.place_ref
  0.7 1.4 %copy-done.1 = f32[1,1024,384]{2,1,0:T(8,128)S(1)} copy-done((f32[1,1024,384]{2,1,0:T(8,128)S(1)}, f32[1,1024,384]{2,1,0:T(8,128)}, u32[]{:S(2)}) %copy-start.1) | copy-done | bytes 1572888
  2.1 1.4 %copy-done.3 = f32[1,1024,384]{2,1,0:T(8,128)S(1)} copy-done((f32[1,1024,384]{2,1,0:T(8,128)S(1)}, f32[1,1024,384]{2,1,0:T(8,128)}, u32[]{:S(2)}) %copy-start.3) | copy-done | bytes 1572888
  3.5 3.6 %shard_map.84 = (f32[1024,128]{1,0:T(8,128)S(1)}, f32[1024,128]{1,0:T(8,128)S(1)}) custom-call(s32[2]{0:T(128)S(1)} %pad_add_fusion.core_ref.place_ref, f32[1024,384]{1,0:T(8,128)S(1)} %bitcast.11, f32[1024,384]{1,0:T(8,128)S(1)} %bitcast.13), custom_call_target="tpu_custom_call" | custom-call | tf_op jit(solution)/shard_map/pallas_call | solution.py:223
  7.1 0.1 collective-permute-start
  7.2 1.9 %collective-permute-done = f32[1024,128]{1,0:T(8,128)S(1)} collective-permute-done((f32[1024,128]{1,0:T(8,128)S(1)}, f32[1024,128]{1,0:T(8,128)S(1)}, u32[]{:S(2)}, u32[]{:S(2)}) %collective-permute-start) | collective-permute-done | bytes 524320 | tf_op jit(solution)/shard_map/ppermute | solution.py:234
  9.1 0.1 add.20
  9.2 0.0 copy-start
  9.2 0.0 copy-start.5
  9.2 0.0 copy-start.6
  9.2 29.0 %all_to_all.10 = f32[32,32,128]{2,1,0:T(8,128)S(1)} all-to-all(f32[32,32,128]{2,1,0:T(8,128)S(1)} %bitcast.15), channel_id=1, replica_groups=mesh['dp'=4,'x'=4,'z'=8,'core'=2] {'x','z'}, dimensions={0} | all-to-all | bytes 1048576 | tf_op jit(solution)/shard_map/all_to_all | solution.py:235
  38.3 0.1 broadcast_in_dim.6
  38.4 22.1 %all_to_all.11 = f32[32,32,128]{2,1,0:T(8,128)S(1)} all-to-all(f32[32,32,128]{2,1,0:T(8,128)S(1)} %broadcast_in_dim.6), channel_id=1, replica_groups=mesh['dp'=4,'x'=4,'z'=8,'core'=2] {'x','z'}, dimensions={0} | all-to-all | bytes 1048576 | tf_op jit(solution)/shard_map/all_to_all | solution.py:238
  60.4 0.0 collective-permute-start.1
  60.4 1.9 %collective-permute-done.1.other_ref = f32[1024,128]{1,0:T(8,128)S(1)} collective-permute-done((f32[1024,128]{1,0:T(8,128)S(1)}, f32[1024,128]{1,0:T(8,128)S(1)}, u32[]{:S(2)}, u32[]{:S(2)}) %collective-permute-start.1) | collective-permute-done | bytes 524320 | tf_op jit(solution)/shard_map/ppermute | solution.py:239
  62.3 8.1 %shard_map.85 = (bf16[768,384]{1,0:T(8,128)(2,1)S(1)}, bf16[768,384]{1,0:T(8,128)(2,1)S(1)}, f32[8,1664]{1,0:T(8,128)S(1)}) custom-call(s32[2]{0:T(128)S(1)} %pad_add_fusion.core_ref.place_ref, f32[8]{0:T(128)S(1)} %copy-done.6, f32[1024,128]{1,0:T(8,128)S(1)} %bitcast.10, f32[1024,128]{1,0:T(8,128)S(1)} %collective-permute-done.1.other_ref, ...), custom_call_target="tpu_custom_call" | custom-call | tf_op jit(solution)/shard_map/pallas_call | solution.py:242
  70.5 0.5 collective-permute-start.4
  71.0 1.6 %collective-permute-start.3 = (f32[8,1664]{1,0:T(8,128)S(1)}, f32[8,1664]{1,0:T(8,128)S(1)}, u32[]{:S(2)}, u32[]{:S(2)}) collective-permute-start(f32[8,1664]{1,0:T(8,128)S(1)} %get-tuple-element.13), channel_id=1, source_target_pairs={{0,64},{64,128},{128,192},{192,0},{1,65},{65,129},{129,193},{193,1... | collective-permute-start | bytes 159752 | tf_op jit(solution)/shard_map/ppermute | solution.py:260
  72.6 3.5 %collective-permute-start.2 = (f32[8,1664]{1,0:T(8,128)S(1)}, f32[8,1664]{1,0:T(8,128)S(1)}, u32[]{:S(2)}, u32[]{:S(2)}) collective-permute-start(f32[8,1664]{1,0:T(8,128)S(1)} %get-tuple-element.13), channel_id=1, source_target_pairs={{0,128},{64,192},{128,0},{192,64},{1,129},{65,193},{129,1},{193,65... | collective-permute-start | bytes 159752 | tf_op jit(solution)/shard_map/ppermute | solution.py:260
  76.1 3.7 %shard_map.86 = f32[1024,384]{1,0:T(8,128)} custom-call(f32[1024,384]{1,0:T(8,128)S(1)} %bitcast.12, f32[1024,384]{1,0:T(8,128)S(1)} %bitcast.14, bf16[768,384]{1,0:T(8,128)(2,1)S(1)} %get-tuple-element.11.ph_ref, bf16[768,384]{1,0:T(8,128)(2,1)S(1)} %get-tuple-element.12.pl_ref), custom_call_target="tpu_custom_call" | custom-call | flops 1811939328 | bytes 4718592 | tf_op jit(solution)/shard_map/pallas_call | solution.py:265
  79.8 0.0 collective-permute-done.2
  79.8 0.5 slice_bitcast_fusion
  80.3 0.6 slice.13
  80.9 0.6 slice.12
  (13 shorter events, 0.1 us)
Async XLA Ops:
  0.7 1.4 %copy-start.1 = (f32[1,1024,384]{2,1,0:T(8,128)S(1)}, f32[1,1024,384]{2,1,0:T(8,128)}, u32[]{:S(2)}) copy-start(f32[1,1024,384]{2,1,0:T(8,128)} %param.5) | copy-start | bytes 4718596
  2.1 1.4 %copy-start.3 = (f32[1,1024,384]{2,1,0:T(8,128)S(1)}, f32[1,1024,384]{2,1,0:T(8,128)}, u32[]{:S(2)}) copy-start(f32[1,1024,384]{2,1,0:T(8,128)} %param.9) | copy-start | bytes 4718596
  7.1 2.0 %collective-permute-start = (f32[1024,128]{1,0:T(8,128)S(1)}, f32[1024,128]{1,0:T(8,128)S(1)}, u32[]{:S(2)}, u32[]{:S(2)}) collective-permute-start(f32[1024,128]{1,0:T(8,128)S(1)} %get-tuple-element.10), channel_id=1, source_target_pairs={{0,1},{1,0},{2,3},{3,2},{4,5},{5,4},{6,7},{7,6},{8,9},{9,8},{10,11... | collective-permute-start | bytes 1572872 | tf_op jit(solution)/shard_map/ppermute | solution.py:234
  9.2 53.2 %copy-start = (f32[384,1152]{1,0:T(8,128)S(1)}, f32[384,1152]{1,0:T(8,128)}, u32[]{:S(2)}) copy-start(f32[384,1152]{1,0:T(8,128)} %w_ref.1) | copy-start | bytes 5308420
  9.2 53.2 %copy-start.5 = (f32[384,384]{1,0:T(8,128)S(1)}, f32[384,384]{1,0:T(8,128)}, u32[]{:S(2)}) copy-start(f32[384,384]{1,0:T(8,128)} %f_ref.1) | copy-start | bytes 1769476
  9.2 53.2 %copy-start.6 = (f32[8]{0:T(128)S(1)}, f32[8]{0:T(128)}, u32[]{:S(2)}) copy-start(f32[8]{0:T(128)} %sharp_ref.1) | copy-start | bytes 100
  60.4 15.7 %copy-start.2 = (f32[1,1024,384]{2,1,0:T(8,128)S(1)}, f32[1,1024,384]{2,1,0:T(8,128)}, u32[]{:S(2)}) copy-start(f32[1,1024,384]{2,1,0:T(8,128)} %param.5) | copy-start | bytes 4718596
  60.4 15.7 %copy-start.4 = (f32[1,1024,384]{2,1,0:T(8,128)S(1)}, f32[1,1024,384]{2,1,0:T(8,128)}, u32[]{:S(2)}) copy-start(f32[1,1024,384]{2,1,0:T(8,128)} %param.9) | copy-start | bytes 4718596
  60.4 1.9 %collective-permute-start.1 = (f32[1024,128]{1,0:T(8,128)S(1)}, f32[1024,128]{1,0:T(8,128)S(1)}, u32[]{:S(2)}, u32[]{:S(2)}) collective-permute-start(f32[1024,128]{1,0:T(8,128)S(1)} %bitcast.9), channel_id=1, source_target_pairs={{0,1},{1,0},{2,3},{3,2},{4,5},{5,4},{6,7},{7,6},{8,9},{9,8},{10,11... | collective-permute-start | bytes 1572872 | tf_op jit(solution)/shard_map/ppermute | solution.py:239
  70.5 9.3 %collective-permute-start.4 = (f32[8,1664]{1,0:T(8,128)S(1)}, f32[8,1664]{1,0:T(8,128)S(1)}, u32[]{:S(2)}, u32[]{:S(2)}) collective-permute-start(f32[8,1664]{1,0:T(8,128)S(1)} %get-tuple-element.13), channel_id=1, source_target_pairs={{0,192},{64,0},{128,64},{192,128},{1,193},{65,1},{129,65},{193,129... | collective-permute-start | bytes 159752 | tf_op jit(solution)/shard_map/ppermute | solution.py:260
  71.0 8.8 %collective-permute-start.3 = (f32[8,1664]{1,0:T(8,128)S(1)}, f32[8,1664]{1,0:T(8,128)S(1)}, u32[]{:S(2)}, u32[]{:S(2)}) collective-permute-start(f32[8,1664]{1,0:T(8,128)S(1)} %get-tuple-element.13), channel_id=1, source_target_pairs={{0,64},{64,128},{128,192},{192,0},{1,65},{65,129},{129,193},{193,1... | collective-permute-start | bytes 159752 | tf_op jit(solution)/shard_map/ppermute | solution.py:260
  72.6 7.2 %collective-permute-start.2 = (f32[8,1664]{1,0:T(8,128)S(1)}, f32[8,1664]{1,0:T(8,128)S(1)}, u32[]{:S(2)}, u32[]{:S(2)}) collective-permute-start(f32[8,1664]{1,0:T(8,128)S(1)} %get-tuple-element.13), channel_id=1, source_target_pairs={{0,128},{64,192},{128,0},{192,64},{1,129},{65,193},{129,1},{193,65... | collective-permute-start | bytes 159752 | tf_op jit(solution)/shard_map/ppermute | solution.py:260

commit v2 on v0

v2 whole, which is shorter than its diff:
```python
import functools
import math

import jax
import jax.numpy as jnp
from jax import lax
from jax.experimental import pallas as pl
from jax.experimental.pallas import tpu as pltpu
from jax.sharding import Mesh, PartitionSpec as P

epsilon = 1e-06
D = 384
VIEWS = 8
HEAD = D // VIEWS
T = 128
W = 256
X_CHIPS, Z_CHIPS, CORES = 4, 8, 2
SHARES = X_CHIPS * Z_CHIPS
ROWS = D // (SHARES * CORES)
HALF = 8 * T
QUARTER = HALF // X_CHIPS
PICK = 16
BLOCKS = [("a", i, j) for i in range(3) for j in range(i, 3)]
BLOCKS += [("b", i, j) for i in range(3) for j in range(3)]


def place_of(at):
    return at // 8, at % 8 // 2, at % 2


f32, bf16 = jnp.float32, jnp.bfloat16
NN = ((1,), (0,))
NT = ((1,), (1,))
TN = ((0,), (0,))


def split(a):
    high = a.astype(bf16)
    return high, (a - high.astype(f32)).astype(bf16)


def dot3(a, b, dims):
    d = functools.partial(
        lax.dot_general, dimension_numbers=(dims, ((), ())), preferred_element_type=f32
    )
    return d(a[0], b[0]) + (d(a[0], b[1]) + d(a[1], b[0]))


def cut(pair, rows, cols):
    return pair[0][rows, cols], pair[1][rows, cols]


ALL = slice(None)
WINDOWS = (slice(0, W), slice(D - W, D))


def join(parts):
    one, two = parts
    return jnp.concatenate([one[:, :T], one[:, T:] + two[:, :T], two[:, T:]], axis=1)


def gram_kernel(place_ref, x_hbm, u_hbm, keep_ref, send_ref, x_ref, u_ref, pay_ref, sems):
    tokens = x_ref.shape[0]
    step = tokens // 4
    copies = []
    for at, (source, target) in enumerate(((x_hbm, x_ref), (u_hbm, u_ref))):
        for k in range(4):
            piece = pl.ds(k * step, step)
            copy = pltpu.make_async_copy(source.at[piece], target.at[piece], sems.at[at * 4 + k])
            copy.start()
            copies.append(copy)
    for copy in copies[:4]:
        copy.wait()
    d = functools.partial(
        lax.dot_general, dimension_numbers=(TN, ((), ())), preferred_element_type=f32
    )
    xh, xl = split(x_ref[...])
    cross = d(xh, xl)
    grams = {"a": d(xh, xh) + cross + cross.T}
    for copy in copies[4:]:
        copy.wait()
    uh, ul = split(u_ref[...])
    grams["b"] = d(xh, uh) + (d(xh, ul) + d(xl, uh))
    for at, (name, i, j) in enumerate(BLOCKS):
        pay_ref[place_of(at)] = grams[name][i * T : (i + 1) * T, j * T : (j + 1) * T]
    pay_ref[place_of(15)] = jnp.zeros((T, T), f32)
    core, chip = place_ref[0], place_ref[2]
    for k in range(X_CHIPS):
        to = lax.rem(chip + k, X_CHIPS)
        piece = pl.ds(k * QUARTER, QUARTER)
        keep_ref[piece] = pay_ref[core, to].reshape(QUARTER, T)
        send_ref[piece] = pay_ref[1 - core, to].reshape(QUARTER, T)


def heads_of(shape, axis, window):
    feature = lax.broadcasted_iota(jnp.int32, shape, axis) + window * (D - W)
    head = jnp.zeros(shape, jnp.int32)
    for h in range(1, VIEWS):
        head = head + jnp.where(feature >= h * HEAD, 1, 0)
    return feature, head


def masks(window):
    _, rows = heads_of((W, W), 0, window)
    _, cols = heads_of((W, W), 1, window)
    own = (rows < VIEWS // 2) if window == 0 else (rows >= VIEWS // 2)
    return (rows == cols) & own


def eye_of(size):
    return lax.broadcasted_iota(jnp.int32, (size, size), 0) == lax.broadcasted_iota(
        jnp.int32, (size, size), 1
    )


def to_col(eye, v):
    return jnp.sum(jnp.where(eye, v, 0.0), axis=1, keepdims=True)


def to_row(eye, v):
    return jnp.sum(jnp.where(eye, v, 0.0), axis=0, keepdims=True)


def sharp_col(sharp_ref, window):
    _, head = heads_of((W, 1), 0, window)
    sharp = jnp.zeros((W, 1), f32)
    for h in range(VIEWS):
        sharp = jnp.where(head == h, sharp_ref[h], sharp)
    return sharp


def pick_of(first, size, offset):
    row = lax.broadcasted_iota(jnp.int32, (PICK, size), 0) + first
    col = lax.broadcasted_iota(jnp.int32, (PICK, size), 1) + offset
    return jnp.where(row == col, 1.0, 0.0).astype(bf16)


def rows_of(pick, pair):
    return tuple(jnp.dot(pick, one, preferred_element_type=f32).astype(bf16) for one in pair)


scale = 1.0 / math.sqrt(262144)


def solve_kernel(
    place_ref, sharp_ref, mine_ref, other_ref, w_ref, f_ref,
    att_ref, m_ref, d_ref, rows_ref, block_ref, a_ref, b_ref,
):
    core, first, chip = place_ref[0], place_ref[1], place_ref[2]
    for k in range(X_CHIPS):
        origin = lax.rem(chip + X_CHIPS - k, X_CHIPS)
        piece = pl.ds(k * QUARTER, QUARTER)
        block_ref[core, origin] = mine_ref[piece].reshape(2, T, T)
        block_ref[1 - core, origin] = other_ref[piece].reshape(2, T, T)
    for at, (name, i, j) in enumerate(BLOCKS):
        block = block_ref[place_of(at)]
        ref = a_ref if name == "a" else b_ref
        ref[i * T : (i + 1) * T, j * T : (j + 1) * T] = block
        if name == "a" and i != j:
            ref[j * T : (j + 1) * T, i * T : (i + 1) * T] = block.T
    a_s, b_s = split(a_ref[...]), split(b_ref[...])
    wq, wk = w_ref[:, :D], w_ref[:, D : 2 * D]
    wqs, wks, wvs, fs = split(wq), split(wk), split(w_ref[:, 2 * D :]), split(f_ref[...])
    tq = dot3(a_s, wqs, NN)
    tk = dot3(a_s, wks, NN)
    c_s = split(dot3(wvs, b_s, TN))
    q_inv = lax.rsqrt(jnp.maximum(jnp.sum(wq * tq, axis=0, keepdims=True), 0.0) + epsilon)
    k_inv = lax.rsqrt(jnp.maximum(jnp.sum(wk * tk, axis=0, keepdims=True), 0.0) + epsilon)
    tks = split(tk)
    pick = pick_of(first, D, 0)
    tq_rows, tk_rows = rows_of(pick, split(tq)), rows_of(pick, tks)
    b_f = split(dot3(rows_of(pick, b_s), fs, NT))
    eye = eye_of(W)
    q_sum, k_sum, q_rows, k_rows, v_rows, att_high, att_low = [], [], [], [], [], [], []
    temp = jnp.zeros((1, T), f32)
    for window, span in enumerate(WINDOWS):
        same = masks(window)
        sharp = sharp_col(sharp_ref, window)
        q_col = to_col(eye, q_inv[:, span])
        cov = dot3(cut(wqs, ALL, span), cut(tks, ALL, span), TN)
        cov = jnp.where(same, cov * q_col * k_inv[:, span], 0.0)
        table = jnp.where(same, jnp.exp(sharp * cov), 0.0)
        total = jnp.sum(table, axis=1, keepdims=True)
        attention = table / jnp.where(total > 0.0, total, 1.0)
        attention_grad = dot3(cut(fs, span, ALL), cut(c_s, span, ALL), NT)
        inner = jnp.sum(attention * attention_grad, axis=1, keepdims=True)
        score_grad = attention * (attention_grad - inner)
        weighed = score_grad * cov
        by_feature = jnp.sum(weighed, axis=1, keepdims=True)
        q_sum.append(to_row(eye, sharp * by_feature))
        k_sum.append(jnp.sum(sharp * weighed, axis=0, keepdims=True))
        m_s = split(sharp * score_grad * q_col * k_inv[:, span])
        m_ref[0, window], m_ref[1, window] = m_s
        att_s = split(attention)
        att_ref[0, window], att_ref[1, window] = att_s
        q_rows.append(dot3(cut(tk_rows, ALL, span), m_s, NT))
        k_rows.append(dot3(cut(tq_rows, ALL, span), m_s, NN))
        v_rows.append(dot3(cut(b_f, ALL, span), att_s, NN))
        high, low = rows_of(pick_of(first, W, window * (D - W)), att_s)
        att_high.append(high)
        att_low.append(low)
        _, head = heads_of((W, T), 0, window)
        lane = lax.broadcasted_iota(jnp.int32, (W, T), 1)
        temp += jnp.sum(jnp.where(head == lane, by_feature, 0.0), axis=0, keepdims=True)
    d_q = join(q_sum) * (q_inv * q_inv)
    d_k = join(k_sum) * (k_inv * k_inv)
    d_ref[0:1] = d_q
    d_ref[1:2] = d_k
    both = [high.astype(f32) + low.astype(f32) for high, low in (tq_rows, tk_rows)]
    rows_ref[:, :D] = (join(q_rows) - both[0] * d_q)[:8] * scale
    rows_ref[:, D : 2 * D] = (join(k_rows) - both[1] * d_k)[:8] * scale
    rows_ref[:, 2 * D : 3 * D] = join(v_rows)[:8] * scale
    rows_ref[:, 3 * D : 4 * D] = dot3((join(att_high), join(att_low)), c_s, NN)[:8] * scale
    rows_ref[:, 4 * D :] = jnp.broadcast_to(temp * scale, (8, T))


def output_kernel(x_ref, u_ref, w_ref, f_ref, att_ref, m_ref, d_ref, out_hbm, out_ref, sems):
    wq, wk = w_ref[:, :D], w_ref[:, D : 2 * D]
    wqs, wks, wvs, fs = split(wq), split(wk), split(w_ref[:, 2 * D :]), split(f_ref[...])
    q_parts, k_parts, v_parts = [], [], []
    for window, span in enumerate(WINDOWS):
        m_s = (m_ref[0, window], m_ref[1, window])
        att_s = (att_ref[0, window], att_ref[1, window])
        q_parts.append(dot3(cut(wks, ALL, span), m_s, NT))
        k_parts.append(dot3(cut(wqs, ALL, span), m_s, NN))
        v_parts.append(dot3(cut(fs, span, ALL), att_s, TN))
    gq = split(join(q_parts) - wq * d_ref[0:1])
    gk = split(join(k_parts) - wk * d_ref[1:2])
    gv = split(join(v_parts))
    p = split(dot3(gq, wqs, NT) + dot3(gk, wks, NT))
    r = split(dot3(gv, wvs, NT))
    both = tuple(jnp.concatenate([one, two], axis=0) for one, two in zip(p, r))
    tokens = x_ref.shape[0]
    step = tokens // 4
    copies = []
    for k in range(4):
        piece = pl.ds(k * step, step)
        xs, us = split(x_ref[piece]), split(u_ref[piece])
        token = tuple(jnp.concatenate([one, two], axis=1) for one, two in zip(xs, us))
        out_ref[piece] = dot3(token, both, NN)
        copy = pltpu.make_async_copy(out_ref.at[piece], out_hbm.at[piece], sems.at[k])
        copy.start()
        copies.append(copy)
    for copy in copies:
        copy.wait()


def total_kernel(own_ref, one_ref, two_ref, three_ref, mixer_ref, output_ref, sharp_ref):
    total = (own_ref[...] + two_ref[...]) + (one_ref[...] + three_ref[...])
    mixer_ref[...] = total[:ROWS, : 3 * D]
    output_ref[...] = total[:ROWS, 3 * D : 4 * D]
    sharp_ref[...] = total[0:1, 4 * D : 4 * D + VIEWS]


smem = pl.BlockSpec(memory_space=pltpu.SMEM)
vmem = pl.BlockSpec(memory_space=pltpu.VMEM)
hbm = pl.BlockSpec(memory_space=pltpu.HBM)


def call(kernel, ins, outs, shapes, scratch=(), flops=0, limit=32):
    return pl.pallas_call(
        kernel,
        in_specs=ins,
        out_specs=outs,
        out_shape=[jax.ShapeDtypeStruct(*one) for one in shapes],
        scratch_shapes=list(scratch),
        compiler_params=pltpu.CompilerParams(vmem_limit_bytes=limit * 1024 * 1024),
        cost_estimate=pl.CostEstimate(flops=flops, bytes_accessed=4 * 1024 * 1024, transcendentals=0),
    )


def body(
    incoming_embeddings,
    stacked_projector,
    final_projector,
    sharpness_per_view,
    upstream_sensitivity,
):
    x = incoming_embeddings[0]
    u = upstream_sensitivity[0]
    tokens = x.shape[0]
    core, chip = lax.axis_index("core"), lax.axis_index("x")
    ctx = (chip * Z_CHIPS + lax.axis_index("z")) * CORES + core
    place = jnp.stack([core, ctx * ROWS, chip]).astype(jnp.int32)
    unit = 2 * 3 * D * D * D

    half = ((HALF, T), f32)
    keep, send = call(
        gram_kernel,
        [smem, hbm, hbm],
        [vmem] * 2,
        [half] * 2,
        [
            pltpu.VMEM((tokens, D), f32),
            pltpu.VMEM((tokens, D), f32),
            pltpu.VMEM((CORES, X_CHIPS, 2, T, T), f32),
            pltpu.SemaphoreType.DMA((8,)),
        ],
        flops=6 * unit,
        limit=56,
    )(place, x, u)

    def swap(array):
        return lax.ppermute(array, "core", [(0, 1), (1, 0)])

    def shift(array, axis, by):
        size = lax.axis_size(axis)
        return lax.ppermute(array, axis, [(i, (i + by) % size) for i in range(size)])

    part = (keep + swap(send)).reshape(X_CHIPS, QUARTER, T)
    others = [shift(part[k], "x", k) for k in range(1, X_CHIPS)]
    part = part[0] + others[0] + others[1] + others[2]
    part = lax.all_to_all(part.reshape(Z_CHIPS, -1, T), "z", 0, 0, tiled=True).sum(axis=0)
    part = jnp.broadcast_to(part, (Z_CHIPS,) + part.shape)
    part = lax.all_to_all(part, "z", 0, 0, tiled=True).reshape(QUARTER, T)
    mine = jnp.concatenate([part] + [shift(part, "x", k) for k in range(1, X_CHIPS)])
    other = swap(mine)

    windows = ((2, 2, W, W), bf16)
    att, m, diagonal, rows = call(
        solve_kernel,
        [smem, smem] + [vmem] * 4,
        [vmem] * 4,
        [windows, windows, ((2, D), f32), ((8, 4 * D + T), f32)],
        [
            pltpu.VMEM((CORES, X_CHIPS, 2, T, T), f32),
            pltpu.VMEM((D, D), f32),
            pltpu.VMEM((D, D), f32),
        ],
        flops=8 * unit,
    )(place, sharpness_per_view, mine, other, stacked_projector, final_projector)

    others = [shift(rows, "dp", k) for k in range(1, lax.axis_size("dp"))]
    (input_grad,) = call(
        output_kernel,
        [vmem] * 7,
        [hbm],
        [((tokens, D), f32)],
        [pltpu.VMEM((tokens, D), f32), pltpu.SemaphoreType.DMA((4,))],
        flops=12 * unit,
    )(x, u, stacked_projector, final_projector, att, m, diagonal)
    mixer_grad, output_grad, sharpness_grad = call(
        total_kernel,
        [vmem] * 4,
        [vmem] * 3,
        [((ROWS, 3 * D), f32), ((ROWS, D), f32), ((1, VIEWS), f32)],
    )(rows, *others)
    return input_grad[None], mixer_grad, output_grad, sharpness_grad.reshape(VIEWS)


def solution(mesh):
    slides = mesh.shape["dp"]
    fine = Mesh(
        mesh.devices.reshape(slides, X_CHIPS, Z_CHIPS, CORES), ("dp", "x", "z", "core")
    )
    ctx = ("x", "z", "core")
    return jax.shard_map(
        body,
        mesh=fine,
        in_specs=(P("dp", ctx, None), P(), P(), P(), P("dp", ctx, None)),
        out_specs=(P("dp", ctx, None), P(ctx, None), P(ctx, None), P()),
        check_vma=False,
    )
```

time: 748 us -> 79.2 us (0.11)
  the two profiles are of different devices: /device:TPU:4 before, /device:TPU:8 now
where the time goes in v2:
time: 79.2 us; the launch traced here: 78.9 us
  blocking collectives  28.8 us (36%)
  Pallas kernels  17.6 us (22%)
  waiting for transfers between devices  16.1 us (20%)
  starting transfers between devices  13.7 us (17%)
  other arithmetic  1.85 us (2%)
    all_to_all x1, blocking collectives, body(): lax.all_to_all(part.reshape(Z_CHIPS, -1, T), 'z', 0, 0, tiled=True)  17.3 us
    ppermute x9, starting transfers between devices, shift(): lax.ppermute(array, axis, [(i, (i + by) % size) for i in range(size)])  13.5 us
    ppermute x9, waiting for transfers between devices, shift(): lax.ppermute(array, axis, [(i, (i + by) % size) for i in range(size)])  12.1 us
    all_to_all x1, blocking collectives, body(): part = lax.all_to_all(part, 'z', 0, 0, tiled=True).reshape(QUARTER, T)  11.5 us
    pallas_call x1, Pallas kernels, body(): call(output_kernel, [vmem] * 7, [hbm], [((tokens, D), f32)], [pltpu.VMEM(...  6.17 us
    pallas_call x1, Pallas kernels, body(): call(gram_kernel, [smem, hbm, hbm], [vmem] * 2, [half] * 2, [pltpu.VMEM((...  5.55 us
    pallas_call x1, Pallas kernels, body(): call(solve_kernel, [smem, smem] + [vmem] * 4, [vmem] * 4, [windows, windo...  5.26 us
    ppermute x2, waiting for transfers between devices, swap(): return lax.ppermute(array, 'core', [(0, 1), (1, 0)])  4 us
  transfers between devices with their start and end apart: 11, of which 8 were waited for; matrix products, arithmetic and copies ran while one was open for 0% of the time, Pallas kernels for 8%

profile of v2, /device:TPU:8, one launch (start us, length us, event | category | flops | bytes accessed | tf_op | source)
XLA Modules:
  0.0 78.9 jit_solution(11722152611136961099)
XLA Ops:
  0.6 0.7 pad_add_fusion.place_ref
  1.3 5.5 %shard_map.84 = (f32[1024,128]{1,0:T(8,128)}, f32[1024,128]{1,0:T(8,128)}) custom-call(s32[3]{0:T(128)} %pad_add_fusion.place_ref, f32[1024,384]{1,0:T(8,128)} %bitcast.9, f32[1024,384]{1,0:T(8,128)} %bitcast.11), custom_call_target="tpu_custom_call" | custom-call | flops 2038431744 | bytes 4194304 | tf_op jit(solution)/shard_map/pallas_call | solution.py:288
  6.9 2.1 %collective-permute-done = f32[1024,128]{1,0:T(8,128)S(1)} collective-permute-done((f32[1024,128]{1,0:T(8,128)}, f32[1024,128]{1,0:T(8,128)S(1)}, u32[]{:S(2)}, u32[]{:S(2)}) %collective-permute-start) | collective-permute-done | bytes 524320 | tf_op jit(solution)/shard_map/ppermute | solution.py:304
  9.1 1.1 %add.20 = f32[1024,128]{1,0:T(8,128)S(1)} add(f32[1024,128]{1,0:T(8,128)} %get-tuple-element.13, f32[1024,128]{1,0:T(8,128)S(1)} %collective-permute-done) | non-fusion elementwise | flops 131072 | bytes 1572864 | tf_op jit(solution)/shard_map/add | solution.py:310
  10.3 1.6 %collective-permute-start.1 = (f32[256,128]{1,0:T(8,128)S(1)}, f32[256,128]{1,0:T(8,128)S(1)}, u32[]{:S(2)}, u32[]{:S(2)}) collective-permute-start(f32[256,128]{1,0:T(8,128)S(1)} %get-tuple-element.22), channel_id=1, source_target_pairs={{0,16},{16,32},{32,48},{48,0},{1,17},{17,33},{33,49},{49,1},{2,18}... | collective-permute-start | bytes 393224 | tf_op jit(solution)/shard_map/ppermute | solution.py:308
  11.8 1.7 %collective-permute-start.3 = (f32[256,128]{1,0:T(8,128)S(1)}, f32[256,128]{1,0:T(8,128)S(1)}, u32[]{:S(2)}, u32[]{:S(2)}) collective-permute-start(f32[256,128]{1,0:T(8,128)S(1)} %get-tuple-element.23), channel_id=1, source_target_pairs={{0,48},{16,0},{32,16},{48,32},{1,49},{17,1},{33,17},{49,33},{2,50}... | collective-permute-start | bytes 393224 | tf_op jit(solution)/shard_map/ppermute | solution.py:308
  13.6 1.8 %collective-permute-start.2 = (f32[256,128]{1,0:T(8,128)S(1)}, f32[256,128]{1,0:T(8,128)S(1)}, u32[]{:S(2)}, u32[]{:S(2)}) collective-permute-start(f32[256,128]{1,0:T(8,128)S(1)} %get-tuple-element.24), channel_id=1, source_target_pairs={{0,32},{16,48},{32,0},{48,16},{1,33},{17,49},{33,1},{49,17},{2,34}... | collective-permute-start | bytes 393224 | tf_op jit(solution)/shard_map/ppermute | solution.py:308
  15.4 1.7 %collective-permute-done.1 = f32[256,128]{1,0:T(8,128)S(1)} collective-permute-done((f32[256,128]{1,0:T(8,128)S(1)}, f32[256,128]{1,0:T(8,128)S(1)}, u32[]{:S(2)}, u32[]{:S(2)}) %collective-permute-start.1) | collective-permute-done | bytes 131104 | tf_op jit(solution)/shard_map/ppermute | solution.py:308
  17.1 2.1 %collective-permute-done.3 = f32[256,128]{1,0:T(8,128)S(1)} collective-permute-done((f32[256,128]{1,0:T(8,128)S(1)}, f32[256,128]{1,0:T(8,128)S(1)}, u32[]{:S(2)}, u32[]{:S(2)}) %collective-permute-start.3) | collective-permute-done | bytes 131104 | tf_op jit(solution)/shard_map/ppermute | solution.py:308
  19.2 1.7 %collective-permute-done.2 = f32[256,128]{1,0:T(8,128)S(1)} collective-permute-done((f32[256,128]{1,0:T(8,128)S(1)}, f32[256,128]{1,0:T(8,128)S(1)}, u32[]{:S(2)}, u32[]{:S(2)}) %collective-permute-start.2) | collective-permute-done | bytes 131104 | tf_op jit(solution)/shard_map/ppermute | solution.py:308
  20.9 17.3 %all_to_all.10 = f32[8,32,128]{2,1,0:T(8,128)S(1)} all-to-all(f32[8,32,128]{2,1,0:T(8,128)S(1)} %bitcast.13), channel_id=1, replica_groups=mesh['dp'=4,'x'=4,'z'=8,'core'=2] {'z'}, dimensions={0} | all-to-all | bytes 262144 | tf_op jit(solution)/shard_map/all_to_all | solution.py:313
  38.3 11.5 %all_to_all.11 = f32[8,32,128]{2,1,0:T(8,128)S(1)} all-to-all(f32[8,32,128]{2,1,0:T(8,128)S(1)} %broadcast_in_dim.6), channel_id=1, replica_groups=mesh['dp'=4,'x'=4,'z'=8,'core'=2] {'z'}, dimensions={0} | all-to-all | bytes 262144 | tf_op jit(solution)/shard_map/all_to_all | solution.py:315
  49.7 2.0 %collective-permute-start.6 = (f32[256,128]{1,0:T(8,128)S(1)}, f32[256,128]{1,0:T(8,128)S(1)}, u32[]{:S(2)}, u32[]{:S(2)}) collective-permute-start(f32[256,128]{1,0:T(8,128)S(1)} %bitcast.14), channel_id=1, source_target_pairs={{0,48},{16,0},{32,16},{48,32},{1,49},{17,1},{33,17},{49,33},{2,50}... | collective-permute-start | bytes 393224 | tf_op jit(solution)/shard_map/ppermute | solution.py:308
  51.7 1.2 %collective-permute-start.5 = (f32[256,128]{1,0:T(8,128)S(1)}, f32[256,128]{1,0:T(8,128)S(1)}, u32[]{:S(2)}, u32[]{:S(2)}) collective-permute-start(f32[256,128]{1,0:T(8,128)S(1)} %bitcast.15), channel_id=1, source_target_pairs={{0,32},{16,48},{32,0},{48,16},{1,33},{17,49},{33,1},{49,17},{2,34}... | collective-permute-start | bytes 393224 | tf_op jit(solution)/shard_map/ppermute | solution.py:308
  53.0 2.7 %collective-permute-done.6 = f32[256,128]{1,0:T(8,128)S(1)} collective-permute-done((f32[256,128]{1,0:T(8,128)S(1)}, f32[256,128]{1,0:T(8,128)S(1)}, u32[]{:S(2)}, u32[]{:S(2)}) %collective-permute-start.6) | collective-permute-done | bytes 131104 | tf_op jit(solution)/shard_map/ppermute | solution.py:308
  55.6 2.6 %collective-permute-done.5 = f32[256,128]{1,0:T(8,128)S(1)} collective-permute-done((f32[256,128]{1,0:T(8,128)S(1)}, f32[256,128]{1,0:T(8,128)S(1)}, u32[]{:S(2)}, u32[]{:S(2)}) %collective-permute-start.5) | collective-permute-done | bytes 131104 | tf_op jit(solution)/shard_map/ppermute | solution.py:308
  58.2 1.4 %collective-permute-done.4 = f32[256,128]{1,0:T(8,128)S(1)} collective-permute-done((f32[256,128]{1,0:T(8,128)S(1)}, f32[256,128]{1,0:T(8,128)S(1)}, u32[]{:S(2)}, u32[]{:S(2)}) %collective-permute-start.4) | collective-permute-done | bytes 131104 | tf_op jit(solution)/shard_map/ppermute | solution.py:308
  59.8 1.9 %collective-permute-done.7.other_ref = f32[1024,128]{1,0:T(8,128)S(1)} collective-permute-done((f32[1024,128]{1,0:T(8,128)S(1)}, f32[1024,128]{1,0:T(8,128)S(1)}, u32[]{:S(2)}, u32[]{:S(2)}) %collective-permute-start.7) | collective-permute-done | bytes 524320 | tf_op jit(solution)/shard_map/ppermute | solution.py:304
  61.7 5.3 %shard_map.85 = (bf16[2,2,256,256]{3,2,1,0:T(8,128)(2,1)S(1)}, bf16[2,2,256,256]{3,2,1,0:T(8,128)(2,1)S(1)}, f32[2,384]{1,0:T(2,128)S(1)}, f32[8,1664]{1,0:T(8,128)S(1)}) custom-call(s32[3]{0:T(128)S(1)} %copy-done, f32[8]{0:T(128)S(1)} %copy-done.5, f32[1024,128]{1,0:T(8,128)S(1)} %pad_maximum_fusion.mine_ref, ...), custom_call_target="tpu_custom_call" | custom-call | flops 2717908992 | bytes 4194304 | tf_op jit(solution)/shard_map/pallas_call | solution.py:320
  66.9 0.7 collective-permute-start.10
  67.6 2.6 %collective-permute-start.9 = (f32[8,1664]{1,0:T(8,128)S(1)}, f32[8,1664]{1,0:T(8,128)S(1)}, u32[]{:S(2)}, u32[]{:S(2)}) collective-permute-start(f32[8,1664]{1,0:T(8,128)S(1)} %get-tuple-element.18.own_ref), channel_id=1, source_target_pairs={{0,128},{64,192},{128,0},{192,64},{1,129},{65,193},{129,1},{193,65... | collective-permute-start | bytes 159752 | tf_op jit(solution)/shard_map/ppermute | solution.py:308
  70.2 1.9 %collective-permute-start.8 = (f32[8,1664]{1,0:T(8,128)S(1)}, f32[8,1664]{1,0:T(8,128)S(1)}, u32[]{:S(2)}, u32[]{:S(2)}) collective-permute-start(f32[8,1664]{1,0:T(8,128)S(1)} %get-tuple-element.18.own_ref), channel_id=1, source_target_pairs={{0,64},{64,128},{128,192},{192,0},{1,65},{65,129},{129,193},{193,1... | collective-permute-start | bytes 159752 | tf_op jit(solution)/shard_map/ppermute | solution.py:308
  72.1 6.2 %shard_map.86 = f32[1024,384]{1,0:T(8,128)} custom-call(f32[1024,384]{1,0:T(8,128)S(1)} %bitcast.10, f32[1024,384]{1,0:T(8,128)S(1)} %bitcast.12, f32[384,1152]{1,0:T(8,128)S(1)} %copy-done.1, f32[384,384]{1,0:T(8,128)S(1)} %copy-done.4, bf16[2,2,256,256]{3,2,1,0:T(8,128)(2,1)S(1)} %get-tuple-element.15.att_ref, ...), custom_call_target="tpu_custom_call" | custom-call | flops 4076863488 | bytes 4194304 | tf_op jit(solution)/shard_map/pallas_call | solution.py:334
  78.3 0.6 shard_map.87
  (23 shorter events, 0.3 us)
Async XLA Ops:
  6.8 2.2 %collective-permute-start = (f32[1024,128]{1,0:T(8,128)}, f32[1024,128]{1,0:T(8,128)S(1)}, u32[]{:S(2)}, u32[]{:S(2)}) collective-permute-start(f32[1024,128]{1,0:T(8,128)} %get-tuple-element.14), channel_id=1, source_target_pairs={{0,1},{1,0},{2,3},{3,2},{4,5},{5,4},{6,7},{7,6},{8,9},{9,8},{10,11... | collective-permute-start | bytes 1572872 | tf_op jit(solution)/shard_map/ppermute | solution.py:304
  10.2 51.5 %copy-start = (s32[3]{0:T(128)S(1)}, s32[3]{0:T(128)}, u32[]{:S(2)}) copy-start(s32[3]{0:T(128)} %pad_add_fusion.place_ref) | copy-start | bytes 40
  10.2 51.5 %copy-start.1 = (f32[384,1152]{1,0:T(8,128)S(1)}, f32[384,1152]{1,0:T(8,128)}, u32[]{:S(2)}) copy-start(f32[384,1152]{1,0:T(8,128)} %w_ref.3) | copy-start | bytes 5308420
  10.2 51.5 %copy-start.4 = (f32[384,384]{1,0:T(8,128)S(1)}, f32[384,384]{1,0:T(8,128)}, u32[]{:S(2)}) copy-start(f32[384,384]{1,0:T(8,128)} %f_ref.3) | copy-start | bytes 1769476
  10.2 51.5 %copy-start.5 = (f32[8]{0:T(128)S(1)}, f32[8]{0:T(128)}, u32[]{:S(2)}) copy-start(f32[8]{0:T(128)} %sharp_ref.1) | copy-start | bytes 100
  10.3 6.8 %collective-permute-start.1 = (f32[256,128]{1,0:T(8,128)S(1)}, f32[256,128]{1,0:T(8,128)S(1)}, u32[]{:S(2)}, u32[]{:S(2)}) collective-permute-start(f32[256,128]{1,0:T(8,128)S(1)} %get-tuple-element.22), channel_id=1, source_target_pairs={{0,16},{16,32},{32,48},{48,0},{1,17},{17,33},{33,49},{49,1},{2,18}... | collective-permute-start | bytes 393224 | tf_op jit(solution)/shard_map/ppermute | solution.py:308
  11.8 7.4 %collective-permute-start.3 = (f32[256,128]{1,0:T(8,128)S(1)}, f32[256,128]{1,0:T(8,128)S(1)}, u32[]{:S(2)}, u32[]{:S(2)}) collective-permute-start(f32[256,128]{1,0:T(8,128)S(1)} %get-tuple-element.23), channel_id=1, source_target_pairs={{0,48},{16,0},{32,16},{48,32},{1,49},{17,1},{33,17},{49,33},{2,50}... | collective-permute-start | bytes 393224 | tf_op jit(solution)/shard_map/ppermute | solution.py:308
  13.6 7.3 %collective-permute-start.2 = (f32[256,128]{1,0:T(8,128)S(1)}, f32[256,128]{1,0:T(8,128)S(1)}, u32[]{:S(2)}, u32[]{:S(2)}) collective-permute-start(f32[256,128]{1,0:T(8,128)S(1)} %get-tuple-element.24), channel_id=1, source_target_pairs={{0,32},{16,48},{32,0},{48,16},{1,33},{17,49},{33,1},{49,17},{2,34}... | collective-permute-start | bytes 393224 | tf_op jit(solution)/shard_map/ppermute | solution.py:308
  49.7 5.9 %collective-permute-start.6 = (f32[256,128]{1,0:T(8,128)S(1)}, f32[256,128]{1,0:T(8,128)S(1)}, u32[]{:S(2)}, u32[]{:S(2)}) collective-permute-start(f32[256,128]{1,0:T(8,128)S(1)} %bitcast.14), channel_id=1, source_target_pairs={{0,48},{16,0},{32,16},{48,32},{1,49},{17,1},{33,17},{49,33},{2,50}... | collective-permute-start | bytes 393224 | tf_op jit(solution)/shard_map/ppermute | solution.py:308
  51.7 6.5 %collective-permute-start.5 = (f32[256,128]{1,0:T(8,128)S(1)}, f32[256,128]{1,0:T(8,128)S(1)}, u32[]{:S(2)}, u32[]{:S(2)}) collective-permute-start(f32[256,128]{1,0:T(8,128)S(1)} %bitcast.15), channel_id=1, source_target_pairs={{0,32},{16,48},{32,0},{48,16},{1,33},{17,49},{33,1},{49,17},{2,34}... | collective-permute-start | bytes 393224 | tf_op jit(solution)/shard_map/ppermute | solution.py:308
  52.9 6.6 %collective-permute-start.4 = (f32[256,128]{1,0:T(8,128)S(1)}, f32[256,128]{1,0:T(8,128)S(1)}, u32[]{:S(2)}, u32[]{:S(2)}) collective-permute-start(f32[256,128]{1,0:T(8,128)S(1)} %bitcast.16), channel_id=1, source_target_pairs={{0,16},{16,32},{32,48},{48,0},{1,17},{17,33},{33,49},{49,1},{2,18}... | collective-permute-start | bytes 393224 | tf_op jit(solution)/shard_map/ppermute | solution.py:308
  59.6 12.5 %copy-start.2 = (f32[1,1024,384]{2,1,0:T(8,128)S(1)}, f32[1,1024,384]{2,1,0:T(8,128)}, u32[]{:S(2)}) copy-start(f32[1,1024,384]{2,1,0:T(8,128)} %param.5) | copy-start | bytes 4718596
  59.6 12.5 %copy-start.3 = (f32[1,1024,384]{2,1,0:T(8,128)S(1)}, f32[1,1024,384]{2,1,0:T(8,128)}, u32[]{:S(2)}) copy-start(f32[1,1024,384]{2,1,0:T(8,128)} %param.9) | copy-start | bytes 4718596
  59.7 2.0 %collective-permute-start.7 = (f32[1024,128]{1,0:T(8,128)S(1)}, f32[1024,128]{1,0:T(8,128)S(1)}, u32[]{:S(2)}, u32[]{:S(2)}) collective-permute-start(f32[1024,128]{1,0:T(8,128)S(1)} %pad_maximum_fusion.mine_ref), channel_id=1, source_target_pairs={{0,1},{1,0},{2,3},{3,2},{4,5},{5,4},{6,7},{7,6},{8,9},{9,8},{10,11... | collective-permute-start | bytes 1572872 | tf_op jit(solution)/shard_map/ppermute | solution.py:304
  66.9 11.3 %collective-permute-start.10 = (f32[8,1664]{1,0:T(8,128)S(1)}, f32[8,1664]{1,0:T(8,128)S(1)}, u32[]{:S(2)}, u32[]{:S(2)}) collective-permute-start(f32[8,1664]{1,0:T(8,128)S(1)} %get-tuple-element.18.own_ref), channel_id=1, source_target_pairs={{0,192},{64,0},{128,64},{192,128},{1,193},{65,1},{129,65},{193,129... | collective-permute-start | bytes 159752 | tf_op jit(solution)/shard_map/ppermute | solution.py:308
  67.6 10.7 %collective-permute-start.9 = (f32[8,1664]{1,0:T(8,128)S(1)}, f32[8,1664]{1,0:T(8,128)S(1)}, u32[]{:S(2)}, u32[]{:S(2)}) collective-permute-start(f32[8,1664]{1,0:T(8,128)S(1)} %get-tuple-element.18.own_ref), channel_id=1, source_target_pairs={{0,128},{64,192},{128,0},{192,64},{1,129},{65,193},{129,1},{193,65... | collective-permute-start | bytes 159752 | tf_op jit(solution)/shard_map/ppermute | solution.py:308
  70.2 8.1 %collective-permute-start.8 = (f32[8,1664]{1,0:T(8,128)S(1)}, f32[8,1664]{1,0:T(8,128)S(1)}, u32[]{:S(2)}, u32[]{:S(2)}) collective-permute-start(f32[8,1664]{1,0:T(8,128)S(1)} %get-tuple-element.18.own_ref), channel_id=1, source_target_pairs={{0,64},{64,128},{128,192},{192,0},{1,65},{65,129},{129,193},{193,1... | collective-permute-start | bytes 159752 | tf_op jit(solution)/shard_map/ppermute | solution.py:308

commit v3 on v2

--- a/solution.py
+++ b/solution.py
@@ -40,10 +40,21 @@
 
 
 def dot3(a, b, dims):
+    (ca,), (cb,) = dims
+    return lax.dot_general(
+        jnp.concatenate([a[0], a[0], a[1]], axis=ca),
+        jnp.concatenate([b[0], b[1], b[0]], axis=cb),
+        (dims, ((), ())),
+        preferred_element_type=f32,
+    )
+
+
+def row_dot3(a, b, dims):
     d = functools.partial(
         lax.dot_general, dimension_numbers=(dims, ((), ())), preferred_element_type=f32
     )
-    return d(a[0], b[0]) + (d(a[0], b[1]) + d(a[1], b[0]))
+    both = d(jnp.concatenate(a, axis=0), b[0])
+    return both[:PICK] + both[PICK:] + d(a[0], b[1])
 
 
 def cut(pair, rows, cols):
@@ -129,29 +140,24 @@
     return sharp
 
 
-def pick_of(first, size, offset):
-    row = lax.broadcasted_iota(jnp.int32, (PICK, size), 0) + first
-    col = lax.broadcasted_iota(jnp.int32, (PICK, size), 1) + offset
-    return jnp.where(row == col, 1.0, 0.0).astype(bf16)
-
-
-def rows_of(pick, pair):
-    return tuple(jnp.dot(pick, one, preferred_element_type=f32).astype(bf16) for one in pair)
+def rows_of(first, load, size):
+    base = jnp.minimum(first // 8 * 8, size - PICK)
+    block = load(pl.ds(pl.multiple_of(base, 8), PICK))
+    return pltpu.roll(block, PICK - (first - base), 0)
 
 
 scale = 1.0 / math.sqrt(262144)
 
 
 def solve_kernel(
-    place_ref, sharp_ref, mine_ref, other_ref, w_ref, f_ref,
-    att_ref, m_ref, d_ref, rows_ref, block_ref, a_ref, b_ref,
+    place_ref, sharp_ref, w_ref, f_ref, m0, m1, m2, m3, o0, o1, o2, o3,
+    gv_ref, m_ref, d_ref, rows_ref, block_ref, a_ref, b_ref, c_ref, t_ref, att_ref,
 ):
     core, first, chip = place_ref[0], place_ref[1], place_ref[2]
     for k in range(X_CHIPS):
         origin = lax.rem(chip + X_CHIPS - k, X_CHIPS)
-        piece = pl.ds(k * QUARTER, QUARTER)
-        block_ref[core, origin] = mine_ref[piece].reshape(2, T, T)
-        block_ref[1 - core, origin] = other_ref[piece].reshape(2, T, T)
+        block_ref[core, origin] = (m0, m1, m2, m3)[k][...].reshape(2, T, T)
+        block_ref[1 - core, origin] = (o0, o1, o2, o3)[k][...].reshape(2, T, T)
     for at, (name, i, j) in enumerate(BLOCKS):
         block = block_ref[place_of(at)]
         ref = a_ref if name == "a" else b_ref
@@ -159,29 +165,45 @@
         if name == "a" and i != j:
             ref[j * T : (j + 1) * T, i * T : (i + 1) * T] = block.T
     a_s, b_s = split(a_ref[...]), split(b_ref[...])
-    wq, wk = w_ref[:, :D], w_ref[:, D : 2 * D]
-    wqs, wks, wvs, fs = split(wq), split(wk), split(w_ref[:, 2 * D :]), split(f_ref[...])
-    tq = dot3(a_s, wqs, NN)
-    tk = dot3(a_s, wks, NN)
-    c_s = split(dot3(wvs, b_s, TN))
-    q_inv = lax.rsqrt(jnp.maximum(jnp.sum(wq * tq, axis=0, keepdims=True), 0.0) + epsilon)
-    k_inv = lax.rsqrt(jnp.maximum(jnp.sum(wk * tk, axis=0, keepdims=True), 0.0) + epsilon)
-    tks = split(tk)
-    pick = pick_of(first, D, 0)
-    tq_rows, tk_rows = rows_of(pick, split(tq)), rows_of(pick, tks)
-    b_f = split(dot3(rows_of(pick, b_s), fs, NT))
+    ws, fs = split(w_ref[...]), split(f_ref[...])
+    t = dot3(a_s, cut(ws, ALL, slice(0, 2 * D)), NN)
+    t_ref[...] = t
+    c = dot3(cut(ws, ALL, slice(2 * D, 3 * D)), b_s, TN)
+    c_ref[...] = c
+    c_s = split(c)
+    square = jnp.sum(w_ref[:, : 2 * D] * t, axis=0, keepdims=True)
+    inverse = lax.rsqrt(jnp.maximum(square, 0.0) + epsilon)
+    q_inv, k_inv = inverse[:, :D], inverse[:, D:]
+    tks = split(t[:, D:])
+    t_rows = rows_of(first, lambda rows: t_ref[rows], D)
+    b_rows = rows_of(first, lambda rows: b_ref[rows], D)
+    tq_rows, tk_rows = split(t_rows[:, :D]), split(t_rows[:, D:])
     eye = eye_of(W)
-    q_sum, k_sum, q_rows, k_rows, v_rows, att_high, att_low = [], [], [], [], [], [], []
+    attentions, covs, mixers = [], [], []
+    for window, span in enumerate(WINDOWS):
+        same = masks(window)
+        cov = dot3(cut(ws, ALL, span), cut(tks, ALL, span), TN)
+        cov = jnp.where(same, cov * to_col(eye, q_inv[:, span]) * k_inv[:, span], 0.0)
+        table = jnp.where(same, jnp.exp(sharp_col(sharp_ref, window) * cov), 0.0)
+        total = jnp.sum(table, axis=1, keepdims=True)
+        attention = table / jnp.where(total > 0.0, total, 1.0)
+        att_ref[window] = attention
+        attentions.append(attention)
+        covs.append(cov)
+        mixers.append(dot3(cut(fs, span, ALL), split(attention), TN))
+    gv = split(join(mixers))
+    gv_ref[0], gv_ref[1] = gv
+    window = jnp.where(first >= D // 2, 1, 0)
+    offset = pl.multiple_of(window * (D - W), T)
+    att_rows = rows_of(first - offset, lambda rows: att_ref[window, rows], W)
+    c_part = split(c_ref[pl.ds(offset, W)])
+    rows_ref[:, 2 * D : 3 * D] = row_dot3(split(b_rows), gv, NN)[:8] * scale
+    rows_ref[:, 3 * D : 4 * D] = row_dot3(split(att_rows), c_part, NN)[:8] * scale
+    q_sum, k_sum, q_rows, k_rows = [], [], [], []
     temp = jnp.zeros((1, T), f32)
     for window, span in enumerate(WINDOWS):
-        same = masks(window)
+        attention, cov = attentions[window], covs[window]
         sharp = sharp_col(sharp_ref, window)
-        q_col = to_col(eye, q_inv[:, span])
-        cov = dot3(cut(wqs, ALL, span), cut(tks, ALL, span), TN)
-        cov = jnp.where(same, cov * q_col * k_inv[:, span], 0.0)
-        table = jnp.where(same, jnp.exp(sharp * cov), 0.0)
-        total = jnp.sum(table, axis=1, keepdims=True)
-        attention = table / jnp.where(total > 0.0, total, 1.0)
         attention_grad = dot3(cut(fs, span, ALL), cut(c_s, span, ALL), NT)
         inner = jnp.sum(attention * attention_grad, axis=1, keepdims=True)
         score_grad = attention * (attention_grad - inner)
@@ -189,16 +211,10 @@
         by_feature = jnp.sum(weighed, axis=1, keepdims=True)
         q_sum.append(to_row(eye, sharp * by_feature))
         k_sum.append(jnp.sum(sharp * weighed, axis=0, keepdims=True))
-        m_s = split(sharp * score_grad * q_col * k_inv[:, span])
+        m_s = split(sharp * score_grad * to_col(eye, q_inv[:, span]) * k_inv[:, span])
         m_ref[0, window], m_ref[1, window] = m_s
-        att_s = split(attention)
-        att_ref[0, window], att_ref[1, window] = att_s
-        q_rows.append(dot3(cut(tk_rows, ALL, span), m_s, NT))
-        k_rows.append(dot3(cut(tq_rows, ALL, span), m_s, NN))
-        v_rows.append(dot3(cut(b_f, ALL, span), att_s, NN))
-        high, low = rows_of(pick_of(first, W, window * (D - W)), att_s)
-        att_high.append(high)
-        att_low.append(low)
+        q_rows.append(row_dot3(cut(tk_rows, ALL, span), m_s, NT))
+        k_rows.append(row_dot3(cut(tq_rows, ALL, span), m_s, NN))
         _, head = heads_of((W, T), 0, window)
         lane = lax.broadcasted_iota(jnp.int32, (W, T), 1)
         temp += jnp.sum(jnp.where(head == lane, by_feature, 0.0), axis=0, keepdims=True)
@@ -206,38 +222,35 @@
     d_k = join(k_sum) * (k_inv * k_inv)
     d_ref[0:1] = d_q
     d_ref[1:2] = d_k
-    both = [high.astype(f32) + low.astype(f32) for high, low in (tq_rows, tk_rows)]
-    rows_ref[:, :D] = (join(q_rows) - both[0] * d_q)[:8] * scale
-    rows_ref[:, D : 2 * D] = (join(k_rows) - both[1] * d_k)[:8] * scale
-    rows_ref[:, 2 * D : 3 * D] = join(v_rows)[:8] * scale
-    rows_ref[:, 3 * D : 4 * D] = dot3((join(att_high), join(att_low)), c_s, NN)[:8] * scale
+    rows_ref[:, :D] = (join(q_rows) - t_rows[:, :D] * d_q)[:8] * scale
+    rows_ref[:, D : 2 * D] = (join(k_rows) - t_rows[:, D:] * d_k)[:8] * scale
     rows_ref[:, 4 * D :] = jnp.broadcast_to(temp * scale, (8, T))
 
 
-def output_kernel(x_ref, u_ref, w_ref, f_ref, att_ref, m_ref, d_ref, out_hbm, out_ref, sems):
-    wq, wk = w_ref[:, :D], w_ref[:, D : 2 * D]
-    wqs, wks, wvs, fs = split(wq), split(wk), split(w_ref[:, 2 * D :]), split(f_ref[...])
-    q_parts, k_parts, v_parts = [], [], []
+def output_kernel(
+    x_ref, u_ref, w_ref, gv_ref, m_ref, d_ref, out_hbm, out_ref, sems
+):
+    ws = split(w_ref[...])
+    q_parts, k_parts = [], []
     for window, span in enumerate(WINDOWS):
         m_s = (m_ref[0, window], m_ref[1, window])
-        att_s = (att_ref[0, window], att_ref[1, window])
-        q_parts.append(dot3(cut(wks, ALL, span), m_s, NT))
-        k_parts.append(dot3(cut(wqs, ALL, span), m_s, NN))
-        v_parts.append(dot3(cut(fs, span, ALL), att_s, TN))
-    gq = split(join(q_parts) - wq * d_ref[0:1])
-    gk = split(join(k_parts) - wk * d_ref[1:2])
-    gv = split(join(v_parts))
-    p = split(dot3(gq, wqs, NT) + dot3(gk, wks, NT))
-    r = split(dot3(gv, wvs, NT))
-    both = tuple(jnp.concatenate([one, two], axis=0) for one, two in zip(p, r))
+        q_parts.append(dot3(cut(ws, ALL, slice(D + span.start, D + span.stop)), m_s, NT))
+        k_parts.append(dot3(cut(ws, ALL, span), m_s, NN))
+    gq = split(join(q_parts) - w_ref[:, :D] * d_ref[0:1])
+    gk = split(join(k_parts) - w_ref[:, D : 2 * D] * d_ref[1:2])
+    g = tuple(jnp.concatenate([one, two], axis=1) for one, two in zip(gq, gk))
+    gv = (gv_ref[0], gv_ref[1])
+    p = split(dot3(g, cut(ws, ALL, slice(0, 2 * D)), NT))
+    r = split(dot3(gv, cut(ws, ALL, slice(2 * D, 3 * D)), NT))
+    factors = tuple(jnp.concatenate([one, two], axis=0) for one, two in zip(p, r))
     tokens = x_ref.shape[0]
-    step = tokens // 4
+    step = tokens // 8
     copies = []
-    for k in range(4):
+    for k in range(8):
         piece = pl.ds(k * step, step)
         xs, us = split(x_ref[piece]), split(u_ref[piece])
         token = tuple(jnp.concatenate([one, two], axis=1) for one, two in zip(xs, us))
-        out_ref[piece] = dot3(token, both, NN)
+        out_ref[piece] = dot3(token, factors, NN)
         copy = pltpu.make_async_copy(out_ref.at[piece], out_hbm.at[piece], sems.at[k])
         copy.start()
         copies.append(copy)
@@ -284,6 +297,9 @@
     place = jnp.stack([core, ctx * ROWS, chip]).astype(jnp.int32)
     unit = 2 * 3 * D * D * D
 
+    def in_hbm(array):
+        return pltpu.with_memory_space_constraint(array, pltpu.HBM)
+
     half = ((HALF, T), f32)
     keep, send = call(
         gram_kernel,
@@ -297,8 +313,7 @@
             pltpu.SemaphoreType.DMA((8,)),
         ],
         flops=6 * unit,
-        limit=56,
-    )(place, x, u)
+    )(place, in_hbm(x), in_hbm(u))
 
     def swap(array):
         return lax.ppermute(array, "core", [(0, 1), (1, 0)])
@@ -313,38 +328,40 @@
     part = lax.all_to_all(part.reshape(Z_CHIPS, -1, T), "z", 0, 0, tiled=True).sum(axis=0)
     part = jnp.broadcast_to(part, (Z_CHIPS,) + part.shape)
     part = lax.all_to_all(part, "z", 0, 0, tiled=True).reshape(QUARTER, T)
-    mine = jnp.concatenate([part] + [shift(part, "x", k) for k in range(1, X_CHIPS)])
-    other = swap(mine)
-
-    windows = ((2, 2, W, W), bf16)
-    att, m, diagonal, rows = call(
+    mine = [part] + [shift(part, "x", k) for k in range(1, X_CHIPS)]
+    other = [swap(piece) for piece in mine]
+
+    gv, m, diagonal, rows = call(
         solve_kernel,
-        [smem, smem] + [vmem] * 4,
+        [smem, smem] + [vmem] * 10,
         [vmem] * 4,
-        [windows, windows, ((2, D), f32), ((8, 4 * D + T), f32)],
+        [((2, D, D), bf16), ((2, 2, W, W), bf16), ((2, D), f32), ((8, 4 * D + T), f32)],
         [
             pltpu.VMEM((CORES, X_CHIPS, 2, T, T), f32),
             pltpu.VMEM((D, D), f32),
             pltpu.VMEM((D, D), f32),
+            pltpu.VMEM((D, D), f32),
+            pltpu.VMEM((D, 2 * D), f32),
+            pltpu.VMEM((2, W, W), f32),
         ],
         flops=8 * unit,
-    )(place, sharpness_per_view, mine, other, stacked_projector, final_projector)
-
-    others = [shift(rows, "dp", k) for k in range(1, lax.axis_size("dp"))]
+    )(place, sharpness_per_view, stacked_projector, final_projector, *mine, *other)
+
+    one, two, three = [shift(rows, "dp", k) for k in range(1, lax.axis_size("dp"))]
     (input_grad,) = call(
         output_kernel,
-        [vmem] * 7,
+        [vmem] * 6,
         [hbm],
         [((tokens, D), f32)],
-        [pltpu.VMEM((tokens, D), f32), pltpu.SemaphoreType.DMA((4,))],
+        [pltpu.VMEM((tokens, D), f32), pltpu.SemaphoreType.DMA((8,))],
         flops=12 * unit,
-    )(x, u, stacked_projector, final_projector, att, m, diagonal)
+    )(x, u, stacked_projector, gv, m, diagonal)
     mixer_grad, output_grad, sharpness_grad = call(
         total_kernel,
         [vmem] * 4,
         [vmem] * 3,
         [((ROWS, 3 * D), f32), ((ROWS, D), f32), ((1, VIEWS), f32)],
-    )(rows, *others)
+    )(rows, one, two, three)
     return input_grad[None], mixer_grad, output_grad, sharpness_grad.reshape(VIEWS)
 
 

time: 79.2 us -> 74.3 us (0.938)
  Pallas kernels: 17.6 us -> 15.6 us
  other arithmetic: 1.85 us -> 0.17 us
    pallas_call x1, Pallas kernels: 5.55 us -> 4.48 us  [body(): call(gram_kernel, [smem, hbm, hbm], [vmem] * 2, [half] * 2, [pltpu.VMEM((...]
    add x1, other arithmetic: 1.12 us -> 0.05 us  [body(): part = (keep + swap(send)).reshape(X_CHIPS, QUARTER, T)]
    pallas_call x2, Pallas kernels: 11.4 us -> 10.5 us  [the longest x1 5.7 us: body(): call(output_kernel, [vmem] * 6, [hbm], [((tokens, D), f32)], [pltpu.VMEM(...]
    ppermute x2 -> x5, waiting for transfers between devices: 4 us -> 3.23 us  [swap(): return lax.ppermute(array, 'core', [(0, 1), (1, 0)])]
  transfers between devices with their start and end apart: 11 -> 14, of which waited for: 8 -> 8; matrix products, arithmetic and copies ran while one was open for 0% -> 0% of each run, Pallas kernels for 8% -> 8%
where the time goes in v3:
time: 74.3 us; the launch traced here: 74.1 us
  blocking collectives  28.8 us (39%)
  Pallas kernels  15.6 us (21%)
  waiting for transfers between devices  15.4 us (21%)
  starting transfers between devices  13.4 us (18%)
    all_to_all x1, blocking collectives, body(): lax.all_to_all(part.reshape(Z_CHIPS, -1, T), 'z', 0, 0, tiled=True)  17.3 us
    ppermute x9, starting transfers between devices, shift(): lax.ppermute(array, axis, [(i, (i + by) % size) for i in range(size)])  13.3 us
    ppermute x9, waiting for transfers between devices, shift(): lax.ppermute(array, axis, [(i, (i + by) % size) for i in range(size)])  12.1 us
    all_to_all x1, blocking collectives, body(): part = lax.all_to_all(part, 'z', 0, 0, tiled=True).reshape(QUARTER, T)  11.5 us
    pallas_call x1, Pallas kernels, body(): call(output_kernel, [vmem] * 6, [hbm], [((tokens, D), f32)], [pltpu.VMEM(...  5.7 us
    pallas_call x1, Pallas kernels, body(): call(solve_kernel, [smem, smem] + [vmem] * 10, [vmem] * 4, [((2, D, D), b...  4.75 us
    pallas_call x1, Pallas kernels, body(): call(gram_kernel, [smem, hbm, hbm], [vmem] * 2, [half] * 2, [pltpu.VMEM((...  4.48 us
    ppermute x5, waiting for transfers between devices, swap(): return lax.ppermute(array, 'core', [(0, 1), (1, 0)])  3.23 us
  transfers between devices with their start and end apart: 14, of which 8 were waited for; matrix products, arithmetic and copies ran while one was open for 0% of the time, Pallas kernels for 8%

profile of v3, /device:TPU:8, one launch (start us, length us, event | category | flops | bytes accessed | tf_op | source)
XLA Modules:
  0.0 74.1 jit_solution(31574155079547756)
XLA Ops:
  0.6 0.1 pad_add_fusion.place_ref
  0.7 4.5 %shard_map.84 = (f32[1024,128]{1,0:T(8,128)S(1)}, f32[1024,128]{1,0:T(8,128)S(1)}) custom-call(s32[3]{0:T(128)S(1)} %pad_add_fusion.place_ref, f32[1024,384]{1,0:T(8,128)} %bitcast.14, f32[1024,384]{1,0:T(8,128)} %bitcast.16), custom_call_target="tpu_custom_call" | custom-call | flops 2038431744 | bytes 4194304 | tf_op jit(solution)/shard_map/pallas_call | solution.py:304
  5.2 0.1 collective-permute-start
  5.3 1.9 %collective-permute-done = f32[1024,128]{1,0:T(8,128)S(1)} collective-permute-done((f32[1024,128]{1,0:T(8,128)S(1)}, f32[1024,128]{1,0:T(8,128)S(1)}, u32[]{:S(2)}, u32[]{:S(2)}) %collective-permute-start) | collective-permute-done | bytes 524320 | tf_op jit(solution)/shard_map/ppermute | solution.py:319
  7.3 1.6 %collective-permute-start.1 = (f32[256,128]{1,0:T(8,128)S(1)}, f32[256,128]{1,0:T(8,128)S(1)}, u32[]{:S(2)}, u32[]{:S(2)}) collective-permute-start(f32[256,128]{1,0:T(8,128)S(1)} %get-tuple-element.22), channel_id=1, source_target_pairs={{0,16},{16,32},{32,48},{48,0},{1,17},{17,33},{33,49},{49,1},{2,18}... | collective-permute-start | bytes 393224 | tf_op jit(solution)/shard_map/ppermute | solution.py:323
  8.9 1.7 %collective-permute-start.3 = (f32[256,128]{1,0:T(8,128)S(1)}, f32[256,128]{1,0:T(8,128)S(1)}, u32[]{:S(2)}, u32[]{:S(2)}) collective-permute-start(f32[256,128]{1,0:T(8,128)S(1)} %get-tuple-element.23), channel_id=1, source_target_pairs={{0,48},{16,0},{32,16},{48,32},{1,49},{17,1},{33,17},{49,33},{2,50}... | collective-permute-start | bytes 393224 | tf_op jit(solution)/shard_map/ppermute | solution.py:323
  10.6 1.8 %collective-permute-start.2 = (f32[256,128]{1,0:T(8,128)S(1)}, f32[256,128]{1,0:T(8,128)S(1)}, u32[]{:S(2)}, u32[]{:S(2)}) collective-permute-start(f32[256,128]{1,0:T(8,128)S(1)} %get-tuple-element.24), channel_id=1, source_target_pairs={{0,32},{16,48},{32,0},{48,16},{1,33},{17,49},{33,1},{49,17},{2,34}... | collective-permute-start | bytes 393224 | tf_op jit(solution)/shard_map/ppermute | solution.py:323
  12.4 1.7 %collective-permute-done.1 = f32[256,128]{1,0:T(8,128)S(1)} collective-permute-done((f32[256,128]{1,0:T(8,128)S(1)}, f32[256,128]{1,0:T(8,128)S(1)}, u32[]{:S(2)}, u32[]{:S(2)}) %collective-permute-start.1) | collective-permute-done | bytes 131104 | tf_op jit(solution)/shard_map/ppermute | solution.py:323
  14.1 2.1 %collective-permute-done.3 = f32[256,128]{1,0:T(8,128)S(1)} collective-permute-done((f32[256,128]{1,0:T(8,128)S(1)}, f32[256,128]{1,0:T(8,128)S(1)}, u32[]{:S(2)}, u32[]{:S(2)}) %collective-permute-start.3) | collective-permute-done | bytes 131104 | tf_op jit(solution)/shard_map/ppermute | solution.py:323
  16.2 1.7 %collective-permute-done.2 = f32[256,128]{1,0:T(8,128)S(1)} collective-permute-done((f32[256,128]{1,0:T(8,128)S(1)}, f32[256,128]{1,0:T(8,128)S(1)}, u32[]{:S(2)}, u32[]{:S(2)}) %collective-permute-start.2) | collective-permute-done | bytes 131104 | tf_op jit(solution)/shard_map/ppermute | solution.py:323
  18.0 17.3 %all_to_all.10 = f32[8,32,128]{2,1,0:T(8,128)S(1)} all-to-all(f32[8,32,128]{2,1,0:T(8,128)S(1)} %bitcast.18), channel_id=1, replica_groups=mesh['dp'=4,'x'=4,'z'=8,'core'=2] {'z'}, dimensions={0} | all-to-all | bytes 262144 | tf_op jit(solution)/shard_map/all_to_all | solution.py:328
  35.3 11.5 %all_to_all.11 = f32[8,32,128]{2,1,0:T(8,128)S(1)} all-to-all(f32[8,32,128]{2,1,0:T(8,128)S(1)} %broadcast_in_dim.6), channel_id=1, replica_groups=mesh['dp'=4,'x'=4,'z'=8,'core'=2] {'z'}, dimensions={0} | all-to-all | bytes 262144 | tf_op jit(solution)/shard_map/all_to_all | solution.py:330
  46.8 2.0 %collective-permute-start.6 = (f32[256,128]{1,0:T(8,128)S(1)}, f32[256,128]{1,0:T(8,128)S(1)}, u32[]{:S(2)}, u32[]{:S(2)}) collective-permute-start(f32[256,128]{1,0:T(8,128)S(1)} %bitcast.9), channel_id=1, source_target_pairs={{0,48},{16,0},{32,16},{48,32},{1,49},{17,1},{33,17},{49,33},{2,50}... | collective-permute-start | bytes 393224 | tf_op jit(solution)/shard_map/ppermute | solution.py:323
  48.8 1.2 %collective-permute-start.5 = (f32[256,128]{1,0:T(8,128)S(1)}, f32[256,128]{1,0:T(8,128)S(1)}, u32[]{:S(2)}, u32[]{:S(2)}) collective-permute-start(f32[256,128]{1,0:T(8,128)S(1)} %bitcast.10), channel_id=1, source_target_pairs={{0,32},{16,48},{32,0},{48,16},{1,33},{17,49},{33,1},{49,17},{2,34}... | collective-permute-start | bytes 393224 | tf_op jit(solution)/shard_map/ppermute | solution.py:323
  50.0 2.7 %collective-permute-done.6.m3 = f32[256,128]{1,0:T(8,128)S(1)} collective-permute-done((f32[256,128]{1,0:T(8,128)S(1)}, f32[256,128]{1,0:T(8,128)S(1)}, u32[]{:S(2)}, u32[]{:S(2)}) %collective-permute-start.6) | collective-permute-done | bytes 131104 | tf_op jit(solution)/shard_map/ppermute | solution.py:323
  52.7 2.6 %collective-permute-done.5.m2 = f32[256,128]{1,0:T(8,128)S(1)} collective-permute-done((f32[256,128]{1,0:T(8,128)S(1)}, f32[256,128]{1,0:T(8,128)S(1)}, u32[]{:S(2)}, u32[]{:S(2)}) %collective-permute-start.5) | collective-permute-done | bytes 131104 | tf_op jit(solution)/shard_map/ppermute | solution.py:323
  55.3 1.4 %collective-permute-done.4.m1 = f32[256,128]{1,0:T(8,128)S(1)} collective-permute-done((f32[256,128]{1,0:T(8,128)S(1)}, f32[256,128]{1,0:T(8,128)S(1)}, u32[]{:S(2)}, u32[]{:S(2)}) %collective-permute-start.4) | collective-permute-done | bytes 131104 | tf_op jit(solution)/shard_map/ppermute | solution.py:323
  56.7 1.3 %collective-permute-done.8.o1 = f32[256,128]{1,0:T(8,128)S(1)} collective-permute-done((f32[256,128]{1,0:T(8,128)S(1)}, f32[256,128]{1,0:T(8,128)S(1)}, u32[]{:S(2)}, u32[]{:S(2)}) %collective-permute-start.8) | collective-permute-done | bytes 131104 | tf_op jit(solution)/shard_map/ppermute | solution.py:319
  58.0 4.7 %shard_map.85 = (bf16[2,384,384]{2,1,0:T(8,128)(2,1)S(1)}, bf16[2,2,256,256]{3,2,1,0:T(8,128)(2,1)S(1)}, f32[2,384]{1,0:T(2,128)S(1)}, f32[8,1664]{1,0:T(8,128)S(1)}) custom-call(s32[3]{0:T(128)S(1)} %pad_add_fusion.place_ref, f32[8]{0:T(128)S(1)} %copy-done.4, f32[384,1152]{1,0:T(8,128)S(1)} %copy-done, f32[384,384]{1,0:T(8,128)S(1)} %copy-done.3, ...), custom_call_target="tpu_custom_call" | custom-call | flops 2717908992 | bytes 4194304 | tf_op jit(solution)/shard_map/pallas_call | solution.py:334
  62.8 0.5 collective-permute-start.13
  63.2 2.6 %collective-permute-start.12 = (f32[8,1664]{1,0:T(8,128)S(1)}, f32[8,1664]{1,0:T(8,128)S(1)}, u32[]{:S(2)}, u32[]{:S(2)}) collective-permute-start(f32[8,1664]{1,0:T(8,128)S(1)} %get-tuple-element.18.own_ref), channel_id=1, source_target_pairs={{0,128},{64,192},{128,0},{192,64},{1,129},{65,193},{129,1},{193,65... | collective-permute-start | bytes 159752 | tf_op jit(solution)/shard_map/ppermute | solution.py:323
  65.8 1.9 %collective-permute-start.11 = (f32[8,1664]{1,0:T(8,128)S(1)}, f32[8,1664]{1,0:T(8,128)S(1)}, u32[]{:S(2)}, u32[]{:S(2)}) collective-permute-start(f32[8,1664]{1,0:T(8,128)S(1)} %get-tuple-element.18.own_ref), channel_id=1, source_target_pairs={{0,64},{64,128},{128,192},{192,0},{1,65},{65,129},{129,193},{193,1... | collective-permute-start | bytes 159752 | tf_op jit(solution)/shard_map/ppermute | solution.py:323
  67.7 5.7 %shard_map.86 = f32[1024,384]{1,0:T(8,128)} custom-call(f32[1024,384]{1,0:T(8,128)S(1)} %bitcast.15, f32[1024,384]{1,0:T(8,128)S(1)} %bitcast.17, f32[384,1152]{1,0:T(8,128)S(1)} %copy-done, bf16[2,384,384]{2,1,0:T(8,128)(2,1)S(1)} %get-tuple-element.15.gv_ref, bf16[2,2,256,256]{3,2,1,0:T(8,128)(2,1)S(1)} %get-tuple-element.16.m_ref, ...), custom_call_target="tpu_custom_call" | custom-call | flops 4076863488 | bytes 4194304 | tf_op jit(solution)/shard_map/pallas_call | solution.py:351
  73.4 0.6 shard_map.87
  (26 shorter events, 0.2 us)
Async XLA Ops:
  5.2 2.0 %collective-permute-start = (f32[1024,128]{1,0:T(8,128)S(1)}, f32[1024,128]{1,0:T(8,128)S(1)}, u32[]{:S(2)}, u32[]{:S(2)}) collective-permute-start(f32[1024,128]{1,0:T(8,128)S(1)} %get-tuple-element.14), channel_id=1, source_target_pairs={{0,1},{1,0},{2,3},{3,2},{4,5},{5,4},{6,7},{7,6},{8,9},{9,8},{10,11... | collective-permute-start | bytes 1572872 | tf_op jit(solution)/shard_map/ppermute | solution.py:319
  7.2 50.8 %copy-start = (f32[384,1152]{1,0:T(8,128)S(1)}, f32[384,1152]{1,0:T(8,128)}, u32[]{:S(2)}) copy-start(f32[384,1152]{1,0:T(8,128)} %w_ref.3) | copy-start | bytes 5308420
  7.2 50.8 %copy-start.3 = (f32[384,384]{1,0:T(8,128)S(1)}, f32[384,384]{1,0:T(8,128)}, u32[]{:S(2)}) copy-start(f32[384,384]{1,0:T(8,128)} %f_ref.1) | copy-start | bytes 1769476
  7.2 50.8 %copy-start.4 = (f32[8]{0:T(128)S(1)}, f32[8]{0:T(128)}, u32[]{:S(2)}) copy-start(f32[8]{0:T(128)} %sharp_ref.1) | copy-start | bytes 100
  7.3 6.8 %collective-permute-start.1 = (f32[256,128]{1,0:T(8,128)S(1)}, f32[256,128]{1,0:T(8,128)S(1)}, u32[]{:S(2)}, u32[]{:S(2)}) collective-permute-start(f32[256,128]{1,0:T(8,128)S(1)} %get-tuple-element.22), channel_id=1, source_target_pairs={{0,16},{16,32},{32,48},{48,0},{1,17},{17,33},{33,49},{49,1},{2,18}... | collective-permute-start | bytes 393224 | tf_op jit(solution)/shard_map/ppermute | solution.py:323
  8.9 7.4 %collective-permute-start.3 = (f32[256,128]{1,0:T(8,128)S(1)}, f32[256,128]{1,0:T(8,128)S(1)}, u32[]{:S(2)}, u32[]{:S(2)}) collective-permute-start(f32[256,128]{1,0:T(8,128)S(1)} %get-tuple-element.23), channel_id=1, source_target_pairs={{0,48},{16,0},{32,16},{48,32},{1,49},{17,1},{33,17},{49,33},{2,50}... | collective-permute-start | bytes 393224 | tf_op jit(solution)/shard_map/ppermute | solution.py:323
  10.6 7.3 %collective-permute-start.2 = (f32[256,128]{1,0:T(8,128)S(1)}, f32[256,128]{1,0:T(8,128)S(1)}, u32[]{:S(2)}, u32[]{:S(2)}) collective-permute-start(f32[256,128]{1,0:T(8,128)S(1)} %get-tuple-element.24), channel_id=1, source_target_pairs={{0,32},{16,48},{32,0},{48,16},{1,33},{17,49},{33,1},{49,17},{2,34}... | collective-permute-start | bytes 393224 | tf_op jit(solution)/shard_map/ppermute | solution.py:323
  46.8 20.9 %copy-start.1 = (f32[1,1024,384]{2,1,0:T(8,128)S(1)}, f32[1,1024,384]{2,1,0:T(8,128)}, u32[]{:S(2)}) copy-start(f32[1,1024,384]{2,1,0:T(8,128)} %param.5) | copy-start | bytes 4718596
  46.8 20.9 %copy-start.2 = (f32[1,1024,384]{2,1,0:T(8,128)S(1)}, f32[1,1024,384]{2,1,0:T(8,128)}, u32[]{:S(2)}) copy-start(f32[1,1024,384]{2,1,0:T(8,128)} %param.9) | copy-start | bytes 4718596
  46.8 5.9 %collective-permute-start.6 = (f32[256,128]{1,0:T(8,128)S(1)}, f32[256,128]{1,0:T(8,128)S(1)}, u32[]{:S(2)}, u32[]{:S(2)}) collective-permute-start(f32[256,128]{1,0:T(8,128)S(1)} %bitcast.9), channel_id=1, source_target_pairs={{0,48},{16,0},{32,16},{48,32},{1,49},{17,1},{33,17},{49,33},{2,50}... | collective-permute-start | bytes 393224 | tf_op jit(solution)/shard_map/ppermute | solution.py:323
  48.8 6.5 %collective-permute-start.5 = (f32[256,128]{1,0:T(8,128)S(1)}, f32[256,128]{1,0:T(8,128)S(1)}, u32[]{:S(2)}, u32[]{:S(2)}) collective-permute-start(f32[256,128]{1,0:T(8,128)S(1)} %bitcast.10), channel_id=1, source_target_pairs={{0,32},{16,48},{32,0},{48,16},{1,33},{17,49},{33,1},{49,17},{2,34}... | collective-permute-start | bytes 393224 | tf_op jit(solution)/shard_map/ppermute | solution.py:323
  50.0 6.6 %collective-permute-start.4 = (f32[256,128]{1,0:T(8,128)S(1)}, f32[256,128]{1,0:T(8,128)S(1)}, u32[]{:S(2)}, u32[]{:S(2)}) collective-permute-start(f32[256,128]{1,0:T(8,128)S(1)} %bitcast.11), channel_id=1, source_target_pairs={{0,16},{16,32},{32,48},{48,0},{1,17},{17,33},{33,49},{49,1},{2,18}... | collective-permute-start | bytes 393224 | tf_op jit(solution)/shard_map/ppermute | solution.py:323
  50.0 6.6 %collective-permute-start.7 = (f32[256,128]{1,0:T(8,128)S(1)}, f32[256,128]{1,0:T(8,128)S(1)}, u32[]{:S(2)}, u32[]{:S(2)}) collective-permute-start(f32[256,128]{1,0:T(8,128)S(1)} %bitcast.12), channel_id=1, source_target_pairs={{0,1},{1,0},{2,3},{3,2},{4,5},{5,4},{6,7},{7,6},{8,9},{9,8},{10,11... | collective-permute-start | bytes 393224 | tf_op jit(solution)/shard_map/ppermute | solution.py:319
  52.7 4.0 %collective-permute-start.10 = (f32[256,128]{1,0:T(8,128)S(1)}, f32[256,128]{1,0:T(8,128)S(1)}, u32[]{:S(2)}, u32[]{:S(2)}) collective-permute-start(f32[256,128]{1,0:T(8,128)S(1)} %collective-permute-done.6.m3), channel_id=1, source_target_pairs={{0,1},{1,0},{2,3},{3,2},{4,5},{5,4},{6,7},{7,6},{8,9},{9,8},{10,11... | collective-permute-start | bytes 393224 | tf_op jit(solution)/shard_map/ppermute | solution.py:319
  55.3 1.4 %collective-permute-start.9 = (f32[256,128]{1,0:T(8,128)S(1)}, f32[256,128]{1,0:T(8,128)S(1)}, u32[]{:S(2)}, u32[]{:S(2)}) collective-permute-start(f32[256,128]{1,0:T(8,128)S(1)} %collective-permute-done.5.m2), channel_id=1, source_target_pairs={{0,1},{1,0},{2,3},{3,2},{4,5},{5,4},{6,7},{7,6},{8,9},{9,8},{10,11... | collective-permute-start | bytes 393224 | tf_op jit(solution)/shard_map/ppermute | solution.py:319
  56.6 1.3 %collective-permute-start.8 = (f32[256,128]{1,0:T(8,128)S(1)}, f32[256,128]{1,0:T(8,128)S(1)}, u32[]{:S(2)}, u32[]{:S(2)}) collective-permute-start(f32[256,128]{1,0:T(8,128)S(1)} %collective-permute-done.4.m1), channel_id=1, source_target_pairs={{0,1},{1,0},{2,3},{3,2},{4,5},{5,4},{6,7},{7,6},{8,9},{9,8},{10,11... | collective-permute-start | bytes 393224 | tf_op jit(solution)/shard_map/ppermute | solution.py:319
  62.8 10.7 %collective-permute-start.13 = (f32[8,1664]{1,0:T(8,128)S(1)}, f32[8,1664]{1,0:T(8,128)S(1)}, u32[]{:S(2)}, u32[]{:S(2)}) collective-permute-start(f32[8,1664]{1,0:T(8,128)S(1)} %get-tuple-element.18.own_ref), channel_id=1, source_target_pairs={{0,192},{64,0},{128,64},{192,128},{1,193},{65,1},{129,65},{193,129... | collective-permute-start | bytes 159752 | tf_op jit(solution)/shard_map/ppermute | solution.py:323
  63.2 10.2 %collective-permute-start.12 = (f32[8,1664]{1,0:T(8,128)S(1)}, f32[8,1664]{1,0:T(8,128)S(1)}, u32[]{:S(2)}, u32[]{:S(2)}) collective-permute-start(f32[8,1664]{1,0:T(8,128)S(1)} %get-tuple-element.18.own_ref), channel_id=1, source_target_pairs={{0,128},{64,192},{128,0},{192,64},{1,129},{65,193},{129,1},{193,65... | collective-permute-start | bytes 159752 | tf_op jit(solution)/shard_map/ppermute | solution.py:323
  65.8 7.6 %collective-permute-start.11 = (f32[8,1664]{1,0:T(8,128)S(1)}, f32[8,1664]{1,0:T(8,128)S(1)}, u32[]{:S(2)}, u32[]{:S(2)}) collective-permute-start(f32[8,1664]{1,0:T(8,128)S(1)} %get-tuple-element.18.own_ref), channel_id=1, source_target_pairs={{0,64},{64,128},{128,192},{192,0},{1,65},{65,129},{129,193},{193,1... | collective-permute-start | bytes 159752 | tf_op jit(solution)/shard_map/ppermute | solution.py:323

commit v4 on v3

--- a/solution.py
+++ b/solution.py
@@ -325,9 +325,8 @@
     part = (keep + swap(send)).reshape(X_CHIPS, QUARTER, T)
     others = [shift(part[k], "x", k) for k in range(1, X_CHIPS)]
     part = part[0] + others[0] + others[1] + others[2]
-    part = lax.all_to_all(part.reshape(Z_CHIPS, -1, T), "z", 0, 0, tiled=True).sum(axis=0)
-    part = jnp.broadcast_to(part, (Z_CHIPS,) + part.shape)
-    part = lax.all_to_all(part, "z", 0, 0, tiled=True).reshape(QUARTER, T)
+    for apart in (4, 2, 1):
+        part = part + lax.ppermute(part, "z", [(i, i ^ apart) for i in range(Z_CHIPS)])
     mine = [part] + [shift(part, "x", k) for k in range(1, X_CHIPS)]
     other = [swap(piece) for piece in mine]
 

time: 74.3 us -> 68.8 us (0.926)
  the two profiles are of different devices: /device:TPU:8 before, /device:TPU:136 now
where the time goes in v4:
time: 68.8 us; the launch traced here: 68.7 us
  waiting for transfers between devices  36.8 us (53%)
  Pallas kernels  15.6 us (23%)
  starting transfers between devices  15.3 us (22%)
  between operations  0.79 us (1%)
    ppermute x3, waiting for transfers between devices, body(): lax.ppermute(part, 'z', [(i, i ^ apart) for i in range(Z_CHIPS)])  21.6 us
    ppermute x9, starting transfers between devices, shift(): lax.ppermute(array, axis, [(i, (i + by) % size) for i in range(size)])  13.2 us
    ppermute x9, waiting for transfers between devices, shift(): lax.ppermute(array, axis, [(i, (i + by) % size) for i in range(size)])  12 us
    pallas_call x1, Pallas kernels, body(): call(output_kernel, [vmem] * 6, [hbm], [((tokens, D), f32)], [pltpu.VMEM(...  5.7 us
    pallas_call x1, Pallas kernels, body(): call(solve_kernel, [smem, smem] + [vmem] * 10, [vmem] * 4, [((2, D, D), b...  4.74 us
    pallas_call x1, Pallas kernels, body(): call(gram_kernel, [smem, hbm, hbm], [vmem] * 2, [half] * 2, [pltpu.VMEM((...  4.48 us
    ppermute x5, waiting for transfers between devices, swap(): return lax.ppermute(array, 'core', [(0, 1), (1, 0)])  3.23 us
    ppermute x3, starting transfers between devices, body(): lax.ppermute(part, 'z', [(i, i ^ apart) for i in range(Z_CHIPS)])  2.01 us
  transfers between devices with their start and end apart: 17, of which 11 were waited for; matrix products, arithmetic and copies ran while one was open for 0% of the time, Pallas kernels for 8%

profile of v4, /device:TPU:136, one launch (start us, length us, event | category | flops | bytes accessed | tf_op | source)
XLA Modules:
  0.0 68.7 jit_solution(17540100454604991201)
XLA Ops:
  0.7 4.5 %shard_map.84 = (f32[1024,128]{1,0:T(8,128)S(1)}, f32[1024,128]{1,0:T(8,128)S(1)}) custom-call(s32[3]{0:T(128)S(1)} %pad_add_fusion.place_ref, f32[1024,384]{1,0:T(8,128)} %bitcast.7, f32[1024,384]{1,0:T(8,128)} %bitcast.9), custom_call_target="tpu_custom_call" | custom-call | flops 2038431744 | bytes 4194304 | tf_op jit(solution)/shard_map/pallas_call | solution.py:304
  5.3 1.9 %collective-permute-done = f32[1024,128]{1,0:T(8,128)S(1)} collective-permute-done((f32[1024,128]{1,0:T(8,128)S(1)}, f32[1024,128]{1,0:T(8,128)S(1)}, u32[]{:S(2)}, u32[]{:S(2)}) %collective-permute-start) | collective-permute-done | bytes 524320 | tf_op jit(solution)/shard_map/ppermute | solution.py:319
  7.3 1.6 %collective-permute-start.1 = (f32[256,128]{1,0:T(8,128)S(1)}, f32[256,128]{1,0:T(8,128)S(1)}, u32[]{:S(2)}, u32[]{:S(2)}) collective-permute-start(f32[256,128]{1,0:T(8,128)S(1)} %get-tuple-element.22), channel_id=1, source_target_pairs={{0,16},{16,32},{32,48},{48,0},{1,17},{17,33},{33,49},{49,1},{2,18}... | collective-permute-start | bytes 393224 | tf_op jit(solution)/shard_map/ppermute | solution.py:323
  8.9 1.7 %collective-permute-start.3 = (f32[256,128]{1,0:T(8,128)S(1)}, f32[256,128]{1,0:T(8,128)S(1)}, u32[]{:S(2)}, u32[]{:S(2)}) collective-permute-start(f32[256,128]{1,0:T(8,128)S(1)} %get-tuple-element.23), channel_id=1, source_target_pairs={{0,48},{16,0},{32,16},{48,32},{1,49},{17,1},{33,17},{49,33},{2,50}... | collective-permute-start | bytes 393224 | tf_op jit(solution)/shard_map/ppermute | solution.py:323
  10.6 1.8 %collective-permute-start.2 = (f32[256,128]{1,0:T(8,128)S(1)}, f32[256,128]{1,0:T(8,128)S(1)}, u32[]{:S(2)}, u32[]{:S(2)}) collective-permute-start(f32[256,128]{1,0:T(8,128)S(1)} %get-tuple-element.24), channel_id=1, source_target_pairs={{0,32},{16,48},{32,0},{48,16},{1,33},{17,49},{33,1},{49,17},{2,34}... | collective-permute-start | bytes 393224 | tf_op jit(solution)/shard_map/ppermute | solution.py:323
  12.5 1.7 %collective-permute-done.1 = f32[256,128]{1,0:T(8,128)S(1)} collective-permute-done((f32[256,128]{1,0:T(8,128)S(1)}, f32[256,128]{1,0:T(8,128)S(1)}, u32[]{:S(2)}, u32[]{:S(2)}) %collective-permute-start.1) | collective-permute-done | bytes 131104 | tf_op jit(solution)/shard_map/ppermute | solution.py:323
  14.2 2.1 %collective-permute-done.3 = f32[256,128]{1,0:T(8,128)S(1)} collective-permute-done((f32[256,128]{1,0:T(8,128)S(1)}, f32[256,128]{1,0:T(8,128)S(1)}, u32[]{:S(2)}, u32[]{:S(2)}) %collective-permute-start.3) | collective-permute-done | bytes 131104 | tf_op jit(solution)/shard_map/ppermute | solution.py:323
  16.3 1.7 %collective-permute-done.2 = f32[256,128]{1,0:T(8,128)S(1)} collective-permute-done((f32[256,128]{1,0:T(8,128)S(1)}, f32[256,128]{1,0:T(8,128)S(1)}, u32[]{:S(2)}, u32[]{:S(2)}) %collective-permute-start.2) | collective-permute-done | bytes 131104 | tf_op jit(solution)/shard_map/ppermute | solution.py:323
  18.1 11.0 %collective-permute-done.4 = f32[256,128]{1,0:T(8,128)S(1)} collective-permute-done((f32[256,128]{1,0:T(8,128)S(1)}, f32[256,128]{1,0:T(8,128)S(1)}, u32[]{:S(2)}, u32[]{:S(2)}) %collective-permute-start.4) | collective-permute-done | bytes 131104 | tf_op jit(solution)/shard_map/ppermute | solution.py:329
  29.1 1.6 %collective-permute-start.5 = (f32[256,128]{1,0:T(8,128)S(1)}, f32[256,128]{1,0:T(8,128)S(1)}, u32[]{:S(2)}, u32[]{:S(2)}) collective-permute-start(f32[256,128]{1,0:T(8,128)S(1)} %add.33), channel_id=1, source_target_pairs={{0,4},{2,6},{4,0},{6,2},{8,12},{10,14},{12,8},{14,10},{1,5},{3,7},... | collective-permute-start | bytes 393224 | tf_op jit(solution)/shard_map/ppermute | solution.py:329
  30.7 5.8 %collective-permute-done.5 = f32[256,128]{1,0:T(8,128)S(1)} collective-permute-done((f32[256,128]{1,0:T(8,128)S(1)}, f32[256,128]{1,0:T(8,128)S(1)}, u32[]{:S(2)}, u32[]{:S(2)}) %collective-permute-start.5) | collective-permute-done | bytes 131104 | tf_op jit(solution)/shard_map/ppermute | solution.py:329
  36.6 0.3 collective-permute-start.6
  36.9 4.8 %collective-permute-done.6 = f32[256,128]{1,0:T(8,128)S(1)} collective-permute-done((f32[256,128]{1,0:T(8,128)S(1)}, f32[256,128]{1,0:T(8,128)S(1)}, u32[]{:S(2)}, u32[]{:S(2)}) %collective-permute-start.6) | collective-permute-done | bytes 131104 | tf_op jit(solution)/shard_map/ppermute | solution.py:329
  41.7 1.7 %collective-permute-start.9 = (f32[256,128]{1,0:T(8,128)S(1)}, f32[256,128]{1,0:T(8,128)S(1)}, u32[]{:S(2)}, u32[]{:S(2)}) collective-permute-start(f32[256,128]{1,0:T(8,128)S(1)} %add.35.m0), channel_id=1, source_target_pairs={{0,48},{16,0},{32,16},{48,32},{1,49},{17,1},{33,17},{49,33},{2,50}... | collective-permute-start | bytes 393224 | tf_op jit(solution)/shard_map/ppermute | solution.py:323
  43.4 1.4 %collective-permute-start.8 = (f32[256,128]{1,0:T(8,128)S(1)}, f32[256,128]{1,0:T(8,128)S(1)}, u32[]{:S(2)}, u32[]{:S(2)}) collective-permute-start(f32[256,128]{1,0:T(8,128)S(1)} %add.35.m0), channel_id=1, source_target_pairs={{0,32},{16,48},{32,0},{48,16},{1,33},{17,49},{33,1},{49,17},{2,34}... | collective-permute-start | bytes 393224 | tf_op jit(solution)/shard_map/ppermute | solution.py:323
  44.8 1.9 %collective-permute-done.9.m3 = f32[256,128]{1,0:T(8,128)S(1)} collective-permute-done((f32[256,128]{1,0:T(8,128)S(1)}, f32[256,128]{1,0:T(8,128)S(1)}, u32[]{:S(2)}, u32[]{:S(2)}) %collective-permute-start.9) | collective-permute-done | bytes 131104 | tf_op jit(solution)/shard_map/ppermute | solution.py:323
  46.7 3.1 %collective-permute-done.8.m2 = f32[256,128]{1,0:T(8,128)S(1)} collective-permute-done((f32[256,128]{1,0:T(8,128)S(1)}, f32[256,128]{1,0:T(8,128)S(1)}, u32[]{:S(2)}, u32[]{:S(2)}) %collective-permute-start.8) | collective-permute-done | bytes 131104 | tf_op jit(solution)/shard_map/ppermute | solution.py:323
  49.9 1.4 %collective-permute-done.7.m1 = f32[256,128]{1,0:T(8,128)S(1)} collective-permute-done((f32[256,128]{1,0:T(8,128)S(1)}, f32[256,128]{1,0:T(8,128)S(1)}, u32[]{:S(2)}, u32[]{:S(2)}) %collective-permute-start.7) | collective-permute-done | bytes 131104 | tf_op jit(solution)/shard_map/ppermute | solution.py:323
  51.3 1.3 %collective-permute-done.11.o1 = f32[256,128]{1,0:T(8,128)S(1)} collective-permute-done((f32[256,128]{1,0:T(8,128)S(1)}, f32[256,128]{1,0:T(8,128)S(1)}, u32[]{:S(2)}, u32[]{:S(2)}) %collective-permute-start.11) | collective-permute-done | bytes 131104 | tf_op jit(solution)/shard_map/ppermute | solution.py:319
  52.6 4.7 %shard_map.85 = (bf16[2,384,384]{2,1,0:T(8,128)(2,1)S(1)}, bf16[2,2,256,256]{3,2,1,0:T(8,128)(2,1)S(1)}, f32[2,384]{1,0:T(2,128)S(1)}, f32[8,1664]{1,0:T(8,128)S(1)}) custom-call(s32[3]{0:T(128)S(1)} %pad_add_fusion.place_ref, f32[8]{0:T(128)S(1)} %copy-done.4, f32[384,1152]{1,0:T(8,128)S(1)} %copy-done, f32[384,384]{1,0:T(8,128)S(1)} %copy-done.3, ...), custom_call_target="tpu_custom_call" | custom-call | flops 2717908992 | bytes 4194304 | tf_op jit(solution)/shard_map/pallas_call | solution.py:333
  57.5 2.9 %collective-permute-start.15 = (f32[8,1664]{1,0:T(8,128)S(1)}, f32[8,1664]{1,0:T(8,128)S(1)}, u32[]{:S(2)}, u32[]{:S(2)}) collective-permute-start(f32[8,1664]{1,0:T(8,128)S(1)} %get-tuple-element.18.own_ref), channel_id=1, source_target_pairs={{0,128},{64,192},{128,0},{192,64},{1,129},{65,193},{129,1},{193,65... | collective-permute-start | bytes 159752 | tf_op jit(solution)/shard_map/ppermute | solution.py:323
  60.4 1.9 %collective-permute-start.14 = (f32[8,1664]{1,0:T(8,128)S(1)}, f32[8,1664]{1,0:T(8,128)S(1)}, u32[]{:S(2)}, u32[]{:S(2)}) collective-permute-start(f32[8,1664]{1,0:T(8,128)S(1)} %get-tuple-element.18.own_ref), channel_id=1, source_target_pairs={{0,64},{64,128},{128,192},{192,0},{1,65},{65,129},{129,193},{193,1... | collective-permute-start | bytes 159752 | tf_op jit(solution)/shard_map/ppermute | solution.py:323
  62.3 5.7 %shard_map.86 = f32[1024,384]{1,0:T(8,128)} custom-call(f32[1024,384]{1,0:T(8,128)S(1)} %bitcast.8, f32[1024,384]{1,0:T(8,128)S(1)} %bitcast.10, f32[384,1152]{1,0:T(8,128)S(1)} %copy-done, bf16[2,384,384]{2,1,0:T(8,128)(2,1)S(1)} %get-tuple-element.15.gv_ref, bf16[2,2,256,256]{3,2,1,0:T(8,128)(2,1)S(1)} %get-tuple-element.16.m_ref, ...), custom_call_target="tpu_custom_call" | custom-call | flops 4076863488 | bytes 4194304 | tf_op jit(solution)/shard_map/pallas_call | solution.py:350
  68.1 0.6 shard_map.87
  (31 shorter events, 0.7 us)
Async XLA Ops:
  5.2 2.0 %collective-permute-start = (f32[1024,128]{1,0:T(8,128)S(1)}, f32[1024,128]{1,0:T(8,128)S(1)}, u32[]{:S(2)}, u32[]{:S(2)}) collective-permute-start(f32[1024,128]{1,0:T(8,128)S(1)} %get-tuple-element.14), channel_id=1, source_target_pairs={{0,1},{1,0},{2,3},{3,2},{4,5},{5,4},{6,7},{7,6},{8,9},{9,8},{10,11... | collective-permute-start | bytes 1572872 | tf_op jit(solution)/shard_map/ppermute | solution.py:319
  7.3 45.4 %copy-start = (f32[384,1152]{1,0:T(8,128)S(1)}, f32[384,1152]{1,0:T(8,128)}, u32[]{:S(2)}) copy-start(f32[384,1152]{1,0:T(8,128)} %w_ref.3) | copy-start | bytes 5308420
  7.3 45.4 %copy-start.3 = (f32[384,384]{1,0:T(8,128)S(1)}, f32[384,384]{1,0:T(8,128)}, u32[]{:S(2)}) copy-start(f32[384,384]{1,0:T(8,128)} %f_ref.1) | copy-start | bytes 1769476
  7.3 45.3 %copy-start.4 = (f32[8]{0:T(128)S(1)}, f32[8]{0:T(128)}, u32[]{:S(2)}) copy-start(f32[8]{0:T(128)} %sharp_ref.1) | copy-start | bytes 100
  7.3 6.8 %collective-permute-start.1 = (f32[256,128]{1,0:T(8,128)S(1)}, f32[256,128]{1,0:T(8,128)S(1)}, u32[]{:S(2)}, u32[]{:S(2)}) collective-permute-start(f32[256,128]{1,0:T(8,128)S(1)} %get-tuple-element.22), channel_id=1, source_target_pairs={{0,16},{16,32},{32,48},{48,0},{1,17},{17,33},{33,49},{49,1},{2,18}... | collective-permute-start | bytes 393224 | tf_op jit(solution)/shard_map/ppermute | solution.py:323
  8.9 7.4 %collective-permute-start.3 = (f32[256,128]{1,0:T(8,128)S(1)}, f32[256,128]{1,0:T(8,128)S(1)}, u32[]{:S(2)}, u32[]{:S(2)}) collective-permute-start(f32[256,128]{1,0:T(8,128)S(1)} %get-tuple-element.23), channel_id=1, source_target_pairs={{0,48},{16,0},{32,16},{48,32},{1,49},{17,1},{33,17},{49,33},{2,50}... | collective-permute-start | bytes 393224 | tf_op jit(solution)/shard_map/ppermute | solution.py:323
  10.6 7.3 %collective-permute-start.2 = (f32[256,128]{1,0:T(8,128)S(1)}, f32[256,128]{1,0:T(8,128)S(1)}, u32[]{:S(2)}, u32[]{:S(2)}) collective-permute-start(f32[256,128]{1,0:T(8,128)S(1)} %get-tuple-element.24), channel_id=1, source_target_pairs={{0,32},{16,48},{32,0},{48,16},{1,33},{17,49},{33,1},{49,17},{2,34}... | collective-permute-start | bytes 393224 | tf_op jit(solution)/shard_map/ppermute | solution.py:323
  18.0 11.1 %collective-permute-start.4 = (f32[256,128]{1,0:T(8,128)S(1)}, f32[256,128]{1,0:T(8,128)S(1)}, u32[]{:S(2)}, u32[]{:S(2)}) collective-permute-start(f32[256,128]{1,0:T(8,128)S(1)} %fusion.1), channel_id=1, source_target_pairs={{0,8},{2,10},{4,12},{6,14},{8,0},{10,2},{12,4},{14,6},{1,9},{3,11}... | collective-permute-start | bytes 393224 | tf_op jit(solution)/shard_map/ppermute | solution.py:329
  29.1 7.5 %collective-permute-start.5 = (f32[256,128]{1,0:T(8,128)S(1)}, f32[256,128]{1,0:T(8,128)S(1)}, u32[]{:S(2)}, u32[]{:S(2)}) collective-permute-start(f32[256,128]{1,0:T(8,128)S(1)} %add.33), channel_id=1, source_target_pairs={{0,4},{2,6},{4,0},{6,2},{8,12},{10,14},{12,8},{14,10},{1,5},{3,7},... | collective-permute-start | bytes 393224 | tf_op jit(solution)/shard_map/ppermute | solution.py:329
  36.6 5.1 %collective-permute-start.6 = (f32[256,128]{1,0:T(8,128)S(1)}, f32[256,128]{1,0:T(8,128)S(1)}, u32[]{:S(2)}, u32[]{:S(2)}) collective-permute-start(f32[256,128]{1,0:T(8,128)S(1)} %add.34), channel_id=1, source_target_pairs={{0,2},{2,0},{4,6},{6,4},{8,10},{10,8},{12,14},{14,12},{1,3},{3,1},... | collective-permute-start | bytes 393224 | tf_op jit(solution)/shard_map/ppermute | solution.py:329
  41.7 20.7 %copy-start.1 = (f32[1,1024,384]{2,1,0:T(8,128)S(1)}, f32[1,1024,384]{2,1,0:T(8,128)}, u32[]{:S(2)}) copy-start(f32[1,1024,384]{2,1,0:T(8,128)} %param.5) | copy-start | bytes 4718596
  41.7 20.7 %copy-start.2 = (f32[1,1024,384]{2,1,0:T(8,128)S(1)}, f32[1,1024,384]{2,1,0:T(8,128)}, u32[]{:S(2)}) copy-start(f32[1,1024,384]{2,1,0:T(8,128)} %param.9) | copy-start | bytes 4718596
  41.7 5.0 %collective-permute-start.9 = (f32[256,128]{1,0:T(8,128)S(1)}, f32[256,128]{1,0:T(8,128)S(1)}, u32[]{:S(2)}, u32[]{:S(2)}) collective-permute-start(f32[256,128]{1,0:T(8,128)S(1)} %add.35.m0), channel_id=1, source_target_pairs={{0,48},{16,0},{32,16},{48,32},{1,49},{17,1},{33,17},{49,33},{2,50}... | collective-permute-start | bytes 393224 | tf_op jit(solution)/shard_map/ppermute | solution.py:323
  43.4 6.5 %collective-permute-start.8 = (f32[256,128]{1,0:T(8,128)S(1)}, f32[256,128]{1,0:T(8,128)S(1)}, u32[]{:S(2)}, u32[]{:S(2)}) collective-permute-start(f32[256,128]{1,0:T(8,128)S(1)} %add.35.m0), channel_id=1, source_target_pairs={{0,32},{16,48},{32,0},{48,16},{1,33},{17,49},{33,1},{49,17},{2,34}... | collective-permute-start | bytes 393224 | tf_op jit(solution)/shard_map/ppermute | solution.py:323
  44.8 6.5 %collective-permute-start.7 = (f32[256,128]{1,0:T(8,128)S(1)}, f32[256,128]{1,0:T(8,128)S(1)}, u32[]{:S(2)}, u32[]{:S(2)}) collective-permute-start(f32[256,128]{1,0:T(8,128)S(1)} %add.35.m0), channel_id=1, source_target_pairs={{0,16},{16,32},{32,48},{48,0},{1,17},{17,33},{33,49},{49,1},{2,18}... | collective-permute-start | bytes 393224 | tf_op jit(solution)/shard_map/ppermute | solution.py:323
  44.8 6.5 %collective-permute-start.10 = (f32[256,128]{1,0:T(8,128)S(1)}, f32[256,128]{1,0:T(8,128)S(1)}, u32[]{:S(2)}, u32[]{:S(2)}) collective-permute-start(f32[256,128]{1,0:T(8,128)S(1)} %add.35.m0), channel_id=1, source_target_pairs={{0,1},{1,0},{2,3},{3,2},{4,5},{5,4},{6,7},{7,6},{8,9},{9,8},{10,11... | collective-permute-start | bytes 393224 | tf_op jit(solution)/shard_map/ppermute | solution.py:319
  46.7 4.5 %collective-permute-start.13 = (f32[256,128]{1,0:T(8,128)S(1)}, f32[256,128]{1,0:T(8,128)S(1)}, u32[]{:S(2)}, u32[]{:S(2)}) collective-permute-start(f32[256,128]{1,0:T(8,128)S(1)} %collective-permute-done.9.m3), channel_id=1, source_target_pairs={{0,1},{1,0},{2,3},{3,2},{4,5},{5,4},{6,7},{7,6},{8,9},{9,8},{10,11... | collective-permute-start | bytes 393224 | tf_op jit(solution)/shard_map/ppermute | solution.py:319
  49.9 1.4 %collective-permute-start.12 = (f32[256,128]{1,0:T(8,128)S(1)}, f32[256,128]{1,0:T(8,128)S(1)}, u32[]{:S(2)}, u32[]{:S(2)}) collective-permute-start(f32[256,128]{1,0:T(8,128)S(1)} %collective-permute-done.8.m2), channel_id=1, source_target_pairs={{0,1},{1,0},{2,3},{3,2},{4,5},{5,4},{6,7},{7,6},{8,9},{9,8},{10,11... | collective-permute-start | bytes 393224 | tf_op jit(solution)/shard_map/ppermute | solution.py:319
  51.3 1.3 %collective-permute-start.11 = (f32[256,128]{1,0:T(8,128)S(1)}, f32[256,128]{1,0:T(8,128)S(1)}, u32[]{:S(2)}, u32[]{:S(2)}) collective-permute-start(f32[256,128]{1,0:T(8,128)S(1)} %collective-permute-done.7.m1), channel_id=1, source_target_pairs={{0,1},{1,0},{2,3},{3,2},{4,5},{5,4},{6,7},{7,6},{8,9},{9,8},{10,11... | collective-permute-start | bytes 393224 | tf_op jit(solution)/shard_map/ppermute | solution.py:319
  57.4 10.7 %collective-permute-start.16 = (f32[8,1664]{1,0:T(8,128)S(1)}, f32[8,1664]{1,0:T(8,128)S(1)}, u32[]{:S(2)}, u32[]{:S(2)}) collective-permute-start(f32[8,1664]{1,0:T(8,128)S(1)} %get-tuple-element.18.own_ref), channel_id=1, source_target_pairs={{0,192},{64,0},{128,64},{192,128},{1,193},{65,1},{129,65},{193,129... | collective-permute-start | bytes 159752 | tf_op jit(solution)/shard_map/ppermute | solution.py:323
  57.5 10.5 %collective-permute-start.15 = (f32[8,1664]{1,0:T(8,128)S(1)}, f32[8,1664]{1,0:T(8,128)S(1)}, u32[]{:S(2)}, u32[]{:S(2)}) collective-permute-start(f32[8,1664]{1,0:T(8,128)S(1)} %get-tuple-element.18.own_ref), channel_id=1, source_target_pairs={{0,128},{64,192},{128,0},{192,64},{1,129},{65,193},{129,1},{193,65... | collective-permute-start | bytes 159752 | tf_op jit(solution)/shard_map/ppermute | solution.py:323
  60.4 7.6 %collective-permute-start.14 = (f32[8,1664]{1,0:T(8,128)S(1)}, f32[8,1664]{1,0:T(8,128)S(1)}, u32[]{:S(2)}, u32[]{:S(2)}) collective-permute-start(f32[8,1664]{1,0:T(8,128)S(1)} %get-tuple-element.18.own_ref), channel_id=1, source_target_pairs={{0,64},{64,128},{128,192},{192,0},{1,65},{65,129},{129,193},{193,1... | collective-permute-start | bytes 159752 | tf_op jit(solution)/shard_map/ppermute | solution.py:323

commit v5 on v4

--- a/solution.py
+++ b/solution.py
@@ -18,7 +18,9 @@
 SHARES = X_CHIPS * Z_CHIPS
 ROWS = D // (SHARES * CORES)
 HALF = 8 * T
-QUARTER = HALF // X_CHIPS
+SQUARE = 4
+AWAY = (3, 2, 1)
+QUARTER = HALF // SQUARE
 PICK = 16
 BLOCKS = [("a", i, j) for i in range(3) for j in range(i, 3)]
 BLOCKS += [("b", i, j) for i in range(3) for j in range(3)]
@@ -96,8 +98,8 @@
         pay_ref[place_of(at)] = grams[name][i * T : (i + 1) * T, j * T : (j + 1) * T]
     pay_ref[place_of(15)] = jnp.zeros((T, T), f32)
     core, chip = place_ref[0], place_ref[2]
-    for k in range(X_CHIPS):
-        to = lax.rem(chip + k, X_CHIPS)
+    for k in range(SQUARE):
+        to = chip ^ k
         piece = pl.ds(k * QUARTER, QUARTER)
         keep_ref[piece] = pay_ref[core, to].reshape(QUARTER, T)
         send_ref[piece] = pay_ref[1 - core, to].reshape(QUARTER, T)
@@ -154,10 +156,9 @@
     gv_ref, m_ref, d_ref, rows_ref, block_ref, a_ref, b_ref, c_ref, t_ref, att_ref,
 ):
     core, first, chip = place_ref[0], place_ref[1], place_ref[2]
-    for k in range(X_CHIPS):
-        origin = lax.rem(chip + X_CHIPS - k, X_CHIPS)
-        block_ref[core, origin] = (m0, m1, m2, m3)[k][...].reshape(2, T, T)
-        block_ref[1 - core, origin] = (o0, o1, o2, o3)[k][...].reshape(2, T, T)
+    for k, mine_ref, other_ref in zip((0,) + AWAY, (m0, m1, m2, m3), (o0, o1, o2, o3)):
+        block_ref[core, chip ^ k] = mine_ref[...].reshape(2, T, T)
+        block_ref[1 - core, chip ^ k] = other_ref[...].reshape(2, T, T)
     for at, (name, i, j) in enumerate(BLOCKS):
         block = block_ref[place_of(at)]
         ref = a_ref if name == "a" else b_ref
@@ -258,7 +259,7 @@
         copy.wait()
 
 
-def total_kernel(own_ref, one_ref, two_ref, three_ref, mixer_ref, output_ref, sharp_ref):
+def total_kernel(own_ref, two_ref, three_ref, one_ref, mixer_ref, output_ref, sharp_ref):
     total = (own_ref[...] + two_ref[...]) + (one_ref[...] + three_ref[...])
     mixer_ref[...] = total[:ROWS, : 3 * D]
     output_ref[...] = total[:ROWS, 3 * D : 4 * D]
@@ -292,8 +293,9 @@
     x = incoming_embeddings[0]
     u = upstream_sensitivity[0]
     tokens = x.shape[0]
-    core, chip = lax.axis_index("core"), lax.axis_index("x")
-    ctx = (chip * Z_CHIPS + lax.axis_index("z")) * CORES + core
+    core, x_chip, z_chip = (lax.axis_index(axis) for axis in ("core", "x", "z"))
+    ctx = (x_chip * Z_CHIPS + z_chip) * CORES + core
+    chip = (x_chip ^ x_chip // 2) % 2 * 2 + z_chip % 2
     place = jnp.stack([core, ctx * ROWS, chip]).astype(jnp.int32)
     unit = 2 * 3 * D * D * D
 
@@ -309,7 +311,7 @@
         [
             pltpu.VMEM((tokens, D), f32),
             pltpu.VMEM((tokens, D), f32),
-            pltpu.VMEM((CORES, X_CHIPS, 2, T, T), f32),
+            pltpu.VMEM((CORES, SQUARE, 2, T, T), f32),
             pltpu.SemaphoreType.DMA((8,)),
         ],
         flops=6 * unit,
@@ -322,12 +324,23 @@
         size = lax.axis_size(axis)
         return lax.ppermute(array, axis, [(i, (i + by) % size) for i in range(size)])
 
-    part = (keep + swap(send)).reshape(X_CHIPS, QUARTER, T)
-    others = [shift(part[k], "x", k) for k in range(1, X_CHIPS)]
-    part = part[0] + others[0] + others[1] + others[2]
-    for apart in (4, 2, 1):
-        part = part + lax.ppermute(part, "z", [(i, i ^ apart) for i in range(Z_CHIPS)])
-    mine = [part] + [shift(part, "x", k) for k in range(1, X_CHIPS)]
+    def exchange(array, x_apart, z_apart):
+        pairs = [
+            (i * Z_CHIPS + j, (i ^ x_apart) * Z_CHIPS + (j ^ z_apart))
+            for i in range(X_CHIPS)
+            for j in range(Z_CHIPS)
+        ]
+        return lax.ppermute(array, ("x", "z"), pairs)
+
+    def within_square(pieces):
+        return [exchange(piece, k // 2, k % 2) for k, piece in zip(AWAY, pieces)]
+
+    part = (keep + swap(send)).reshape(SQUARE, QUARTER, T)
+    others = within_square([part[k] for k in AWAY])
+    part = (part[0] + others[0]) + (others[1] + others[2])
+    for apart in ((3, 0), (0, 6), (0, 2)):
+        part = part + exchange(part, *apart)
+    mine = [part] + within_square([part] * 3)
     other = [swap(piece) for piece in mine]
 
     gv, m, diagonal, rows = call(
@@ -336,7 +349,7 @@
         [vmem] * 4,
         [((2, D, D), bf16), ((2, 2, W, W), bf16), ((2, D), f32), ((8, 4 * D + T), f32)],
         [
-            pltpu.VMEM((CORES, X_CHIPS, 2, T, T), f32),
+            pltpu.VMEM((CORES, SQUARE, 2, T, T), f32),
             pltpu.VMEM((D, D), f32),
             pltpu.VMEM((D, D), f32),
             pltpu.VMEM((D, D), f32),
@@ -360,7 +373,7 @@
         [vmem] * 4,
         [vmem] * 3,
         [((ROWS, 3 * D), f32), ((ROWS, D), f32), ((1, VIEWS), f32)],
-    )(rows, one, two, three)
+    )(rows, two, three, one)
     return input_grad[None], mixer_grad, output_grad, sharpness_grad.reshape(VIEWS)
 
 

time: 68.8 us -> 66.6 us (0.968)
  the two profiles are of different devices: /device:TPU:136 before, /device:TPU:4 now
where the time goes in v5:
time: 66.6 us; the launch traced here: 66.5 us
  waiting for transfers between devices  28.2 us (42%)
  starting transfers between devices  21.6 us (32%)
  Pallas kernels  15.6 us (23%)
  between operations  0.81 us (1%)
    ppermute x9, waiting for transfers between devices, exchange(): return lax.ppermute(array, ('x', 'z'), pairs)  25 us
    ppermute x9, starting transfers between devices, exchange(): return lax.ppermute(array, ('x', 'z'), pairs)  16.3 us
    pallas_call x1, Pallas kernels, body(): call(output_kernel, [vmem] * 6, [hbm], [((tokens, D), f32)], [pltpu.VMEM(...  5.7 us
    ppermute x3, starting transfers between devices, shift(): lax.ppermute(array, axis, [(i, (i + by) % size) for i in range(size)])  5.24 us
    pallas_call x1, Pallas kernels, body(): call(solve_kernel, [smem, smem] + [vmem] * 10, [vmem] * 4, [((2, D, D), b...  4.75 us
    pallas_call x1, Pallas kernels, body(): call(gram_kernel, [smem, hbm, hbm], [vmem] * 2, [half] * 2, [pltpu.VMEM((...  4.48 us
    ppermute x5, waiting for transfers between devices, swap(): return lax.ppermute(array, 'core', [(0, 1), (1, 0)])  3.23 us
  transfers between devices with their start and end apart: 17, of which 10 were waited for; matrix products, arithmetic and copies ran while one was open for 0% of the time, Pallas kernels for 9%

profile of v5, /device:TPU:4, one launch (start us, length us, event | category | flops | bytes accessed | tf_op | source)
XLA Modules:
  0.0 66.5 jit_solution(1394937647145616262)
XLA Ops:
  0.7 4.5 %shard_map.84 = (f32[1024,128]{1,0:T(8,128)S(1)}, f32[1024,128]{1,0:T(8,128)S(1)}) custom-call(s32[3]{0:T(128)S(1)} %pad_add_fusion.place_ref, f32[1024,384]{1,0:T(8,128)} %bitcast.7, f32[1024,384]{1,0:T(8,128)} %bitcast.9), custom_call_target="tpu_custom_call" | custom-call | flops 2038431744 | bytes 4194304 | tf_op jit(solution)/shard_map/pallas_call | solution.py:306
  5.3 1.9 %collective-permute-done = f32[1024,128]{1,0:T(8,128)S(1)} collective-permute-done((f32[1024,128]{1,0:T(8,128)S(1)}, f32[1024,128]{1,0:T(8,128)S(1)}, u32[]{:S(2)}, u32[]{:S(2)}) %collective-permute-start) | collective-permute-done | bytes 524320 | tf_op jit(solution)/shard_map/ppermute | solution.py:321
  7.4 2.0 %collective-permute-start.3 = (f32[256,128]{1,0:T(8,128)S(1)}, f32[256,128]{1,0:T(8,128)S(1)}, u32[]{:S(2)}, u32[]{:S(2)}) collective-permute-start(f32[256,128]{1,0:T(8,128)S(1)} %get-tuple-element.22), channel_id=1, source_target_pairs={{0,2},{2,0},{4,6},{6,4},{8,10},{10,8},{12,14},{14,12},{16,18},{18,... | collective-permute-start | bytes 393224 | tf_op jit(solution)/shard_map/ppermute | solution.py:333
  9.4 1.2 %collective-permute-start.2 = (f32[256,128]{1,0:T(8,128)S(1)}, f32[256,128]{1,0:T(8,128)S(1)}, u32[]{:S(2)}, u32[]{:S(2)}) collective-permute-start(f32[256,128]{1,0:T(8,128)S(1)} %get-tuple-element.23), channel_id=1, source_target_pairs={{0,16},{2,18},{4,20},{6,22},{8,24},{10,26},{12,28},{14,30},{16,0},... | collective-permute-start | bytes 393224 | tf_op jit(solution)/shard_map/ppermute | solution.py:333
  10.9 2.3 %collective-permute-done.3 = f32[256,128]{1,0:T(8,128)S(1)} collective-permute-done((f32[256,128]{1,0:T(8,128)S(1)}, f32[256,128]{1,0:T(8,128)S(1)}, u32[]{:S(2)}, u32[]{:S(2)}) %collective-permute-start.3) | collective-permute-done | bytes 131104 | tf_op jit(solution)/shard_map/ppermute | solution.py:333
  13.3 4.2 %collective-permute-done.2 = f32[256,128]{1,0:T(8,128)S(1)} collective-permute-done((f32[256,128]{1,0:T(8,128)S(1)}, f32[256,128]{1,0:T(8,128)S(1)}, u32[]{:S(2)}, u32[]{:S(2)}) %collective-permute-start.2) | collective-permute-done | bytes 131104 | tf_op jit(solution)/shard_map/ppermute | solution.py:333
  17.5 0.7 %collective-permute-start.4 = (f32[256,128]{1,0:T(8,128)S(1)}, f32[256,128]{1,0:T(8,128)S(1)}, u32[]{:S(2)}, u32[]{:S(2)}) collective-permute-start(f32[256,128]{1,0:T(8,128)S(1)} %fusion), channel_id=1, source_target_pairs={{0,48},{2,50},{4,52},{6,54},{8,56},{10,58},{12,60},{14,62},{16,32}... | collective-permute-start | bytes 393224 | tf_op jit(solution)/shard_map/ppermute | solution.py:333
  18.2 4.4 %collective-permute-done.4 = f32[256,128]{1,0:T(8,128)S(1)} collective-permute-done((f32[256,128]{1,0:T(8,128)S(1)}, f32[256,128]{1,0:T(8,128)S(1)}, u32[]{:S(2)}, u32[]{:S(2)}) %collective-permute-start.4) | collective-permute-done | bytes 131104 | tf_op jit(solution)/shard_map/ppermute | solution.py:333
  22.5 5.5 %collective-permute-start.5 = (f32[256,128]{1,0:T(8,128)S(1)}, f32[256,128]{1,0:T(8,128)S(1)}, u32[]{:S(2)}, u32[]{:S(2)}) collective-permute-start(f32[256,128]{1,0:T(8,128)S(1)} %add.47), channel_id=1, source_target_pairs={{0,12},{2,14},{4,8},{6,10},{8,4},{10,6},{12,0},{14,2},{16,28},{18,... | collective-permute-start | bytes 393224 | tf_op jit(solution)/shard_map/ppermute | solution.py:333
  28.0 3.9 %collective-permute-done.5 = f32[256,128]{1,0:T(8,128)S(1)} collective-permute-done((f32[256,128]{1,0:T(8,128)S(1)}, f32[256,128]{1,0:T(8,128)S(1)}, u32[]{:S(2)}, u32[]{:S(2)}) %collective-permute-start.5) | collective-permute-done | bytes 131104 | tf_op jit(solution)/shard_map/ppermute | solution.py:333
  32.0 2.5 %collective-permute-start.6 = (f32[256,128]{1,0:T(8,128)S(1)}, f32[256,128]{1,0:T(8,128)S(1)}, u32[]{:S(2)}, u32[]{:S(2)}) collective-permute-start(f32[256,128]{1,0:T(8,128)S(1)} %add.48), channel_id=1, source_target_pairs={{0,4},{2,6},{4,0},{6,2},{8,12},{10,14},{12,8},{14,10},{16,20},{18,... | collective-permute-start | bytes 393224 | tf_op jit(solution)/shard_map/ppermute | solution.py:333
  34.5 4.4 %collective-permute-done.6 = f32[256,128]{1,0:T(8,128)S(1)} collective-permute-done((f32[256,128]{1,0:T(8,128)S(1)}, f32[256,128]{1,0:T(8,128)S(1)}, u32[]{:S(2)}, u32[]{:S(2)}) %collective-permute-start.6) | collective-permute-done | bytes 131104 | tf_op jit(solution)/shard_map/ppermute | solution.py:333
  38.9 1.6 %collective-permute-start.9 = (f32[256,128]{1,0:T(8,128)S(1)}, f32[256,128]{1,0:T(8,128)S(1)}, u32[]{:S(2)}, u32[]{:S(2)}) collective-permute-start(f32[256,128]{1,0:T(8,128)S(1)} %add.49.m0), channel_id=1, source_target_pairs={{0,2},{2,0},{4,6},{6,4},{8,10},{10,8},{12,14},{14,12},{16,18},{18,... | collective-permute-start | bytes 393224 | tf_op jit(solution)/shard_map/ppermute | solution.py:333
  40.5 2.4 %collective-permute-start.8 = (f32[256,128]{1,0:T(8,128)S(1)}, f32[256,128]{1,0:T(8,128)S(1)}, u32[]{:S(2)}, u32[]{:S(2)}) collective-permute-start(f32[256,128]{1,0:T(8,128)S(1)} %add.49.m0), channel_id=1, source_target_pairs={{0,16},{2,18},{4,20},{6,22},{8,24},{10,26},{12,28},{14,30},{16,0},... | collective-permute-start | bytes 393224 | tf_op jit(solution)/shard_map/ppermute | solution.py:333
  42.9 1.0 %collective-permute-done.9.m3 = f32[256,128]{1,0:T(8,128)S(1)} collective-permute-done((f32[256,128]{1,0:T(8,128)S(1)}, f32[256,128]{1,0:T(8,128)S(1)}, u32[]{:S(2)}, u32[]{:S(2)}) %collective-permute-start.9) | collective-permute-done | bytes 131104 | tf_op jit(solution)/shard_map/ppermute | solution.py:333
  44.0 2.8 %collective-permute-done.8.m2 = f32[256,128]{1,0:T(8,128)S(1)} collective-permute-done((f32[256,128]{1,0:T(8,128)S(1)}, f32[256,128]{1,0:T(8,128)S(1)}, u32[]{:S(2)}, u32[]{:S(2)}) %collective-permute-start.8) | collective-permute-done | bytes 131104 | tf_op jit(solution)/shard_map/ppermute | solution.py:333
  46.8 1.9 %collective-permute-done.7.m1 = f32[256,128]{1,0:T(8,128)S(1)} collective-permute-done((f32[256,128]{1,0:T(8,128)S(1)}, f32[256,128]{1,0:T(8,128)S(1)}, u32[]{:S(2)}, u32[]{:S(2)}) %collective-permute-start.7) | collective-permute-done | bytes 131104 | tf_op jit(solution)/shard_map/ppermute | solution.py:333
  48.7 1.3 %collective-permute-done.11.o1 = f32[256,128]{1,0:T(8,128)S(1)} collective-permute-done((f32[256,128]{1,0:T(8,128)S(1)}, f32[256,128]{1,0:T(8,128)S(1)}, u32[]{:S(2)}, u32[]{:S(2)}) %collective-permute-start.11) | collective-permute-done | bytes 131104 | tf_op jit(solution)/shard_map/ppermute | solution.py:321
  50.1 4.8 %shard_map.85 = (bf16[2,384,384]{2,1,0:T(8,128)(2,1)S(1)}, bf16[2,2,256,256]{3,2,1,0:T(8,128)(2,1)S(1)}, f32[2,384]{1,0:T(2,128)S(1)}, f32[8,1664]{1,0:T(8,128)S(1)}) custom-call(s32[3]{0:T(128)S(1)} %pad_add_fusion.place_ref, f32[8]{0:T(128)S(1)} %copy-done.4, f32[384,1152]{1,0:T(8,128)S(1)} %copy-done, f32[384,384]{1,0:T(8,128)S(1)} %copy-done.3, ...), custom_call_target="tpu_custom_call" | custom-call | flops 2717908992 | bytes 4194304 | tf_op jit(solution)/shard_map/pallas_call | solution.py:346
  54.8 1.6 %collective-permute-start.16 = (f32[8,1664]{1,0:T(8,128)S(1)}, f32[8,1664]{1,0:T(8,128)S(1)}, u32[]{:S(2)}, u32[]{:S(2)}) collective-permute-start(f32[8,1664]{1,0:T(8,128)S(1)} %get-tuple-element.18.own_ref), channel_id=1, source_target_pairs={{0,64},{64,128},{128,192},{192,0},{1,65},{65,129},{129,193},{193,1... | collective-permute-start | bytes 159752 | tf_op jit(solution)/shard_map/ppermute | solution.py:325
  56.4 1.7 %collective-permute-start.15 = (f32[8,1664]{1,0:T(8,128)S(1)}, f32[8,1664]{1,0:T(8,128)S(1)}, u32[]{:S(2)}, u32[]{:S(2)}) collective-permute-start(f32[8,1664]{1,0:T(8,128)S(1)} %get-tuple-element.18.own_ref), channel_id=1, source_target_pairs={{0,192},{64,0},{128,64},{192,128},{1,193},{65,1},{129,65},{193,129... | collective-permute-start | bytes 159752 | tf_op jit(solution)/shard_map/ppermute | solution.py:325
  58.1 2.0 %collective-permute-start.14 = (f32[8,1664]{1,0:T(8,128)S(1)}, f32[8,1664]{1,0:T(8,128)S(1)}, u32[]{:S(2)}, u32[]{:S(2)}) collective-permute-start(f32[8,1664]{1,0:T(8,128)S(1)} %get-tuple-element.18.own_ref), channel_id=1, source_target_pairs={{0,128},{64,192},{128,0},{192,64},{1,129},{65,193},{129,1},{193,65... | collective-permute-start | bytes 159752 | tf_op jit(solution)/shard_map/ppermute | solution.py:325
  60.1 5.7 %shard_map.86 = f32[1024,384]{1,0:T(8,128)} custom-call(f32[1024,384]{1,0:T(8,128)S(1)} %bitcast.8, f32[1024,384]{1,0:T(8,128)S(1)} %bitcast.10, f32[384,1152]{1,0:T(8,128)S(1)} %copy-done, bf16[2,384,384]{2,1,0:T(8,128)(2,1)S(1)} %get-tuple-element.15.gv_ref, bf16[2,2,256,256]{3,2,1,0:T(8,128)(2,1)S(1)} %get-tuple-element.16.m_ref, ...), custom_call_target="tpu_custom_call" | custom-call | flops 4076863488 | bytes 4194304 | tf_op jit(solution)/shard_map/pallas_call | solution.py:363
  65.8 0.6 shard_map.87
  (31 shorter events, 0.8 us)
Async XLA Ops:
  5.2 2.0 %collective-permute-start = (f32[1024,128]{1,0:T(8,128)S(1)}, f32[1024,128]{1,0:T(8,128)S(1)}, u32[]{:S(2)}, u32[]{:S(2)}) collective-permute-start(f32[1024,128]{1,0:T(8,128)S(1)} %get-tuple-element.14), channel_id=1, source_target_pairs={{0,1},{1,0},{2,3},{3,2},{4,5},{5,4},{6,7},{7,6},{8,9},{9,8},{10,11... | collective-permute-start | bytes 1572872 | tf_op jit(solution)/shard_map/ppermute | solution.py:321
  7.3 42.8 %copy-start = (f32[384,1152]{1,0:T(8,128)S(1)}, f32[384,1152]{1,0:T(8,128)}, u32[]{:S(2)}) copy-start(f32[384,1152]{1,0:T(8,128)} %w_ref.3) | copy-start | bytes 5308420
  7.3 42.8 %copy-start.3 = (f32[384,384]{1,0:T(8,128)S(1)}, f32[384,384]{1,0:T(8,128)}, u32[]{:S(2)}) copy-start(f32[384,384]{1,0:T(8,128)} %f_ref.1) | copy-start | bytes 1769476
  7.3 42.8 %copy-start.4 = (f32[8]{0:T(128)S(1)}, f32[8]{0:T(128)}, u32[]{:S(2)}) copy-start(f32[8]{0:T(128)} %sharp_ref.1) | copy-start | bytes 100
  7.4 5.9 %collective-permute-start.3 = (f32[256,128]{1,0:T(8,128)S(1)}, f32[256,128]{1,0:T(8,128)S(1)}, u32[]{:S(2)}, u32[]{:S(2)}) collective-permute-start(f32[256,128]{1,0:T(8,128)S(1)} %get-tuple-element.22), channel_id=1, source_target_pairs={{0,2},{2,0},{4,6},{6,4},{8,10},{10,8},{12,14},{14,12},{16,18},{18,... | collective-permute-start | bytes 393224 | tf_op jit(solution)/shard_map/ppermute | solution.py:333
  9.4 8.1 %collective-permute-start.2 = (f32[256,128]{1,0:T(8,128)S(1)}, f32[256,128]{1,0:T(8,128)S(1)}, u32[]{:S(2)}, u32[]{:S(2)}) collective-permute-start(f32[256,128]{1,0:T(8,128)S(1)} %get-tuple-element.23), channel_id=1, source_target_pairs={{0,16},{2,18},{4,20},{6,22},{8,24},{10,26},{12,28},{14,30},{16,0},... | collective-permute-start | bytes 393224 | tf_op jit(solution)/shard_map/ppermute | solution.py:333
  10.6 6.9 %collective-permute-start.1 = (f32[256,128]{1,0:T(8,128)S(1)}, f32[256,128]{1,0:T(8,128)S(1)}, u32[]{:S(2)}, u32[]{:S(2)}) collective-permute-start(f32[256,128]{1,0:T(8,128)S(1)} %get-tuple-element.24), channel_id=1, source_target_pairs={{0,18},{2,16},{4,22},{6,20},{8,26},{10,24},{12,30},{14,28},{16,2},... | collective-permute-start | bytes 393224 | tf_op jit(solution)/shard_map/ppermute | solution.py:333
  17.5 5.1 %collective-permute-start.4 = (f32[256,128]{1,0:T(8,128)S(1)}, f32[256,128]{1,0:T(8,128)S(1)}, u32[]{:S(2)}, u32[]{:S(2)}) collective-permute-start(f32[256,128]{1,0:T(8,128)S(1)} %fusion), channel_id=1, source_target_pairs={{0,48},{2,50},{4,52},{6,54},{8,56},{10,58},{12,60},{14,62},{16,32}... | collective-permute-start | bytes 393224 | tf_op jit(solution)/shard_map/ppermute | solution.py:333
  22.5 9.4 %collective-permute-start.5 = (f32[256,128]{1,0:T(8,128)S(1)}, f32[256,128]{1,0:T(8,128)S(1)}, u32[]{:S(2)}, u32[]{:S(2)}) collective-permute-start(f32[256,128]{1,0:T(8,128)S(1)} %add.47), channel_id=1, source_target_pairs={{0,12},{2,14},{4,8},{6,10},{8,4},{10,6},{12,0},{14,2},{16,28},{18,... | collective-permute-start | bytes 393224 | tf_op jit(solution)/shard_map/ppermute | solution.py:333
  32.0 6.9 %collective-permute-start.6 = (f32[256,128]{1,0:T(8,128)S(1)}, f32[256,128]{1,0:T(8,128)S(1)}, u32[]{:S(2)}, u32[]{:S(2)}) collective-permute-start(f32[256,128]{1,0:T(8,128)S(1)} %add.48), channel_id=1, source_target_pairs={{0,4},{2,6},{4,0},{6,2},{8,12},{10,14},{12,8},{14,10},{16,20},{18,... | collective-permute-start | bytes 393224 | tf_op jit(solution)/shard_map/ppermute | solution.py:333
  38.9 21.2 %copy-start.1 = (f32[1,1024,384]{2,1,0:T(8,128)S(1)}, f32[1,1024,384]{2,1,0:T(8,128)}, u32[]{:S(2)}) copy-start(f32[1,1024,384]{2,1,0:T(8,128)} %param.5) | copy-start | bytes 4718596
  38.9 21.2 %copy-start.2 = (f32[1,1024,384]{2,1,0:T(8,128)S(1)}, f32[1,1024,384]{2,1,0:T(8,128)}, u32[]{:S(2)}) copy-start(f32[1,1024,384]{2,1,0:T(8,128)} %param.9) | copy-start | bytes 4718596
  38.9 5.1 %collective-permute-start.9 = (f32[256,128]{1,0:T(8,128)S(1)}, f32[256,128]{1,0:T(8,128)S(1)}, u32[]{:S(2)}, u32[]{:S(2)}) collective-permute-start(f32[256,128]{1,0:T(8,128)S(1)} %add.49.m0), channel_id=1, source_target_pairs={{0,2},{2,0},{4,6},{6,4},{8,10},{10,8},{12,14},{14,12},{16,18},{18,... | collective-permute-start | bytes 393224 | tf_op jit(solution)/shard_map/ppermute | solution.py:333
  40.5 6.3 %collective-permute-start.8 = (f32[256,128]{1,0:T(8,128)S(1)}, f32[256,128]{1,0:T(8,128)S(1)}, u32[]{:S(2)}, u32[]{:S(2)}) collective-permute-start(f32[256,128]{1,0:T(8,128)S(1)} %add.49.m0), channel_id=1, source_target_pairs={{0,16},{2,18},{4,20},{6,22},{8,24},{10,26},{12,28},{14,30},{16,0},... | collective-permute-start | bytes 393224 | tf_op jit(solution)/shard_map/ppermute | solution.py:333
  42.9 5.9 %collective-permute-start.7 = (f32[256,128]{1,0:T(8,128)S(1)}, f32[256,128]{1,0:T(8,128)S(1)}, u32[]{:S(2)}, u32[]{:S(2)}) collective-permute-start(f32[256,128]{1,0:T(8,128)S(1)} %add.49.m0), channel_id=1, source_target_pairs={{0,18},{2,16},{4,22},{6,20},{8,26},{10,24},{12,30},{14,28},{16,2},... | collective-permute-start | bytes 393224 | tf_op jit(solution)/shard_map/ppermute | solution.py:333
  42.9 5.8 %collective-permute-start.10 = (f32[256,128]{1,0:T(8,128)S(1)}, f32[256,128]{1,0:T(8,128)S(1)}, u32[]{:S(2)}, u32[]{:S(2)}) collective-permute-start(f32[256,128]{1,0:T(8,128)S(1)} %add.49.m0), channel_id=1, source_target_pairs={{0,1},{1,0},{2,3},{3,2},{4,5},{5,4},{6,7},{7,6},{8,9},{9,8},{10,11... | collective-permute-start | bytes 393224 | tf_op jit(solution)/shard_map/ppermute | solution.py:321
  44.0 4.8 %collective-permute-start.13 = (f32[256,128]{1,0:T(8,128)S(1)}, f32[256,128]{1,0:T(8,128)S(1)}, u32[]{:S(2)}, u32[]{:S(2)}) collective-permute-start(f32[256,128]{1,0:T(8,128)S(1)} %collective-permute-done.9.m3), channel_id=1, source_target_pairs={{0,1},{1,0},{2,3},{3,2},{4,5},{5,4},{6,7},{7,6},{8,9},{9,8},{10,11... | collective-permute-start | bytes 393224 | tf_op jit(solution)/shard_map/ppermute | solution.py:321
  46.8 2.0 %collective-permute-start.12 = (f32[256,128]{1,0:T(8,128)S(1)}, f32[256,128]{1,0:T(8,128)S(1)}, u32[]{:S(2)}, u32[]{:S(2)}) collective-permute-start(f32[256,128]{1,0:T(8,128)S(1)} %collective-permute-done.8.m2), channel_id=1, source_target_pairs={{0,1},{1,0},{2,3},{3,2},{4,5},{5,4},{6,7},{7,6},{8,9},{9,8},{10,11... | collective-permute-start | bytes 393224 | tf_op jit(solution)/shard_map/ppermute | solution.py:321
  48.7 1.3 %collective-permute-start.11 = (f32[256,128]{1,0:T(8,128)S(1)}, f32[256,128]{1,0:T(8,128)S(1)}, u32[]{:S(2)}, u32[]{:S(2)}) collective-permute-start(f32[256,128]{1,0:T(8,128)S(1)} %collective-permute-done.7.m1), channel_id=1, source_target_pairs={{0,1},{1,0},{2,3},{3,2},{4,5},{5,4},{6,7},{7,6},{8,9},{9,8},{10,11... | collective-permute-start | bytes 393224 | tf_op jit(solution)/shard_map/ppermute | solution.py:321
  54.8 11.0 %collective-permute-start.16 = (f32[8,1664]{1,0:T(8,128)S(1)}, f32[8,1664]{1,0:T(8,128)S(1)}, u32[]{:S(2)}, u32[]{:S(2)}) collective-permute-start(f32[8,1664]{1,0:T(8,128)S(1)} %get-tuple-element.18.own_ref), channel_id=1, source_target_pairs={{0,64},{64,128},{128,192},{192,0},{1,65},{65,129},{129,193},{193,1... | collective-permute-start | bytes 159752 | tf_op jit(solution)/shard_map/ppermute | solution.py:325
  56.4 9.4 %collective-permute-start.15 = (f32[8,1664]{1,0:T(8,128)S(1)}, f32[8,1664]{1,0:T(8,128)S(1)}, u32[]{:S(2)}, u32[]{:S(2)}) collective-permute-start(f32[8,1664]{1,0:T(8,128)S(1)} %get-tuple-element.18.own_ref), channel_id=1, source_target_pairs={{0,192},{64,0},{128,64},{192,128},{1,193},{65,1},{129,65},{193,129... | collective-permute-start | bytes 159752 | tf_op jit(solution)/shard_map/ppermute | solution.py:325
  58.1 7.7 %collective-permute-start.14 = (f32[8,1664]{1,0:T(8,128)S(1)}, f32[8,1664]{1,0:T(8,128)S(1)}, u32[]{:S(2)}, u32[]{:S(2)}) collective-permute-start(f32[8,1664]{1,0:T(8,128)S(1)} %get-tuple-element.18.own_ref), channel_id=1, source_target_pairs={{0,128},{64,192},{128,0},{192,64},{1,129},{65,193},{129,1},{193,65... | collective-permute-start | bytes 159752 | tf_op jit(solution)/shard_map/ppermute | solution.py:325

commit v6 on v5

--- a/solution.py
+++ b/solution.py
@@ -73,27 +73,31 @@
 
 
 def gram_kernel(place_ref, x_hbm, u_hbm, keep_ref, send_ref, x_ref, u_ref, pay_ref, sems):
-    tokens = x_ref.shape[0]
-    step = tokens // 4
+    step = x_ref.shape[0] // 2
     copies = []
-    for at, (source, target) in enumerate(((x_hbm, x_ref), (u_hbm, u_ref))):
-        for k in range(4):
-            piece = pl.ds(k * step, step)
-            copy = pltpu.make_async_copy(source.at[piece], target.at[piece], sems.at[at * 4 + k])
+    for part in range(2):
+        piece = pl.ds(part * step, step)
+        for at, (source, target) in enumerate(((x_hbm, x_ref), (u_hbm, u_ref))):
+            copy = pltpu.make_async_copy(
+                source.at[piece], target.at[piece], sems.at[part * 2 + at]
+            )
             copy.start()
             copies.append(copy)
-    for copy in copies[:4]:
-        copy.wait()
     d = functools.partial(
         lax.dot_general, dimension_numbers=(TN, ((), ())), preferred_element_type=f32
     )
-    xh, xl = split(x_ref[...])
-    cross = d(xh, xl)
-    grams = {"a": d(xh, xh) + cross + cross.T}
-    for copy in copies[4:]:
-        copy.wait()
-    uh, ul = split(u_ref[...])
-    grams["b"] = d(xh, uh) + (d(xh, ul) + d(xl, uh))
+    sums = []
+    for part in range(2):
+        piece = pl.ds(part * step, step)
+        copies[2 * part].wait()
+        copies[2 * part + 1].wait()
+        xh, xl = split(x_ref[piece])
+        uh, ul = split(u_ref[piece])
+        wide = d(xh, jnp.concatenate([xh, xl, uh, ul], axis=1))
+        mixed = wide[:, 2 * D : 3 * D] + wide[:, 3 * D :] + d(xl, uh)
+        sums.append((wide[:, :D], wide[:, D : 2 * D], mixed))
+    whole, cross, mixed = (one + two for one, two in zip(*sums))
+    grams = {"a": whole + cross + cross.T, "b": mixed}
     for at, (name, i, j) in enumerate(BLOCKS):
         pay_ref[place_of(at)] = grams[name][i * T : (i + 1) * T, j * T : (j + 1) * T]
     pay_ref[place_of(15)] = jnp.zeros((T, T), f32)
@@ -167,15 +171,20 @@
             ref[j * T : (j + 1) * T, i * T : (i + 1) * T] = block.T
     a_s, b_s = split(a_ref[...]), split(b_ref[...])
     ws, fs = split(w_ref[...]), split(f_ref[...])
-    t = dot3(a_s, cut(ws, ALL, slice(0, 2 * D)), NN)
-    t_ref[...] = t
+    tk = dot3(a_s, cut(ws, ALL, slice(D, 2 * D)), NN)
     c = dot3(cut(ws, ALL, slice(2 * D, 3 * D)), b_s, TN)
+    tks, c_s = split(tk), split(c)
+    raw = [dot3(cut(ws, ALL, span), cut(tks, ALL, span), TN) for span in WINDOWS]
+    tq = dot3(a_s, cut(ws, ALL, slice(0, D)), NN)
+    t_ref[:, :D], t_ref[:, D:] = tq, tk
     c_ref[...] = c
-    c_s = split(c)
-    square = jnp.sum(w_ref[:, : 2 * D] * t, axis=0, keepdims=True)
-    inverse = lax.rsqrt(jnp.maximum(square, 0.0) + epsilon)
-    q_inv, k_inv = inverse[:, :D], inverse[:, D:]
-    tks = split(t[:, D:])
+    attention_grads = [
+        dot3(cut(fs, span, ALL), cut(c_s, span, ALL), NT) for span in WINDOWS
+    ]
+    q_square = jnp.sum(w_ref[:, :D] * tq, axis=0, keepdims=True)
+    k_square = jnp.sum(w_ref[:, D : 2 * D] * tk, axis=0, keepdims=True)
+    q_inv = lax.rsqrt(jnp.maximum(q_square, 0.0) + epsilon)
+    k_inv = lax.rsqrt(jnp.maximum(k_square, 0.0) + epsilon)
     t_rows = rows_of(first, lambda rows: t_ref[rows], D)
     b_rows = rows_of(first, lambda rows: b_ref[rows], D)
     tq_rows, tk_rows = split(t_rows[:, :D]), split(t_rows[:, D:])
@@ -183,8 +192,7 @@
     attentions, covs, mixers = [], [], []
     for window, span in enumerate(WINDOWS):
         same = masks(window)
-        cov = dot3(cut(ws, ALL, span), cut(tks, ALL, span), TN)
-        cov = jnp.where(same, cov * to_col(eye, q_inv[:, span]) * k_inv[:, span], 0.0)
+        cov = jnp.where(same, raw[window] * to_col(eye, q_inv[:, span]) * k_inv[:, span], 0.0)
         table = jnp.where(same, jnp.exp(sharp_col(sharp_ref, window) * cov), 0.0)
         total = jnp.sum(table, axis=1, keepdims=True)
         attention = table / jnp.where(total > 0.0, total, 1.0)
@@ -205,7 +213,7 @@
     for window, span in enumerate(WINDOWS):
         attention, cov = attentions[window], covs[window]
         sharp = sharp_col(sharp_ref, window)
-        attention_grad = dot3(cut(fs, span, ALL), cut(c_s, span, ALL), NT)
+        attention_grad = attention_grads[window]
         inner = jnp.sum(attention * attention_grad, axis=1, keepdims=True)
         score_grad = attention * (attention_grad - inner)
         weighed = score_grad * cov
@@ -241,7 +249,11 @@
     gk = split(join(k_parts) - w_ref[:, D : 2 * D] * d_ref[1:2])
     g = tuple(jnp.concatenate([one, two], axis=1) for one, two in zip(gq, gk))
     gv = (gv_ref[0], gv_ref[1])
-    p = split(dot3(g, cut(ws, ALL, slice(0, 2 * D)), NT))
+    wqk = cut(ws, ALL, slice(0, 2 * D))
+    corner = dot3(cut(g, slice(0, T), ALL), cut(wqk, slice(0, T), ALL), NT)
+    others = dot3(g, cut(wqk, slice(T, D), ALL), NT)
+    corner = jnp.concatenate([corner, others[:T, :T].T, others[:T, T:].T], axis=0)
+    p = split(jnp.concatenate([corner, others], axis=1))
     r = split(dot3(gv, cut(ws, ALL, slice(2 * D, 3 * D)), NT))
     factors = tuple(jnp.concatenate([one, two], axis=0) for one, two in zip(p, r))
     tokens = x_ref.shape[0]
@@ -312,7 +324,7 @@
             pltpu.VMEM((tokens, D), f32),
             pltpu.VMEM((tokens, D), f32),
             pltpu.VMEM((CORES, SQUARE, 2, T, T), f32),
-            pltpu.SemaphoreType.DMA((8,)),
+            pltpu.SemaphoreType.DMA((4,)),
         ],
         flops=6 * unit,
     )(place, in_hbm(x), in_hbm(u))

time: 66.6 us -> 65.2 us (0.979)
  Pallas kernels: 15.6 us -> 14.1 us
    pallas_call x1, Pallas kernels: 4.75 us -> 4.07 us  [body(): call(solve_kernel, [smem, smem] + [vmem] * 10, [vmem] * 4, [((2, D, D), b...]
  transfers between devices with their start and end apart: 17 -> 17, of which waited for: 10 -> 10; matrix products, arithmetic and copies ran while one was open for 0% -> 0% of each run, Pallas kernels for 9% -> 8%
where the time goes in v6:
time: 65.2 us; the launch traced here: 65.1 us
  waiting for transfers between devices  28.2 us (43%)
  starting transfers between devices  21.7 us (33%)
  Pallas kernels  14.1 us (22%)
  between operations  0.81 us (1%)
    ppermute x9, waiting for transfers between devices, exchange(): return lax.ppermute(array, ('x', 'z'), pairs)  25 us
    ppermute x9, starting transfers between devices, exchange(): return lax.ppermute(array, ('x', 'z'), pairs)  16.3 us
    pallas_call x1, Pallas kernels, body(): call(output_kernel, [vmem] * 6, [hbm], [((tokens, D), f32)], [pltpu.VMEM(...  5.37 us
    ppermute x3, starting transfers between devices, shift(): lax.ppermute(array, axis, [(i, (i + by) % size) for i in range(size)])  5.29 us
    pallas_call x1, Pallas kernels, body(): call(solve_kernel, [smem, smem] + [vmem] * 10, [vmem] * 4, [((2, D, D), b...  4.07 us
    pallas_call x1, Pallas kernels, body(): call(gram_kernel, [smem, hbm, hbm], [vmem] * 2, [half] * 2, [pltpu.VMEM((...  4.05 us
    ppermute x5, waiting for transfers between devices, swap(): return lax.ppermute(array, 'core', [(0, 1), (1, 0)])  3.23 us
  transfers between devices with their start and end apart: 17, of which 10 were waited for; matrix products, arithmetic and copies ran while one was open for 0% of the time, Pallas kernels for 8%

profile of v6, /device:TPU:4, one launch (start us, length us, event | category | flops | bytes accessed | tf_op | source)
XLA Modules:
  0.0 65.1 jit_solution(13920120720812226062)
XLA Ops:
  0.7 4.1 %shard_map.84 = (f32[1024,128]{1,0:T(8,128)S(1)}, f32[1024,128]{1,0:T(8,128)S(1)}) custom-call(s32[3]{0:T(128)S(1)} %pad_add_fusion.place_ref, f32[1024,384]{1,0:T(8,128)} %bitcast.7, f32[1024,384]{1,0:T(8,128)} %bitcast.9), custom_call_target="tpu_custom_call" | custom-call | flops 2038431744 | bytes 4194304 | tf_op jit(solution)/shard_map/pallas_call | solution.py:318
  4.9 1.9 %collective-permute-done = f32[1024,128]{1,0:T(8,128)S(1)} collective-permute-done((f32[1024,128]{1,0:T(8,128)S(1)}, f32[1024,128]{1,0:T(8,128)S(1)}, u32[]{:S(2)}, u32[]{:S(2)}) %collective-permute-start) | collective-permute-done | bytes 524320 | tf_op jit(solution)/shard_map/ppermute | solution.py:333
  6.9 2.0 %collective-permute-start.3 = (f32[256,128]{1,0:T(8,128)S(1)}, f32[256,128]{1,0:T(8,128)S(1)}, u32[]{:S(2)}, u32[]{:S(2)}) collective-permute-start(f32[256,128]{1,0:T(8,128)S(1)} %get-tuple-element.22), channel_id=1, source_target_pairs={{0,2},{2,0},{4,6},{6,4},{8,10},{10,8},{12,14},{14,12},{16,18},{18,... | collective-permute-start | bytes 393224 | tf_op jit(solution)/shard_map/ppermute | solution.py:345
  8.9 1.2 %collective-permute-start.2 = (f32[256,128]{1,0:T(8,128)S(1)}, f32[256,128]{1,0:T(8,128)S(1)}, u32[]{:S(2)}, u32[]{:S(2)}) collective-permute-start(f32[256,128]{1,0:T(8,128)S(1)} %get-tuple-element.23), channel_id=1, source_target_pairs={{0,16},{2,18},{4,20},{6,22},{8,24},{10,26},{12,28},{14,30},{16,0},... | collective-permute-start | bytes 393224 | tf_op jit(solution)/shard_map/ppermute | solution.py:345
  10.5 2.3 %collective-permute-done.3 = f32[256,128]{1,0:T(8,128)S(1)} collective-permute-done((f32[256,128]{1,0:T(8,128)S(1)}, f32[256,128]{1,0:T(8,128)S(1)}, u32[]{:S(2)}, u32[]{:S(2)}) %collective-permute-start.3) | collective-permute-done | bytes 131104 | tf_op jit(solution)/shard_map/ppermute | solution.py:345
  12.8 4.2 %collective-permute-done.2 = f32[256,128]{1,0:T(8,128)S(1)} collective-permute-done((f32[256,128]{1,0:T(8,128)S(1)}, f32[256,128]{1,0:T(8,128)S(1)}, u32[]{:S(2)}, u32[]{:S(2)}) %collective-permute-start.2) | collective-permute-done | bytes 131104 | tf_op jit(solution)/shard_map/ppermute | solution.py:345
  17.1 0.7 %collective-permute-start.4 = (f32[256,128]{1,0:T(8,128)S(1)}, f32[256,128]{1,0:T(8,128)S(1)}, u32[]{:S(2)}, u32[]{:S(2)}) collective-permute-start(f32[256,128]{1,0:T(8,128)S(1)} %fusion), channel_id=1, source_target_pairs={{0,48},{2,50},{4,52},{6,54},{8,56},{10,58},{12,60},{14,62},{16,32}... | collective-permute-start | bytes 393224 | tf_op jit(solution)/shard_map/ppermute | solution.py:345
  17.7 4.4 %collective-permute-done.4 = f32[256,128]{1,0:T(8,128)S(1)} collective-permute-done((f32[256,128]{1,0:T(8,128)S(1)}, f32[256,128]{1,0:T(8,128)S(1)}, u32[]{:S(2)}, u32[]{:S(2)}) %collective-permute-start.4) | collective-permute-done | bytes 131104 | tf_op jit(solution)/shard_map/ppermute | solution.py:345
  22.1 5.5 %collective-permute-start.5 = (f32[256,128]{1,0:T(8,128)S(1)}, f32[256,128]{1,0:T(8,128)S(1)}, u32[]{:S(2)}, u32[]{:S(2)}) collective-permute-start(f32[256,128]{1,0:T(8,128)S(1)} %add.47), channel_id=1, source_target_pairs={{0,12},{2,14},{4,8},{6,10},{8,4},{10,6},{12,0},{14,2},{16,28},{18,... | collective-permute-start | bytes 393224 | tf_op jit(solution)/shard_map/ppermute | solution.py:345
  27.6 3.9 %collective-permute-done.5 = f32[256,128]{1,0:T(8,128)S(1)} collective-permute-done((f32[256,128]{1,0:T(8,128)S(1)}, f32[256,128]{1,0:T(8,128)S(1)}, u32[]{:S(2)}, u32[]{:S(2)}) %collective-permute-start.5) | collective-permute-done | bytes 131104 | tf_op jit(solution)/shard_map/ppermute | solution.py:345
  31.6 2.5 %collective-permute-start.6 = (f32[256,128]{1,0:T(8,128)S(1)}, f32[256,128]{1,0:T(8,128)S(1)}, u32[]{:S(2)}, u32[]{:S(2)}) collective-permute-start(f32[256,128]{1,0:T(8,128)S(1)} %add.48), channel_id=1, source_target_pairs={{0,4},{2,6},{4,0},{6,2},{8,12},{10,14},{12,8},{14,10},{16,20},{18,... | collective-permute-start | bytes 393224 | tf_op jit(solution)/shard_map/ppermute | solution.py:345
  34.1 4.4 %collective-permute-done.6 = f32[256,128]{1,0:T(8,128)S(1)} collective-permute-done((f32[256,128]{1,0:T(8,128)S(1)}, f32[256,128]{1,0:T(8,128)S(1)}, u32[]{:S(2)}, u32[]{:S(2)}) %collective-permute-start.6) | collective-permute-done | bytes 131104 | tf_op jit(solution)/shard_map/ppermute | solution.py:345
  38.5 1.6 %collective-permute-start.9 = (f32[256,128]{1,0:T(8,128)S(1)}, f32[256,128]{1,0:T(8,128)S(1)}, u32[]{:S(2)}, u32[]{:S(2)}) collective-permute-start(f32[256,128]{1,0:T(8,128)S(1)} %add.49.m0), channel_id=1, source_target_pairs={{0,2},{2,0},{4,6},{6,4},{8,10},{10,8},{12,14},{14,12},{16,18},{18,... | collective-permute-start | bytes 393224 | tf_op jit(solution)/shard_map/ppermute | solution.py:345
  40.1 2.3 %collective-permute-start.8 = (f32[256,128]{1,0:T(8,128)S(1)}, f32[256,128]{1,0:T(8,128)S(1)}, u32[]{:S(2)}, u32[]{:S(2)}) collective-permute-start(f32[256,128]{1,0:T(8,128)S(1)} %add.49.m0), channel_id=1, source_target_pairs={{0,16},{2,18},{4,20},{6,22},{8,24},{10,26},{12,28},{14,30},{16,0},... | collective-permute-start | bytes 393224 | tf_op jit(solution)/shard_map/ppermute | solution.py:345
  42.5 1.0 %collective-permute-done.9.m3 = f32[256,128]{1,0:T(8,128)S(1)} collective-permute-done((f32[256,128]{1,0:T(8,128)S(1)}, f32[256,128]{1,0:T(8,128)S(1)}, u32[]{:S(2)}, u32[]{:S(2)}) %collective-permute-start.9) | collective-permute-done | bytes 131104 | tf_op jit(solution)/shard_map/ppermute | solution.py:345
  43.5 2.8 %collective-permute-done.8.m2 = f32[256,128]{1,0:T(8,128)S(1)} collective-permute-done((f32[256,128]{1,0:T(8,128)S(1)}, f32[256,128]{1,0:T(8,128)S(1)}, u32[]{:S(2)}, u32[]{:S(2)}) %collective-permute-start.8) | collective-permute-done | bytes 131104 | tf_op jit(solution)/shard_map/ppermute | solution.py:345
  46.4 1.9 %collective-permute-done.7.m1 = f32[256,128]{1,0:T(8,128)S(1)} collective-permute-done((f32[256,128]{1,0:T(8,128)S(1)}, f32[256,128]{1,0:T(8,128)S(1)}, u32[]{:S(2)}, u32[]{:S(2)}) %collective-permute-start.7) | collective-permute-done | bytes 131104 | tf_op jit(solution)/shard_map/ppermute | solution.py:345
  48.3 1.3 %collective-permute-done.11.o1 = f32[256,128]{1,0:T(8,128)S(1)} collective-permute-done((f32[256,128]{1,0:T(8,128)S(1)}, f32[256,128]{1,0:T(8,128)S(1)}, u32[]{:S(2)}, u32[]{:S(2)}) %collective-permute-start.11) | collective-permute-done | bytes 131104 | tf_op jit(solution)/shard_map/ppermute | solution.py:333
  49.7 4.1 %shard_map.85 = (bf16[2,384,384]{2,1,0:T(8,128)(2,1)S(1)}, bf16[2,2,256,256]{3,2,1,0:T(8,128)(2,1)S(1)}, f32[2,384]{1,0:T(2,128)S(1)}, f32[8,1664]{1,0:T(8,128)S(1)}) custom-call(s32[3]{0:T(128)S(1)} %pad_add_fusion.place_ref, f32[8]{0:T(128)S(1)} %copy-done.4, f32[384,1152]{1,0:T(8,128)S(1)} %copy-done, f32[384,384]{1,0:T(8,128)S(1)} %copy-done.3, ...), custom_call_target="tpu_custom_call" | custom-call | flops 2717908992 | bytes 4194304 | tf_op jit(solution)/shard_map/pallas_call | solution.py:358
  53.7 1.6 %collective-permute-start.16 = (f32[8,1664]{1,0:T(8,128)S(1)}, f32[8,1664]{1,0:T(8,128)S(1)}, u32[]{:S(2)}, u32[]{:S(2)}) collective-permute-start(f32[8,1664]{1,0:T(8,128)S(1)} %get-tuple-element.18.own_ref), channel_id=1, source_target_pairs={{0,64},{64,128},{128,192},{192,0},{1,65},{65,129},{129,193},{193,1... | collective-permute-start | bytes 159752 | tf_op jit(solution)/shard_map/ppermute | solution.py:337
  55.4 1.7 %collective-permute-start.15 = (f32[8,1664]{1,0:T(8,128)S(1)}, f32[8,1664]{1,0:T(8,128)S(1)}, u32[]{:S(2)}, u32[]{:S(2)}) collective-permute-start(f32[8,1664]{1,0:T(8,128)S(1)} %get-tuple-element.18.own_ref), channel_id=1, source_target_pairs={{0,192},{64,0},{128,64},{192,128},{1,193},{65,1},{129,65},{193,129... | collective-permute-start | bytes 159752 | tf_op jit(solution)/shard_map/ppermute | solution.py:337
  57.0 2.0 %collective-permute-start.14 = (f32[8,1664]{1,0:T(8,128)S(1)}, f32[8,1664]{1,0:T(8,128)S(1)}, u32[]{:S(2)}, u32[]{:S(2)}) collective-permute-start(f32[8,1664]{1,0:T(8,128)S(1)} %get-tuple-element.18.own_ref), channel_id=1, source_target_pairs={{0,128},{64,192},{128,0},{192,64},{1,129},{65,193},{129,1},{193,65... | collective-permute-start | bytes 159752 | tf_op jit(solution)/shard_map/ppermute | solution.py:337
  59.0 5.4 %shard_map.86 = f32[1024,384]{1,0:T(8,128)} custom-call(f32[1024,384]{1,0:T(8,128)S(1)} %bitcast.8, f32[1024,384]{1,0:T(8,128)S(1)} %bitcast.10, f32[384,1152]{1,0:T(8,128)S(1)} %copy-done, bf16[2,384,384]{2,1,0:T(8,128)(2,1)S(1)} %get-tuple-element.15.gv_ref, bf16[2,2,256,256]{3,2,1,0:T(8,128)(2,1)S(1)} %get-tuple-element.16.m_ref, ...), custom_call_target="tpu_custom_call" | custom-call | flops 4076863488 | bytes 4194304 | tf_op jit(solution)/shard_map/pallas_call | solution.py:375
  64.4 0.6 shard_map.87
  (31 shorter events, 0.8 us)
Async XLA Ops:
  4.8 2.0 %collective-permute-start = (f32[1024,128]{1,0:T(8,128)S(1)}, f32[1024,128]{1,0:T(8,128)S(1)}, u32[]{:S(2)}, u32[]{:S(2)}) collective-permute-start(f32[1024,128]{1,0:T(8,128)S(1)} %get-tuple-element.14), channel_id=1, source_target_pairs={{0,1},{1,0},{2,3},{3,2},{4,5},{5,4},{6,7},{7,6},{8,9},{9,8},{10,11... | collective-permute-start | bytes 1572872 | tf_op jit(solution)/shard_map/ppermute | solution.py:333
  6.9 42.8 %copy-start = (f32[384,1152]{1,0:T(8,128)S(1)}, f32[384,1152]{1,0:T(8,128)}, u32[]{:S(2)}) copy-start(f32[384,1152]{1,0:T(8,128)} %w_ref.3) | copy-start | bytes 5308420
  6.9 42.8 %copy-start.3 = (f32[384,384]{1,0:T(8,128)S(1)}, f32[384,384]{1,0:T(8,128)}, u32[]{:S(2)}) copy-start(f32[384,384]{1,0:T(8,128)} %f_ref.1) | copy-start | bytes 1769476
  6.9 42.8 %copy-start.4 = (f32[8]{0:T(128)S(1)}, f32[8]{0:T(128)}, u32[]{:S(2)}) copy-start(f32[8]{0:T(128)} %sharp_ref.1) | copy-start | bytes 100
  6.9 5.9 %collective-permute-start.3 = (f32[256,128]{1,0:T(8,128)S(1)}, f32[256,128]{1,0:T(8,128)S(1)}, u32[]{:S(2)}, u32[]{:S(2)}) collective-permute-start(f32[256,128]{1,0:T(8,128)S(1)} %get-tuple-element.22), channel_id=1, source_target_pairs={{0,2},{2,0},{4,6},{6,4},{8,10},{10,8},{12,14},{14,12},{16,18},{18,... | collective-permute-start | bytes 393224 | tf_op jit(solution)/shard_map/ppermute | solution.py:345
  8.9 8.1 %collective-permute-start.2 = (f32[256,128]{1,0:T(8,128)S(1)}, f32[256,128]{1,0:T(8,128)S(1)}, u32[]{:S(2)}, u32[]{:S(2)}) collective-permute-start(f32[256,128]{1,0:T(8,128)S(1)} %get-tuple-element.23), channel_id=1, source_target_pairs={{0,16},{2,18},{4,20},{6,22},{8,24},{10,26},{12,28},{14,30},{16,0},... | collective-permute-start | bytes 393224 | tf_op jit(solution)/shard_map/ppermute | solution.py:345
  10.1 6.9 %collective-permute-start.1 = (f32[256,128]{1,0:T(8,128)S(1)}, f32[256,128]{1,0:T(8,128)S(1)}, u32[]{:S(2)}, u32[]{:S(2)}) collective-permute-start(f32[256,128]{1,0:T(8,128)S(1)} %get-tuple-element.24), channel_id=1, source_target_pairs={{0,18},{2,16},{4,22},{6,20},{8,26},{10,24},{12,30},{14,28},{16,2},... | collective-permute-start | bytes 393224 | tf_op jit(solution)/shard_map/ppermute | solution.py:345
  17.1 5.1 %collective-permute-start.4 = (f32[256,128]{1,0:T(8,128)S(1)}, f32[256,128]{1,0:T(8,128)S(1)}, u32[]{:S(2)}, u32[]{:S(2)}) collective-permute-start(f32[256,128]{1,0:T(8,128)S(1)} %fusion), channel_id=1, source_target_pairs={{0,48},{2,50},{4,52},{6,54},{8,56},{10,58},{12,60},{14,62},{16,32}... | collective-permute-start | bytes 393224 | tf_op jit(solution)/shard_map/ppermute | solution.py:345
  22.1 9.4 %collective-permute-start.5 = (f32[256,128]{1,0:T(8,128)S(1)}, f32[256,128]{1,0:T(8,128)S(1)}, u32[]{:S(2)}, u32[]{:S(2)}) collective-permute-start(f32[256,128]{1,0:T(8,128)S(1)} %add.47), channel_id=1, source_target_pairs={{0,12},{2,14},{4,8},{6,10},{8,4},{10,6},{12,0},{14,2},{16,28},{18,... | collective-permute-start | bytes 393224 | tf_op jit(solution)/shard_map/ppermute | solution.py:345
  31.6 6.9 %collective-permute-start.6 = (f32[256,128]{1,0:T(8,128)S(1)}, f32[256,128]{1,0:T(8,128)S(1)}, u32[]{:S(2)}, u32[]{:S(2)}) collective-permute-start(f32[256,128]{1,0:T(8,128)S(1)} %add.48), channel_id=1, source_target_pairs={{0,4},{2,6},{4,0},{6,2},{8,12},{10,14},{12,8},{14,10},{16,20},{18,... | collective-permute-start | bytes 393224 | tf_op jit(solution)/shard_map/ppermute | solution.py:345
  38.4 20.6 %copy-start.1 = (f32[1,1024,384]{2,1,0:T(8,128)S(1)}, f32[1,1024,384]{2,1,0:T(8,128)}, u32[]{:S(2)}) copy-start(f32[1,1024,384]{2,1,0:T(8,128)} %param.5) | copy-start | bytes 4718596
  38.5 20.6 %copy-start.2 = (f32[1,1024,384]{2,1,0:T(8,128)S(1)}, f32[1,1024,384]{2,1,0:T(8,128)}, u32[]{:S(2)}) copy-start(f32[1,1024,384]{2,1,0:T(8,128)} %param.9) | copy-start | bytes 4718596
  38.5 5.1 %collective-permute-start.9 = (f32[256,128]{1,0:T(8,128)S(1)}, f32[256,128]{1,0:T(8,128)S(1)}, u32[]{:S(2)}, u32[]{:S(2)}) collective-permute-start(f32[256,128]{1,0:T(8,128)S(1)} %add.49.m0), channel_id=1, source_target_pairs={{0,2},{2,0},{4,6},{6,4},{8,10},{10,8},{12,14},{14,12},{16,18},{18,... | collective-permute-start | bytes 393224 | tf_op jit(solution)/shard_map/ppermute | solution.py:345
  40.1 6.3 %collective-permute-start.8 = (f32[256,128]{1,0:T(8,128)S(1)}, f32[256,128]{1,0:T(8,128)S(1)}, u32[]{:S(2)}, u32[]{:S(2)}) collective-permute-start(f32[256,128]{1,0:T(8,128)S(1)} %add.49.m0), channel_id=1, source_target_pairs={{0,16},{2,18},{4,20},{6,22},{8,24},{10,26},{12,28},{14,30},{16,0},... | collective-permute-start | bytes 393224 | tf_op jit(solution)/shard_map/ppermute | solution.py:345
  42.4 5.9 %collective-permute-start.7 = (f32[256,128]{1,0:T(8,128)S(1)}, f32[256,128]{1,0:T(8,128)S(1)}, u32[]{:S(2)}, u32[]{:S(2)}) collective-permute-start(f32[256,128]{1,0:T(8,128)S(1)} %add.49.m0), channel_id=1, source_target_pairs={{0,18},{2,16},{4,22},{6,20},{8,26},{10,24},{12,30},{14,28},{16,2},... | collective-permute-start | bytes 393224 | tf_op jit(solution)/shard_map/ppermute | solution.py:345
  42.5 5.8 %collective-permute-start.10 = (f32[256,128]{1,0:T(8,128)S(1)}, f32[256,128]{1,0:T(8,128)S(1)}, u32[]{:S(2)}, u32[]{:S(2)}) collective-permute-start(f32[256,128]{1,0:T(8,128)S(1)} %add.49.m0), channel_id=1, source_target_pairs={{0,1},{1,0},{2,3},{3,2},{4,5},{5,4},{6,7},{7,6},{8,9},{9,8},{10,11... | collective-permute-start | bytes 393224 | tf_op jit(solution)/shard_map/ppermute | solution.py:333
  43.5 4.8 %collective-permute-start.13 = (f32[256,128]{1,0:T(8,128)S(1)}, f32[256,128]{1,0:T(8,128)S(1)}, u32[]{:S(2)}, u32[]{:S(2)}) collective-permute-start(f32[256,128]{1,0:T(8,128)S(1)} %collective-permute-done.9.m3), channel_id=1, source_target_pairs={{0,1},{1,0},{2,3},{3,2},{4,5},{5,4},{6,7},{7,6},{8,9},{9,8},{10,11... | collective-permute-start | bytes 393224 | tf_op jit(solution)/shard_map/ppermute | solution.py:333
  46.4 2.0 %collective-permute-start.12 = (f32[256,128]{1,0:T(8,128)S(1)}, f32[256,128]{1,0:T(8,128)S(1)}, u32[]{:S(2)}, u32[]{:S(2)}) collective-permute-start(f32[256,128]{1,0:T(8,128)S(1)} %collective-permute-done.8.m2), channel_id=1, source_target_pairs={{0,1},{1,0},{2,3},{3,2},{4,5},{5,4},{6,7},{7,6},{8,9},{9,8},{10,11... | collective-permute-start | bytes 393224 | tf_op jit(solution)/shard_map/ppermute | solution.py:333
  48.3 1.3 %collective-permute-start.11 = (f32[256,128]{1,0:T(8,128)S(1)}, f32[256,128]{1,0:T(8,128)S(1)}, u32[]{:S(2)}, u32[]{:S(2)}) collective-permute-start(f32[256,128]{1,0:T(8,128)S(1)} %collective-permute-done.7.m1), channel_id=1, source_target_pairs={{0,1},{1,0},{2,3},{3,2},{4,5},{5,4},{6,7},{7,6},{8,9},{9,8},{10,11... | collective-permute-start | bytes 393224 | tf_op jit(solution)/shard_map/ppermute | solution.py:333
  53.7 10.7 %collective-permute-start.16 = (f32[8,1664]{1,0:T(8,128)S(1)}, f32[8,1664]{1,0:T(8,128)S(1)}, u32[]{:S(2)}, u32[]{:S(2)}) collective-permute-start(f32[8,1664]{1,0:T(8,128)S(1)} %get-tuple-element.18.own_ref), channel_id=1, source_target_pairs={{0,64},{64,128},{128,192},{192,0},{1,65},{65,129},{129,193},{193,1... | collective-permute-start | bytes 159752 | tf_op jit(solution)/shard_map/ppermute | solution.py:337
  55.4 9.1 %collective-permute-start.15 = (f32[8,1664]{1,0:T(8,128)S(1)}, f32[8,1664]{1,0:T(8,128)S(1)}, u32[]{:S(2)}, u32[]{:S(2)}) collective-permute-start(f32[8,1664]{1,0:T(8,128)S(1)} %get-tuple-element.18.own_ref), channel_id=1, source_target_pairs={{0,192},{64,0},{128,64},{192,128},{1,193},{65,1},{129,65},{193,129... | collective-permute-start | bytes 159752 | tf_op jit(solution)/shard_map/ppermute | solution.py:337
  57.0 7.4 %collective-permute-start.14 = (f32[8,1664]{1,0:T(8,128)S(1)}, f32[8,1664]{1,0:T(8,128)S(1)}, u32[]{:S(2)}, u32[]{:S(2)}) collective-permute-start(f32[8,1664]{1,0:T(8,128)S(1)} %get-tuple-element.18.own_ref), channel_id=1, source_target_pairs={{0,128},{64,192},{128,0},{192,64},{1,129},{65,193},{129,1},{193,65... | collective-permute-start | bytes 159752 | tf_op jit(solution)/shard_map/ppermute | solution.py:337

commit v7 on v6

--- a/solution.py
+++ b/solution.py
@@ -17,17 +17,21 @@
 X_CHIPS, Z_CHIPS, CORES = 4, 8, 2
 SHARES = X_CHIPS * Z_CHIPS
 ROWS = D // (SHARES * CORES)
-HALF = 8 * T
+HALF = 7 * T
 SQUARE = 4
 AWAY = (3, 2, 1)
 QUARTER = HALF // SQUARE
 PICK = 16
-BLOCKS = [("a", i, j) for i in range(3) for j in range(i, 3)]
+BLOCKS = [("a", 0, 1), ("a", 0, 2), ("a", 1, 2), ("pair", 0, 0), ("last", 0, 0)]
 BLOCKS += [("b", i, j) for i in range(3) for j in range(3)]
 
 
 def place_of(at):
-    return at // 8, at % 8 // 2, at % 2
+    return at // 7, slice(at % 7 * T, (at % 7 + 1) * T)
+
+
+def quarter_of(place):
+    return pl.ds(pl.multiple_of(place * QUARTER, 8), QUARTER)
 
 
 f32, bf16 = jnp.float32, jnp.bfloat16
@@ -70,6 +74,10 @@
 def join(parts):
     one, two = parts
     return jnp.concatenate([one[:, :T], one[:, T:] + two[:, :T], two[:, T:]], axis=1)
+
+
+def iotas():
+    return (lax.broadcasted_iota(jnp.int32, (T, T), axis) for axis in range(2))
 
 
 def gram_kernel(place_ref, x_hbm, u_hbm, keep_ref, send_ref, x_ref, u_ref, pay_ref, sems):
@@ -97,16 +105,23 @@
         mixed = wide[:, 2 * D : 3 * D] + wide[:, 3 * D :] + d(xl, uh)
         sums.append((wide[:, :D], wide[:, D : 2 * D], mixed))
     whole, cross, mixed = (one + two for one, two in zip(*sums))
-    grams = {"a": whole + cross + cross.T, "b": mixed}
+    a = whole + cross + cross.T
     for at, (name, i, j) in enumerate(BLOCKS):
-        pay_ref[place_of(at)] = grams[name][i * T : (i + 1) * T, j * T : (j + 1) * T]
-    pay_ref[place_of(15)] = jnp.zeros((T, T), f32)
+        if name in ("a", "b"):
+            source = a if name == "a" else mixed
+            pay_ref[place_of(at)] = source[i * T : (i + 1) * T, j * T : (j + 1) * T]
+    row, col = iotas()
+    first, second, third = (a[i * T : (i + 1) * T, i * T : (i + 1) * T] for i in range(3))
+    diagonal = jnp.sum(jnp.where(row == col, second, 0.0), axis=0, keepdims=True)
+    hidden = jnp.where(row == T - 1, diagonal, diagonal[:, T - 1 :])
+    pay_ref[place_of(3)] = jnp.where(row <= col, first, second)
+    pay_ref[place_of(4)] = jnp.where(row <= col, third, hidden)
     core, chip = place_ref[0], place_ref[2]
     for k in range(SQUARE):
         to = chip ^ k
         piece = pl.ds(k * QUARTER, QUARTER)
-        keep_ref[piece] = pay_ref[core, to].reshape(QUARTER, T)
-        send_ref[piece] = pay_ref[1 - core, to].reshape(QUARTER, T)
+        keep_ref[piece] = pay_ref[core, quarter_of(to)]
+        send_ref[piece] = pay_ref[1 - core, quarter_of(to)]
 
 
 def heads_of(shape, axis, window):
@@ -161,14 +176,23 @@
 ):
     core, first, chip = place_ref[0], place_ref[1], place_ref[2]
     for k, mine_ref, other_ref in zip((0,) + AWAY, (m0, m1, m2, m3), (o0, o1, o2, o3)):
-        block_ref[core, chip ^ k] = mine_ref[...].reshape(2, T, T)
-        block_ref[1 - core, chip ^ k] = other_ref[...].reshape(2, T, T)
+        block_ref[core, quarter_of(chip ^ k)] = mine_ref[...]
+        block_ref[1 - core, quarter_of(chip ^ k)] = other_ref[...]
     for at, (name, i, j) in enumerate(BLOCKS):
-        block = block_ref[place_of(at)]
-        ref = a_ref if name == "a" else b_ref
-        ref[i * T : (i + 1) * T, j * T : (j + 1) * T] = block
-        if name == "a" and i != j:
-            ref[j * T : (j + 1) * T, i * T : (i + 1) * T] = block.T
+        if name in ("a", "b"):
+            block = block_ref[place_of(at)]
+            ref = a_ref if name == "a" else b_ref
+            ref[i * T : (i + 1) * T, j * T : (j + 1) * T] = block
+            if name == "a":
+                ref[j * T : (j + 1) * T, i * T : (i + 1) * T] = block.T
+    row, col = iotas()
+    pair, last = block_ref[place_of(3)], block_ref[place_of(4)]
+    pair_t = pair.T
+    diagonal = jnp.where(col[:1] == T - 1, last[T // 2 : T // 2 + 1, :1], last[T - 1 :])
+    a_ref[:T, :T] = jnp.where(row <= col, pair, pair_t)
+    second = jnp.where(row > col, pair, pair_t)
+    a_ref[T : 2 * T, T : 2 * T] = jnp.where(row == col, diagonal, second)
+    a_ref[2 * T :, 2 * T :] = jnp.where(row <= col, last, last.T)
     a_s, b_s = split(a_ref[...]), split(b_ref[...])
     ws, fs = split(w_ref[...]), split(f_ref[...])
     tk = dot3(a_s, cut(ws, ALL, slice(D, 2 * D)), NN)
@@ -323,7 +347,7 @@
         [
             pltpu.VMEM((tokens, D), f32),
             pltpu.VMEM((tokens, D), f32),
-            pltpu.VMEM((CORES, SQUARE, 2, T, T), f32),
+            pltpu.VMEM((CORES, HALF, T), f32),
             pltpu.SemaphoreType.DMA((4,)),
         ],
         flops=6 * unit,
@@ -361,7 +385,7 @@
         [vmem] * 4,
         [((2, D, D), bf16), ((2, 2, W, W), bf16), ((2, D), f32), ((8, 4 * D + T), f32)],
         [
-            pltpu.VMEM((CORES, SQUARE, 2, T, T), f32),
+            pltpu.VMEM((CORES, HALF, T), f32),
             pltpu.VMEM((D, D), f32),
             pltpu.VMEM((D, D), f32),
             pltpu.VMEM((D, D), f32),

time: 65.2 us -> 63.5 us (0.974)
  waiting for transfers between devices: 28.2 us -> 26.4 us
    ppermute x9, waiting for transfers between devices: 25 us -> 23.3 us  [exchange(): return lax.ppermute(array, ('x', 'z'), pairs)]
where the time goes in v7:
time: 63.5 us; the launch traced here: 63.4 us
  waiting for transfers between devices  26.4 us (42%)
  starting transfers between devices  21.9 us (34%)
  Pallas kernels  14.2 us (22%)
  between operations  0.79 us (1%)
    ppermute x9, waiting for transfers between devices, exchange(): return lax.ppermute(array, ('x', 'z'), pairs)  23.3 us
    ppermute x9, starting transfers between devices, exchange(): return lax.ppermute(array, ('x', 'z'), pairs)  16.5 us
    pallas_call x1, Pallas kernels, body(): call(output_kernel, [vmem] * 6, [hbm], [((tokens, D), f32)], [pltpu.VMEM(...  5.38 us
    ppermute x3, starting transfers between devices, shift(): lax.ppermute(array, axis, [(i, (i + by) % size) for i in range(size)])  5.29 us
    pallas_call x1, Pallas kernels, body(): call(solve_kernel, [smem, smem] + [vmem] * 10, [vmem] * 4, [((2, D, D), b...  4.11 us
    pallas_call x1, Pallas kernels, body(): call(gram_kernel, [smem, hbm, hbm], [vmem] * 2, [half] * 2, [pltpu.VMEM((...  4.04 us
    ppermute x5, waiting for transfers between devices, swap(): return lax.ppermute(array, 'core', [(0, 1), (1, 0)])  3.11 us
  transfers between devices with their start and end apart: 17, of which 10 were waited for; matrix products, arithmetic and copies ran while one was open for 0% of the time, Pallas kernels for 8%

profile of v7, /device:TPU:4, one launch (start us, length us, event | category | flops | bytes accessed | tf_op | source)
XLA Modules:
  0.0 63.4 jit_solution(17858437305902648681)
XLA Ops:
  0.7 4.0 %shard_map.84 = (f32[896,128]{1,0:T(8,128)S(1)}, f32[896,128]{1,0:T(8,128)S(1)}) custom-call(s32[3]{0:T(128)S(1)} %pad_add_fusion.place_ref, f32[1024,384]{1,0:T(8,128)} %bitcast.7, f32[1024,384]{1,0:T(8,128)} %bitcast.9), custom_call_target="tpu_custom_call" | custom-call | flops 2038431744 | bytes 4194304 | tf_op jit(solution)/shard_map/pallas_call | solution.py:342
  4.9 1.8 %collective-permute-done = f32[896,128]{1,0:T(8,128)S(1)} collective-permute-done((f32[896,128]{1,0:T(8,128)S(1)}, f32[896,128]{1,0:T(8,128)S(1)}, u32[]{:S(2)}, u32[]{:S(2)}) %collective-permute-start) | collective-permute-done | bytes 458784 | tf_op jit(solution)/shard_map/ppermute | solution.py:357
  6.8 2.0 %collective-permute-start.3 = (f32[224,128]{1,0:T(8,128)S(1)}, f32[224,128]{1,0:T(8,128)S(1)}, u32[]{:S(2)}, u32[]{:S(2)}) collective-permute-start(f32[224,128]{1,0:T(8,128)S(1)} %get-tuple-element.22), channel_id=1, source_target_pairs={{0,2},{2,0},{4,6},{6,4},{8,10},{10,8},{12,14},{14,12},{16,18},{18,... | collective-permute-start | bytes 344072 | tf_op jit(solution)/shard_map/ppermute | solution.py:369
  8.8 1.2 %collective-permute-start.2 = (f32[224,128]{1,0:T(8,128)S(1)}, f32[224,128]{1,0:T(8,128)S(1)}, u32[]{:S(2)}, u32[]{:S(2)}) collective-permute-start(f32[224,128]{1,0:T(8,128)S(1)} %get-tuple-element.23), channel_id=1, source_target_pairs={{0,16},{2,18},{4,20},{6,22},{8,24},{10,26},{12,28},{14,30},{16,0},... | collective-permute-start | bytes 344072 | tf_op jit(solution)/shard_map/ppermute | solution.py:369
  10.4 1.9 %collective-permute-done.3 = f32[224,128]{1,0:T(8,128)S(1)} collective-permute-done((f32[224,128]{1,0:T(8,128)S(1)}, f32[224,128]{1,0:T(8,128)S(1)}, u32[]{:S(2)}, u32[]{:S(2)}) %collective-permute-start.3) | collective-permute-done | bytes 114720 | tf_op jit(solution)/shard_map/ppermute | solution.py:369
  12.3 3.9 %collective-permute-done.2 = f32[224,128]{1,0:T(8,128)S(1)} collective-permute-done((f32[224,128]{1,0:T(8,128)S(1)}, f32[224,128]{1,0:T(8,128)S(1)}, u32[]{:S(2)}, u32[]{:S(2)}) %collective-permute-start.2) | collective-permute-done | bytes 114720 | tf_op jit(solution)/shard_map/ppermute | solution.py:369
  16.2 0.7 %collective-permute-start.4 = (f32[224,128]{1,0:T(8,128)S(1)}, f32[224,128]{1,0:T(8,128)S(1)}, u32[]{:S(2)}, u32[]{:S(2)}) collective-permute-start(f32[224,128]{1,0:T(8,128)S(1)} %fusion), channel_id=1, source_target_pairs={{0,48},{2,50},{4,52},{6,54},{8,56},{10,58},{12,60},{14,62},{16,32}... | collective-permute-start | bytes 344072 | tf_op jit(solution)/shard_map/ppermute | solution.py:369
  16.9 4.2 %collective-permute-done.4 = f32[224,128]{1,0:T(8,128)S(1)} collective-permute-done((f32[224,128]{1,0:T(8,128)S(1)}, f32[224,128]{1,0:T(8,128)S(1)}, u32[]{:S(2)}, u32[]{:S(2)}) %collective-permute-start.4) | collective-permute-done | bytes 114720 | tf_op jit(solution)/shard_map/ppermute | solution.py:369
  21.1 5.5 %collective-permute-start.5 = (f32[224,128]{1,0:T(8,128)S(1)}, f32[224,128]{1,0:T(8,128)S(1)}, u32[]{:S(2)}, u32[]{:S(2)}) collective-permute-start(f32[224,128]{1,0:T(8,128)S(1)} %add.47), channel_id=1, source_target_pairs={{0,12},{2,14},{4,8},{6,10},{8,4},{10,6},{12,0},{14,2},{16,28},{18,... | collective-permute-start | bytes 344072 | tf_op jit(solution)/shard_map/ppermute | solution.py:369
  26.6 3.6 %collective-permute-done.5 = f32[224,128]{1,0:T(8,128)S(1)} collective-permute-done((f32[224,128]{1,0:T(8,128)S(1)}, f32[224,128]{1,0:T(8,128)S(1)}, u32[]{:S(2)}, u32[]{:S(2)}) %collective-permute-start.5) | collective-permute-done | bytes 114720 | tf_op jit(solution)/shard_map/ppermute | solution.py:369
  30.2 2.5 %collective-permute-start.6 = (f32[224,128]{1,0:T(8,128)S(1)}, f32[224,128]{1,0:T(8,128)S(1)}, u32[]{:S(2)}, u32[]{:S(2)}) collective-permute-start(f32[224,128]{1,0:T(8,128)S(1)} %add.48), channel_id=1, source_target_pairs={{0,4},{2,6},{4,0},{6,2},{8,12},{10,14},{12,8},{14,10},{16,20},{18,... | collective-permute-start | bytes 344072 | tf_op jit(solution)/shard_map/ppermute | solution.py:369
  32.7 4.0 %collective-permute-done.6 = f32[224,128]{1,0:T(8,128)S(1)} collective-permute-done((f32[224,128]{1,0:T(8,128)S(1)}, f32[224,128]{1,0:T(8,128)S(1)}, u32[]{:S(2)}, u32[]{:S(2)}) %collective-permute-start.6) | collective-permute-done | bytes 114720 | tf_op jit(solution)/shard_map/ppermute | solution.py:369
  36.8 1.5 %collective-permute-start.9 = (f32[224,128]{1,0:T(8,128)S(1)}, f32[224,128]{1,0:T(8,128)S(1)}, u32[]{:S(2)}, u32[]{:S(2)}) collective-permute-start(f32[224,128]{1,0:T(8,128)S(1)} %add.49.m0), channel_id=1, source_target_pairs={{0,2},{2,0},{4,6},{6,4},{8,10},{10,8},{12,14},{14,12},{16,18},{18,... | collective-permute-start | bytes 344072 | tf_op jit(solution)/shard_map/ppermute | solution.py:369
  38.3 2.6 %collective-permute-start.8 = (f32[224,128]{1,0:T(8,128)S(1)}, f32[224,128]{1,0:T(8,128)S(1)}, u32[]{:S(2)}, u32[]{:S(2)}) collective-permute-start(f32[224,128]{1,0:T(8,128)S(1)} %add.49.m0), channel_id=1, source_target_pairs={{0,16},{2,18},{4,20},{6,22},{8,24},{10,26},{12,28},{14,30},{16,0},... | collective-permute-start | bytes 344072 | tf_op jit(solution)/shard_map/ppermute | solution.py:369
  41.0 0.7 %collective-permute-done.9.m3 = f32[224,128]{1,0:T(8,128)S(1)} collective-permute-done((f32[224,128]{1,0:T(8,128)S(1)}, f32[224,128]{1,0:T(8,128)S(1)}, u32[]{:S(2)}, u32[]{:S(2)}) %collective-permute-start.9) | collective-permute-done | bytes 114720 | tf_op jit(solution)/shard_map/ppermute | solution.py:369
  41.7 2.9 %collective-permute-done.8.m2 = f32[224,128]{1,0:T(8,128)S(1)} collective-permute-done((f32[224,128]{1,0:T(8,128)S(1)}, f32[224,128]{1,0:T(8,128)S(1)}, u32[]{:S(2)}, u32[]{:S(2)}) %collective-permute-start.8) | collective-permute-done | bytes 114720 | tf_op jit(solution)/shard_map/ppermute | solution.py:369
  44.5 2.1 %collective-permute-done.7.m1 = f32[224,128]{1,0:T(8,128)S(1)} collective-permute-done((f32[224,128]{1,0:T(8,128)S(1)}, f32[224,128]{1,0:T(8,128)S(1)}, u32[]{:S(2)}, u32[]{:S(2)}) %collective-permute-start.7) | collective-permute-done | bytes 114720 | tf_op jit(solution)/shard_map/ppermute | solution.py:369
  46.7 1.3 %collective-permute-done.11.o1 = f32[224,128]{1,0:T(8,128)S(1)} collective-permute-done((f32[224,128]{1,0:T(8,128)S(1)}, f32[224,128]{1,0:T(8,128)S(1)}, u32[]{:S(2)}, u32[]{:S(2)}) %collective-permute-start.11) | collective-permute-done | bytes 114720 | tf_op jit(solution)/shard_map/ppermute | solution.py:357
  48.0 4.1 %shard_map.85 = (bf16[2,384,384]{2,1,0:T(8,128)(2,1)S(1)}, bf16[2,2,256,256]{3,2,1,0:T(8,128)(2,1)S(1)}, f32[2,384]{1,0:T(2,128)S(1)}, f32[8,1664]{1,0:T(8,128)S(1)}) custom-call(s32[3]{0:T(128)S(1)} %pad_add_fusion.place_ref, f32[8]{0:T(128)S(1)} %copy-done.4, f32[384,1152]{1,0:T(8,128)S(1)} %copy-done, f32[384,384]{1,0:T(8,128)S(1)} %copy-done.3, ...), custom_call_target="tpu_custom_call" | custom-call | flops 2717908992 | bytes 4194304 | tf_op jit(solution)/shard_map/pallas_call | solution.py:382
  52.1 1.7 %collective-permute-start.16 = (f32[8,1664]{1,0:T(8,128)S(1)}, f32[8,1664]{1,0:T(8,128)S(1)}, u32[]{:S(2)}, u32[]{:S(2)}) collective-permute-start(f32[8,1664]{1,0:T(8,128)S(1)} %get-tuple-element.18.own_ref), channel_id=1, source_target_pairs={{0,64},{64,128},{128,192},{192,0},{1,65},{65,129},{129,193},{193,1... | collective-permute-start | bytes 159752 | tf_op jit(solution)/shard_map/ppermute | solution.py:361
  53.7 1.6 %collective-permute-start.15 = (f32[8,1664]{1,0:T(8,128)S(1)}, f32[8,1664]{1,0:T(8,128)S(1)}, u32[]{:S(2)}, u32[]{:S(2)}) collective-permute-start(f32[8,1664]{1,0:T(8,128)S(1)} %get-tuple-element.18.own_ref), channel_id=1, source_target_pairs={{0,192},{64,0},{128,64},{192,128},{1,193},{65,1},{129,65},{193,129... | collective-permute-start | bytes 159752 | tf_op jit(solution)/shard_map/ppermute | solution.py:361
  55.4 2.0 %collective-permute-start.14 = (f32[8,1664]{1,0:T(8,128)S(1)}, f32[8,1664]{1,0:T(8,128)S(1)}, u32[]{:S(2)}, u32[]{:S(2)}) collective-permute-start(f32[8,1664]{1,0:T(8,128)S(1)} %get-tuple-element.18.own_ref), channel_id=1, source_target_pairs={{0,128},{64,192},{128,0},{192,64},{1,129},{65,193},{129,1},{193,65... | collective-permute-start | bytes 159752 | tf_op jit(solution)/shard_map/ppermute | solution.py:361
  57.4 5.4 %shard_map.86 = f32[1024,384]{1,0:T(8,128)} custom-call(f32[1024,384]{1,0:T(8,128)S(1)} %bitcast.8, f32[1024,384]{1,0:T(8,128)S(1)} %bitcast.10, f32[384,1152]{1,0:T(8,128)S(1)} %copy-done, bf16[2,384,384]{2,1,0:T(8,128)(2,1)S(1)} %get-tuple-element.15.gv_ref, bf16[2,2,256,256]{3,2,1,0:T(8,128)(2,1)S(1)} %get-tuple-element.16.m_ref, ...), custom_call_target="tpu_custom_call" | custom-call | flops 4076863488 | bytes 4194304 | tf_op jit(solution)/shard_map/pallas_call | solution.py:399
  62.8 0.6 %shard_map.87 = (f32[6,1152]{1,0:T(8,128)}, f32[6,384]{1,0:T(8,128)}, f32[1,8]{1,0:T(1,128)}) custom-call(f32[8,1664]{1,0:T(8,128)S(1)} %get-tuple-element.18.own_ref, f32[8,1664]{1,0:T(8,128)S(1)} %collective-permute-done.14.two_ref, f32[8,1664]{1,0:T(8,128)S(1)} %collective-permute-done.15.three_ref, f32[8,1664]{1,0:T(8,128)S(1)} %collective-permute-done.16.one_ref), custom_call_target="tpu_custom_call" | custom-call | bytes 4194304 | tf_op jit(solution)/shard_map/pallas_call | solution.py:407
  (31 shorter events, 0.7 us)
Async XLA Ops:
  4.8 1.9 %collective-permute-start = (f32[896,128]{1,0:T(8,128)S(1)}, f32[896,128]{1,0:T(8,128)S(1)}, u32[]{:S(2)}, u32[]{:S(2)}) collective-permute-start(f32[896,128]{1,0:T(8,128)S(1)} %get-tuple-element.14), channel_id=1, source_target_pairs={{0,1},{1,0},{2,3},{3,2},{4,5},{5,4},{6,7},{7,6},{8,9},{9,8},{10,11... | collective-permute-start | bytes 1376264 | tf_op jit(solution)/shard_map/ppermute | solution.py:357
  6.7 41.3 %copy-start = (f32[384,1152]{1,0:T(8,128)S(1)}, f32[384,1152]{1,0:T(8,128)}, u32[]{:S(2)}) copy-start(f32[384,1152]{1,0:T(8,128)} %w_ref.3) | copy-start | bytes 5308420
  6.7 41.3 %copy-start.3 = (f32[384,384]{1,0:T(8,128)S(1)}, f32[384,384]{1,0:T(8,128)}, u32[]{:S(2)}) copy-start(f32[384,384]{1,0:T(8,128)} %f_ref.1) | copy-start | bytes 1769476
  6.7 41.3 %copy-start.4 = (f32[8]{0:T(128)S(1)}, f32[8]{0:T(128)}, u32[]{:S(2)}) copy-start(f32[8]{0:T(128)} %sharp_ref.1) | copy-start | bytes 100
  6.8 5.5 %collective-permute-start.3 = (f32[224,128]{1,0:T(8,128)S(1)}, f32[224,128]{1,0:T(8,128)S(1)}, u32[]{:S(2)}, u32[]{:S(2)}) collective-permute-start(f32[224,128]{1,0:T(8,128)S(1)} %get-tuple-element.22), channel_id=1, source_target_pairs={{0,2},{2,0},{4,6},{6,4},{8,10},{10,8},{12,14},{14,12},{16,18},{18,... | collective-permute-start | bytes 344072 | tf_op jit(solution)/shard_map/ppermute | solution.py:369
  8.8 7.4 %collective-permute-start.2 = (f32[224,128]{1,0:T(8,128)S(1)}, f32[224,128]{1,0:T(8,128)S(1)}, u32[]{:S(2)}, u32[]{:S(2)}) collective-permute-start(f32[224,128]{1,0:T(8,128)S(1)} %get-tuple-element.23), channel_id=1, source_target_pairs={{0,16},{2,18},{4,20},{6,22},{8,24},{10,26},{12,28},{14,30},{16,0},... | collective-permute-start | bytes 344072 | tf_op jit(solution)/shard_map/ppermute | solution.py:369
  10.0 6.2 %collective-permute-start.1 = (f32[224,128]{1,0:T(8,128)S(1)}, f32[224,128]{1,0:T(8,128)S(1)}, u32[]{:S(2)}, u32[]{:S(2)}) collective-permute-start(f32[224,128]{1,0:T(8,128)S(1)} %get-tuple-element.24), channel_id=1, source_target_pairs={{0,18},{2,16},{4,22},{6,20},{8,26},{10,24},{12,30},{14,28},{16,2},... | collective-permute-start | bytes 344072 | tf_op jit(solution)/shard_map/ppermute | solution.py:369
  16.2 4.9 %collective-permute-start.4 = (f32[224,128]{1,0:T(8,128)S(1)}, f32[224,128]{1,0:T(8,128)S(1)}, u32[]{:S(2)}, u32[]{:S(2)}) collective-permute-start(f32[224,128]{1,0:T(8,128)S(1)} %fusion), channel_id=1, source_target_pairs={{0,48},{2,50},{4,52},{6,54},{8,56},{10,58},{12,60},{14,62},{16,32}... | collective-permute-start | bytes 344072 | tf_op jit(solution)/shard_map/ppermute | solution.py:369
  21.1 9.1 %collective-permute-start.5 = (f32[224,128]{1,0:T(8,128)S(1)}, f32[224,128]{1,0:T(8,128)S(1)}, u32[]{:S(2)}, u32[]{:S(2)}) collective-permute-start(f32[224,128]{1,0:T(8,128)S(1)} %add.47), channel_id=1, source_target_pairs={{0,12},{2,14},{4,8},{6,10},{8,4},{10,6},{12,0},{14,2},{16,28},{18,... | collective-permute-start | bytes 344072 | tf_op jit(solution)/shard_map/ppermute | solution.py:369
  30.2 6.6 %collective-permute-start.6 = (f32[224,128]{1,0:T(8,128)S(1)}, f32[224,128]{1,0:T(8,128)S(1)}, u32[]{:S(2)}, u32[]{:S(2)}) collective-permute-start(f32[224,128]{1,0:T(8,128)S(1)} %add.48), channel_id=1, source_target_pairs={{0,4},{2,6},{4,0},{6,2},{8,12},{10,14},{12,8},{14,10},{16,20},{18,... | collective-permute-start | bytes 344072 | tf_op jit(solution)/shard_map/ppermute | solution.py:369
  36.8 20.6 %copy-start.1 = (f32[1,1024,384]{2,1,0:T(8,128)S(1)}, f32[1,1024,384]{2,1,0:T(8,128)}, u32[]{:S(2)}) copy-start(f32[1,1024,384]{2,1,0:T(8,128)} %param.5) | copy-start | bytes 4718596
  36.8 20.6 %copy-start.2 = (f32[1,1024,384]{2,1,0:T(8,128)S(1)}, f32[1,1024,384]{2,1,0:T(8,128)}, u32[]{:S(2)}) copy-start(f32[1,1024,384]{2,1,0:T(8,128)} %param.9) | copy-start | bytes 4718596
  36.8 4.9 %collective-permute-start.9 = (f32[224,128]{1,0:T(8,128)S(1)}, f32[224,128]{1,0:T(8,128)S(1)}, u32[]{:S(2)}, u32[]{:S(2)}) collective-permute-start(f32[224,128]{1,0:T(8,128)S(1)} %add.49.m0), channel_id=1, source_target_pairs={{0,2},{2,0},{4,6},{6,4},{8,10},{10,8},{12,14},{14,12},{16,18},{18,... | collective-permute-start | bytes 344072 | tf_op jit(solution)/shard_map/ppermute | solution.py:369
  38.3 6.2 %collective-permute-start.8 = (f32[224,128]{1,0:T(8,128)S(1)}, f32[224,128]{1,0:T(8,128)S(1)}, u32[]{:S(2)}, u32[]{:S(2)}) collective-permute-start(f32[224,128]{1,0:T(8,128)S(1)} %add.49.m0), channel_id=1, source_target_pairs={{0,16},{2,18},{4,20},{6,22},{8,24},{10,26},{12,28},{14,30},{16,0},... | collective-permute-start | bytes 344072 | tf_op jit(solution)/shard_map/ppermute | solution.py:369
  41.0 5.7 %collective-permute-start.7 = (f32[224,128]{1,0:T(8,128)S(1)}, f32[224,128]{1,0:T(8,128)S(1)}, u32[]{:S(2)}, u32[]{:S(2)}) collective-permute-start(f32[224,128]{1,0:T(8,128)S(1)} %add.49.m0), channel_id=1, source_target_pairs={{0,18},{2,16},{4,22},{6,20},{8,26},{10,24},{12,30},{14,28},{16,2},... | collective-permute-start | bytes 344072 | tf_op jit(solution)/shard_map/ppermute | solution.py:369
  41.0 5.7 %collective-permute-start.10 = (f32[224,128]{1,0:T(8,128)S(1)}, f32[224,128]{1,0:T(8,128)S(1)}, u32[]{:S(2)}, u32[]{:S(2)}) collective-permute-start(f32[224,128]{1,0:T(8,128)S(1)} %add.49.m0), channel_id=1, source_target_pairs={{0,1},{1,0},{2,3},{3,2},{4,5},{5,4},{6,7},{7,6},{8,9},{9,8},{10,11... | collective-permute-start | bytes 344072 | tf_op jit(solution)/shard_map/ppermute | solution.py:357
  41.7 5.0 %collective-permute-start.13 = (f32[224,128]{1,0:T(8,128)S(1)}, f32[224,128]{1,0:T(8,128)S(1)}, u32[]{:S(2)}, u32[]{:S(2)}) collective-permute-start(f32[224,128]{1,0:T(8,128)S(1)} %collective-permute-done.9.m3), channel_id=1, source_target_pairs={{0,1},{1,0},{2,3},{3,2},{4,5},{5,4},{6,7},{7,6},{8,9},{9,8},{10,11... | collective-permute-start | bytes 344072 | tf_op jit(solution)/shard_map/ppermute | solution.py:357
  44.5 2.1 %collective-permute-start.12 = (f32[224,128]{1,0:T(8,128)S(1)}, f32[224,128]{1,0:T(8,128)S(1)}, u32[]{:S(2)}, u32[]{:S(2)}) collective-permute-start(f32[224,128]{1,0:T(8,128)S(1)} %collective-permute-done.8.m2), channel_id=1, source_target_pairs={{0,1},{1,0},{2,3},{3,2},{4,5},{5,4},{6,7},{7,6},{8,9},{9,8},{10,11... | collective-permute-start | bytes 344072 | tf_op jit(solution)/shard_map/ppermute | solution.py:357
  46.6 1.3 %collective-permute-start.11 = (f32[224,128]{1,0:T(8,128)S(1)}, f32[224,128]{1,0:T(8,128)S(1)}, u32[]{:S(2)}, u32[]{:S(2)}) collective-permute-start(f32[224,128]{1,0:T(8,128)S(1)} %collective-permute-done.7.m1), channel_id=1, source_target_pairs={{0,1},{1,0},{2,3},{3,2},{4,5},{5,4},{6,7},{7,6},{8,9},{9,8},{10,11... | collective-permute-start | bytes 344072 | tf_op jit(solution)/shard_map/ppermute | solution.py:357
  52.1 10.7 %collective-permute-start.16 = (f32[8,1664]{1,0:T(8,128)S(1)}, f32[8,1664]{1,0:T(8,128)S(1)}, u32[]{:S(2)}, u32[]{:S(2)}) collective-permute-start(f32[8,1664]{1,0:T(8,128)S(1)} %get-tuple-element.18.own_ref), channel_id=1, source_target_pairs={{0,64},{64,128},{128,192},{192,0},{1,65},{65,129},{129,193},{193,1... | collective-permute-start | bytes 159752 | tf_op jit(solution)/shard_map/ppermute | solution.py:361
  53.7 9.0 %collective-permute-start.15 = (f32[8,1664]{1,0:T(8,128)S(1)}, f32[8,1664]{1,0:T(8,128)S(1)}, u32[]{:S(2)}, u32[]{:S(2)}) collective-permute-start(f32[8,1664]{1,0:T(8,128)S(1)} %get-tuple-element.18.own_ref), channel_id=1, source_target_pairs={{0,192},{64,0},{128,64},{192,128},{1,193},{65,1},{129,65},{193,129... | collective-permute-start | bytes 159752 | tf_op jit(solution)/shard_map/ppermute | solution.py:361
  55.4 7.4 %collective-permute-start.14 = (f32[8,1664]{1,0:T(8,128)S(1)}, f32[8,1664]{1,0:T(8,128)S(1)}, u32[]{:S(2)}, u32[]{:S(2)}) collective-permute-start(f32[8,1664]{1,0:T(8,128)S(1)} %get-tuple-element.18.own_ref), channel_id=1, source_target_pairs={{0,128},{64,192},{128,0},{192,64},{1,129},{65,193},{129,1},{193,65... | collective-permute-start | bytes 159752 | tf_op jit(solution)/shard_map/ppermute | solution.py:361

commit v8 on v7

--- a/solution.py
+++ b/solution.py
@@ -80,7 +80,8 @@
     return (lax.broadcasted_iota(jnp.int32, (T, T), axis) for axis in range(2))
 
 
-def gram_kernel(place_ref, x_hbm, u_hbm, keep_ref, send_ref, x_ref, u_ref, pay_ref, sems):
+def gram_kernel(place_ref, x_hbm, u_hbm, *refs):
+    keeps, sends, (x_ref, u_ref, pay_ref, sems) = refs[:SQUARE], refs[SQUARE : 2 * SQUARE], refs[2 * SQUARE :]
     step = x_ref.shape[0] // 2
     copies = []
     for part in range(2):
@@ -119,9 +120,8 @@
     core, chip = place_ref[0], place_ref[2]
     for k in range(SQUARE):
         to = chip ^ k
-        piece = pl.ds(k * QUARTER, QUARTER)
-        keep_ref[piece] = pay_ref[core, quarter_of(to)]
-        send_ref[piece] = pay_ref[1 - core, quarter_of(to)]
+        keeps[k][...] = pay_ref[core, quarter_of(to)]
+        sends[k][...] = pay_ref[1 - core, quarter_of(to)]
 
 
 def heads_of(shape, axis, window):
@@ -338,12 +338,12 @@
     def in_hbm(array):
         return pltpu.with_memory_space_constraint(array, pltpu.HBM)
 
-    half = ((HALF, T), f32)
-    keep, send = call(
+    quarter = ((QUARTER, T), f32)
+    pieces = call(
         gram_kernel,
         [smem, hbm, hbm],
-        [vmem] * 2,
-        [half] * 2,
+        [vmem] * 2 * SQUARE,
+        [quarter] * 2 * SQUARE,
         [
             pltpu.VMEM((tokens, D), f32),
             pltpu.VMEM((tokens, D), f32),
@@ -371,8 +371,8 @@
     def within_square(pieces):
         return [exchange(piece, k // 2, k % 2) for k, piece in zip(AWAY, pieces)]
 
-    part = (keep + swap(send)).reshape(SQUARE, QUARTER, T)
-    others = within_square([part[k] for k in AWAY])
+    part = [keep + swap(send) for keep, send in zip(pieces[:SQUARE], pieces[SQUARE:])]
+    others = [exchange(part[k], k // 2, k % 2) for k in reversed(AWAY)]
     part = (part[0] + others[0]) + (others[1] + others[2])
     for apart in ((3, 0), (0, 6), (0, 2)):
         part = part + exchange(part, *apart)

time: 63.5 us -> 63.3 us (level)
  waiting for transfers between devices: 26.4 us -> 24.4 us
  starting transfers between devices: 21.9 us -> 23.6 us
    ppermute x5 -> x8, waiting for transfers between devices: 3.11 us -> 1.62 us  [swap(): return lax.ppermute(array, 'core', [(0, 1), (1, 0)])]
    ppermute x5 -> x8, starting transfers between devices: 0.1 us -> 1.3 us  [swap(): return lax.ppermute(array, 'core', [(0, 1), (1, 0)])]
  transfers between devices with their start and end apart: 17 -> 20, of which waited for: 10 -> 10; matrix products, arithmetic and copies ran while one was open for 0% -> 0% of each run, Pallas kernels for 8% -> 8%
where the time goes in v8:
time: 63.3 us; the launch traced here: 63.2 us
  waiting for transfers between devices  24.4 us (39%)
  starting transfers between devices  23.6 us (37%)
  Pallas kernels  14.2 us (22%)
  between operations  0.82 us (1%)
    ppermute x9, waiting for transfers between devices, exchange(): return lax.ppermute(array, ('x', 'z'), pairs)  22.8 us
    ppermute x9, starting transfers between devices, exchange(): return lax.ppermute(array, ('x', 'z'), pairs)  17 us
    pallas_call x1, Pallas kernels, body(): call(output_kernel, [vmem] * 6, [hbm], [((tokens, D), f32)], [pltpu.VMEM(...  5.37 us
    ppermute x3, starting transfers between devices, shift(): lax.ppermute(array, axis, [(i, (i + by) % size) for i in range(size)])  5.3 us
    pallas_call x1, Pallas kernels, body(): call(solve_kernel, [smem, smem] + [vmem] * 10, [vmem] * 4, [((2, D, D), b...  4.11 us
    pallas_call x1, Pallas kernels, body(): call(gram_kernel, [smem, hbm, hbm], [vmem] * 2 * SQUARE, [quarter] * 2 *...  4.04 us
    ppermute x8, waiting for transfers between devices, swap(): return lax.ppermute(array, 'core', [(0, 1), (1, 0)])  1.62 us
    ppermute x8, starting transfers between devices, swap(): return lax.ppermute(array, 'core', [(0, 1), (1, 0)])  1.3 us
  transfers between devices with their start and end apart: 20, of which 10 were waited for; matrix products, arithmetic and copies ran while one was open for 0% of the time, Pallas kernels for 8%

profile of v8, /device:TPU:4, one launch (start us, length us, event | category | flops | bytes accessed | tf_op | source)
XLA Modules:
  0.0 63.2 jit_solution(5050258640599756742)
XLA Ops:
  0.7 4.0 %shard_map.84 = (f32[224,128]{1,0:T(8,128)S(1)}, f32[224,128]{1,0:T(8,128)S(1)}, f32[224,128]{1,0:T(8,128)S(1)}, f32[224,128]{1,0:T(8,128)S(1)}, f32[224,128]{1,...) custom-call(s32[3]{0:T(128)S(1)} %pad_add_fusion.place_ref, ...), custom_call_target="tpu_custom_call" | custom-call | flops 2038431744 | bytes 4194304 | tf_op jit(solution)/shard_map/pallas_call | solution.py:342
  4.9 0.5 collective-permute-start.3
  6.3 2.0 %collective-permute-start.2 = (f32[224,128]{1,0:T(8,128)S(1)}, f32[224,128]{1,0:T(8,128)S(1)}, u32[]{:S(2)}, u32[]{:S(2)}) collective-permute-start(f32[224,128]{1,0:T(8,128)S(1)} %add.53), channel_id=1, source_target_pairs={{0,2},{2,0},{4,6},{6,4},{8,10},{10,8},{12,14},{14,12},{16,18},{18,... | collective-permute-start | bytes 344072 | tf_op jit(solution)/shard_map/ppermute | solution.py:369
  8.3 1.3 %collective-permute-start.4 = (f32[224,128]{1,0:T(8,128)S(1)}, f32[224,128]{1,0:T(8,128)S(1)}, u32[]{:S(2)}, u32[]{:S(2)}) collective-permute-start(f32[224,128]{1,0:T(8,128)S(1)} %add.55), channel_id=1, source_target_pairs={{0,16},{2,18},{4,20},{6,22},{8,24},{10,26},{12,28},{14,30},{16,0},... | collective-permute-start | bytes 344072 | tf_op jit(solution)/shard_map/ppermute | solution.py:369
  9.6 0.5 collective-permute-start.6
  10.1 1.7 %collective-permute-done.2 = f32[224,128]{1,0:T(8,128)S(1)} collective-permute-done((f32[224,128]{1,0:T(8,128)S(1)}, f32[224,128]{1,0:T(8,128)S(1)}, u32[]{:S(2)}, u32[]{:S(2)}) %collective-permute-start.2) | collective-permute-done | bytes 114720 | tf_op jit(solution)/shard_map/ppermute | solution.py:369
  11.8 4.0 %collective-permute-done.4 = f32[224,128]{1,0:T(8,128)S(1)} collective-permute-done((f32[224,128]{1,0:T(8,128)S(1)}, f32[224,128]{1,0:T(8,128)S(1)}, u32[]{:S(2)}, u32[]{:S(2)}) %collective-permute-start.4) | collective-permute-done | bytes 114720 | tf_op jit(solution)/shard_map/ppermute | solution.py:369
  15.8 0.6 collective-permute-start.7
  16.4 4.3 %collective-permute-done.7 = f32[224,128]{1,0:T(8,128)S(1)} collective-permute-done((f32[224,128]{1,0:T(8,128)S(1)}, f32[224,128]{1,0:T(8,128)S(1)}, u32[]{:S(2)}, u32[]{:S(2)}) %collective-permute-start.7) | collective-permute-done | bytes 114720 | tf_op jit(solution)/shard_map/ppermute | solution.py:369
  20.7 5.5 %collective-permute-start.8 = (f32[224,128]{1,0:T(8,128)S(1)}, f32[224,128]{1,0:T(8,128)S(1)}, u32[]{:S(2)}, u32[]{:S(2)}) collective-permute-start(f32[224,128]{1,0:T(8,128)S(1)} %add.59), channel_id=1, source_target_pairs={{0,12},{2,14},{4,8},{6,10},{8,4},{10,6},{12,0},{14,2},{16,28},{18,... | collective-permute-start | bytes 344072 | tf_op jit(solution)/shard_map/ppermute | solution.py:369
  26.2 3.6 %collective-permute-done.8 = f32[224,128]{1,0:T(8,128)S(1)} collective-permute-done((f32[224,128]{1,0:T(8,128)S(1)}, f32[224,128]{1,0:T(8,128)S(1)}, u32[]{:S(2)}, u32[]{:S(2)}) %collective-permute-start.8) | collective-permute-done | bytes 114720 | tf_op jit(solution)/shard_map/ppermute | solution.py:369
  29.8 2.6 %collective-permute-start.9 = (f32[224,128]{1,0:T(8,128)S(1)}, f32[224,128]{1,0:T(8,128)S(1)}, u32[]{:S(2)}, u32[]{:S(2)}) collective-permute-start(f32[224,128]{1,0:T(8,128)S(1)} %add.60), channel_id=1, source_target_pairs={{0,4},{2,6},{4,0},{6,2},{8,12},{10,14},{12,8},{14,10},{16,20},{18,... | collective-permute-start | bytes 344072 | tf_op jit(solution)/shard_map/ppermute | solution.py:369
  32.3 3.8 %collective-permute-done.9 = f32[224,128]{1,0:T(8,128)S(1)} collective-permute-done((f32[224,128]{1,0:T(8,128)S(1)}, f32[224,128]{1,0:T(8,128)S(1)}, u32[]{:S(2)}, u32[]{:S(2)}) %collective-permute-start.9) | collective-permute-done | bytes 114720 | tf_op jit(solution)/shard_map/ppermute | solution.py:369
  36.2 2.0 %collective-permute-start.12 = (f32[224,128]{1,0:T(8,128)S(1)}, f32[224,128]{1,0:T(8,128)S(1)}, u32[]{:S(2)}, u32[]{:S(2)}) collective-permute-start(f32[224,128]{1,0:T(8,128)S(1)} %add.61.m0), channel_id=1, source_target_pairs={{0,2},{2,0},{4,6},{6,4},{8,10},{10,8},{12,14},{14,12},{16,18},{18,... | collective-permute-start | bytes 344072 | tf_op jit(solution)/shard_map/ppermute | solution.py:369
  38.1 2.6 %collective-permute-start.11 = (f32[224,128]{1,0:T(8,128)S(1)}, f32[224,128]{1,0:T(8,128)S(1)}, u32[]{:S(2)}, u32[]{:S(2)}) collective-permute-start(f32[224,128]{1,0:T(8,128)S(1)} %add.61.m0), channel_id=1, source_target_pairs={{0,16},{2,18},{4,20},{6,22},{8,24},{10,26},{12,28},{14,30},{16,0},... | collective-permute-start | bytes 344072 | tf_op jit(solution)/shard_map/ppermute | solution.py:369
  41.2 3.1 %collective-permute-done.11.m2 = f32[224,128]{1,0:T(8,128)S(1)} collective-permute-done((f32[224,128]{1,0:T(8,128)S(1)}, f32[224,128]{1,0:T(8,128)S(1)}, u32[]{:S(2)}, u32[]{:S(2)}) %collective-permute-start.11) | collective-permute-done | bytes 114720 | tf_op jit(solution)/shard_map/ppermute | solution.py:369
  44.3 2.1 %collective-permute-done.10.m1 = f32[224,128]{1,0:T(8,128)S(1)} collective-permute-done((f32[224,128]{1,0:T(8,128)S(1)}, f32[224,128]{1,0:T(8,128)S(1)}, u32[]{:S(2)}, u32[]{:S(2)}) %collective-permute-start.10) | collective-permute-done | bytes 114720 | tf_op jit(solution)/shard_map/ppermute | solution.py:369
  46.4 1.3 %collective-permute-done.14.o1 = f32[224,128]{1,0:T(8,128)S(1)} collective-permute-done((f32[224,128]{1,0:T(8,128)S(1)}, f32[224,128]{1,0:T(8,128)S(1)}, u32[]{:S(2)}, u32[]{:S(2)}) %collective-permute-start.14) | collective-permute-done | bytes 114720 | tf_op jit(solution)/shard_map/ppermute | solution.py:357
  47.8 4.1 %shard_map.85 = (bf16[2,384,384]{2,1,0:T(8,128)(2,1)S(1)}, bf16[2,2,256,256]{3,2,1,0:T(8,128)(2,1)S(1)}, f32[2,384]{1,0:T(2,128)S(1)}, f32[8,1664]{1,0:T(8,128)S(1)}) custom-call(s32[3]{0:T(128)S(1)} %pad_add_fusion.place_ref, f32[8]{0:T(128)S(1)} %copy-done.4, f32[384,1152]{1,0:T(8,128)S(1)} %copy-done, f32[384,384]{1,0:T(8,128)S(1)} %copy-done.3, ...), custom_call_target="tpu_custom_call" | custom-call | flops 2717908992 | bytes 4194304 | tf_op jit(solution)/shard_map/pallas_call | solution.py:382
  51.9 1.6 %collective-permute-start.19 = (f32[8,1664]{1,0:T(8,128)S(1)}, f32[8,1664]{1,0:T(8,128)S(1)}, u32[]{:S(2)}, u32[]{:S(2)}) collective-permute-start(f32[8,1664]{1,0:T(8,128)S(1)} %get-tuple-element.30.own_ref), channel_id=1, source_target_pairs={{0,64},{64,128},{128,192},{192,0},{1,65},{65,129},{129,193},{193,1... | collective-permute-start | bytes 159752 | tf_op jit(solution)/shard_map/ppermute | solution.py:361
  53.5 1.7 %collective-permute-start.18 = (f32[8,1664]{1,0:T(8,128)S(1)}, f32[8,1664]{1,0:T(8,128)S(1)}, u32[]{:S(2)}, u32[]{:S(2)}) collective-permute-start(f32[8,1664]{1,0:T(8,128)S(1)} %get-tuple-element.30.own_ref), channel_id=1, source_target_pairs={{0,192},{64,0},{128,64},{192,128},{1,193},{65,1},{129,65},{193,129... | collective-permute-start | bytes 159752 | tf_op jit(solution)/shard_map/ppermute | solution.py:361
  55.2 2.0 %collective-permute-start.17 = (f32[8,1664]{1,0:T(8,128)S(1)}, f32[8,1664]{1,0:T(8,128)S(1)}, u32[]{:S(2)}, u32[]{:S(2)}) collective-permute-start(f32[8,1664]{1,0:T(8,128)S(1)} %get-tuple-element.30.own_ref), channel_id=1, source_target_pairs={{0,128},{64,192},{128,0},{192,64},{1,129},{65,193},{129,1},{193,65... | collective-permute-start | bytes 159752 | tf_op jit(solution)/shard_map/ppermute | solution.py:361
  57.2 5.4 %shard_map.86 = f32[1024,384]{1,0:T(8,128)} custom-call(f32[1024,384]{1,0:T(8,128)S(1)} %bitcast.8, f32[1024,384]{1,0:T(8,128)S(1)} %bitcast.10, f32[384,1152]{1,0:T(8,128)S(1)} %copy-done, bf16[2,384,384]{2,1,0:T(8,128)(2,1)S(1)} %get-tuple-element.27.gv_ref, bf16[2,2,256,256]{3,2,1,0:T(8,128)(2,1)S(1)} %get-tuple-element.28.m_ref, ...), custom_call_target="tpu_custom_call" | custom-call | flops 4076863488 | bytes 4194304 | tf_op jit(solution)/shard_map/pallas_call | solution.py:399
  62.6 0.6 %shard_map.87 = (f32[6,1152]{1,0:T(8,128)}, f32[6,384]{1,0:T(8,128)}, f32[1,8]{1,0:T(1,128)}) custom-call(f32[8,1664]{1,0:T(8,128)S(1)} %get-tuple-element.30.own_ref, f32[8,1664]{1,0:T(8,128)S(1)} %collective-permute-done.17.two_ref, f32[8,1664]{1,0:T(8,128)S(1)} %collective-permute-done.18.three_ref, f32[8,1664]{1,0:T(8,128)S(1)} %collective-permute-done.19.one_ref), custom_call_target="tpu_custom_call" | custom-call | bytes 4194304 | tf_op jit(solution)/shard_map/pallas_call | solution.py:407
  (38 shorter events, 1.7 us)
Async XLA Ops:
  4.8 43.0 %copy-start = (f32[384,1152]{1,0:T(8,128)S(1)}, f32[384,1152]{1,0:T(8,128)}, u32[]{:S(2)}) copy-start(f32[384,1152]{1,0:T(8,128)} %w_ref.3) | copy-start | bytes 5308420
  4.8 42.9 %copy-start.3 = (f32[384,384]{1,0:T(8,128)S(1)}, f32[384,384]{1,0:T(8,128)}, u32[]{:S(2)}) copy-start(f32[384,384]{1,0:T(8,128)} %f_ref.1) | copy-start | bytes 1769476
  4.8 42.9 %copy-start.4 = (f32[8]{0:T(128)S(1)}, f32[8]{0:T(128)}, u32[]{:S(2)}) copy-start(f32[8]{0:T(128)} %sharp_ref.1) | copy-start | bytes 100
  4.8 1.4 %collective-permute-start.1 = (f32[224,128]{1,0:T(8,128)S(1)}, f32[224,128]{1,0:T(8,128)S(1)}, u32[]{:S(2)}, u32[]{:S(2)}) collective-permute-start(f32[224,128]{1,0:T(8,128)S(1)} %get-tuple-element.22), channel_id=1, source_target_pairs={{0,1},{1,0},{2,3},{3,2},{4,5},{5,4},{6,7},{7,6},{8,9},{9,8},{10,11... | collective-permute-start | bytes 344072 | tf_op jit(solution)/shard_map/ppermute | solution.py:357
  4.9 3.3 %collective-permute-start.3 = (f32[224,128]{1,0:T(8,128)S(1)}, f32[224,128]{1,0:T(8,128)S(1)}, u32[]{:S(2)}, u32[]{:S(2)}) collective-permute-start(f32[224,128]{1,0:T(8,128)S(1)} %get-tuple-element.24), channel_id=1, source_target_pairs={{0,1},{1,0},{2,3},{3,2},{4,5},{5,4},{6,7},{7,6},{8,9},{9,8},{10,11... | collective-permute-start | bytes 344072 | tf_op jit(solution)/shard_map/ppermute | solution.py:357
  5.4 4.2 %collective-permute-start.5 = (f32[224,128]{1,0:T(8,128)S(1)}, f32[224,128]{1,0:T(8,128)S(1)}, u32[]{:S(2)}, u32[]{:S(2)}) collective-permute-start(f32[224,128]{1,0:T(8,128)S(1)} %get-tuple-element.26), channel_id=1, source_target_pairs={{0,1},{1,0},{2,3},{3,2},{4,5},{5,4},{6,7},{7,6},{8,9},{9,8},{10,11... | collective-permute-start | bytes 344072 | tf_op jit(solution)/shard_map/ppermute | solution.py:357
  5.5 4.5 %collective-permute-start = (f32[224,128]{1,0:T(8,128)S(1)}, f32[224,128]{1,0:T(8,128)S(1)}, u32[]{:S(2)}, u32[]{:S(2)}) collective-permute-start(f32[224,128]{1,0:T(8,128)S(1)} %get-tuple-element.20), channel_id=1, source_target_pairs={{0,1},{1,0},{2,3},{3,2},{4,5},{5,4},{6,7},{7,6},{8,9},{9,8},{10,11... | collective-permute-start | bytes 344072 | tf_op jit(solution)/shard_map/ppermute | solution.py:357
  6.3 5.5 %collective-permute-start.2 = (f32[224,128]{1,0:T(8,128)S(1)}, f32[224,128]{1,0:T(8,128)S(1)}, u32[]{:S(2)}, u32[]{:S(2)}) collective-permute-start(f32[224,128]{1,0:T(8,128)S(1)} %add.53), channel_id=1, source_target_pairs={{0,2},{2,0},{4,6},{6,4},{8,10},{10,8},{12,14},{14,12},{16,18},{18,... | collective-permute-start | bytes 344072 | tf_op jit(solution)/shard_map/ppermute | solution.py:369
  8.3 7.5 %collective-permute-start.4 = (f32[224,128]{1,0:T(8,128)S(1)}, f32[224,128]{1,0:T(8,128)S(1)}, u32[]{:S(2)}, u32[]{:S(2)}) collective-permute-start(f32[224,128]{1,0:T(8,128)S(1)} %add.55), channel_id=1, source_target_pairs={{0,16},{2,18},{4,20},{6,22},{8,24},{10,26},{12,28},{14,30},{16,0},... | collective-permute-start | bytes 344072 | tf_op jit(solution)/shard_map/ppermute | solution.py:369
  9.6 6.2 %collective-permute-start.6 = (f32[224,128]{1,0:T(8,128)S(1)}, f32[224,128]{1,0:T(8,128)S(1)}, u32[]{:S(2)}, u32[]{:S(2)}) collective-permute-start(f32[224,128]{1,0:T(8,128)S(1)} %add.56), channel_id=1, source_target_pairs={{0,18},{2,16},{4,22},{6,20},{8,26},{10,24},{12,30},{14,28},{16,2},... | collective-permute-start | bytes 344072 | tf_op jit(solution)/shard_map/ppermute | solution.py:369
  15.8 4.9 %collective-permute-start.7 = (f32[224,128]{1,0:T(8,128)S(1)}, f32[224,128]{1,0:T(8,128)S(1)}, u32[]{:S(2)}, u32[]{:S(2)}) collective-permute-start(f32[224,128]{1,0:T(8,128)S(1)} %add_add_fusion), channel_id=1, source_target_pairs={{0,48},{2,50},{4,52},{6,54},{8,56},{10,58},{12,60},{14,62},{16,32}... | collective-permute-start | bytes 344072 | tf_op jit(solution)/shard_map/ppermute | solution.py:369
  20.7 9.1 %collective-permute-start.8 = (f32[224,128]{1,0:T(8,128)S(1)}, f32[224,128]{1,0:T(8,128)S(1)}, u32[]{:S(2)}, u32[]{:S(2)}) collective-permute-start(f32[224,128]{1,0:T(8,128)S(1)} %add.59), channel_id=1, source_target_pairs={{0,12},{2,14},{4,8},{6,10},{8,4},{10,6},{12,0},{14,2},{16,28},{18,... | collective-permute-start | bytes 344072 | tf_op jit(solution)/shard_map/ppermute | solution.py:369
  29.8 6.4 %collective-permute-start.9 = (f32[224,128]{1,0:T(8,128)S(1)}, f32[224,128]{1,0:T(8,128)S(1)}, u32[]{:S(2)}, u32[]{:S(2)}) collective-permute-start(f32[224,128]{1,0:T(8,128)S(1)} %add.60), channel_id=1, source_target_pairs={{0,4},{2,6},{4,0},{6,2},{8,12},{10,14},{12,8},{14,10},{16,20},{18,... | collective-permute-start | bytes 344072 | tf_op jit(solution)/shard_map/ppermute | solution.py:369
  36.1 21.0 %copy-start.1 = (f32[1,1024,384]{2,1,0:T(8,128)S(1)}, f32[1,1024,384]{2,1,0:T(8,128)}, u32[]{:S(2)}) copy-start(f32[1,1024,384]{2,1,0:T(8,128)} %param.5) | copy-start | bytes 4718596
  36.2 4.9 %collective-permute-start.12 = (f32[224,128]{1,0:T(8,128)S(1)}, f32[224,128]{1,0:T(8,128)S(1)}, u32[]{:S(2)}, u32[]{:S(2)}) collective-permute-start(f32[224,128]{1,0:T(8,128)S(1)} %add.61.m0), channel_id=1, source_target_pairs={{0,2},{2,0},{4,6},{6,4},{8,10},{10,8},{12,14},{14,12},{16,18},{18,... | collective-permute-start | bytes 344072 | tf_op jit(solution)/shard_map/ppermute | solution.py:369
  38.1 6.2 %collective-permute-start.11 = (f32[224,128]{1,0:T(8,128)S(1)}, f32[224,128]{1,0:T(8,128)S(1)}, u32[]{:S(2)}, u32[]{:S(2)}) collective-permute-start(f32[224,128]{1,0:T(8,128)S(1)} %add.61.m0), channel_id=1, source_target_pairs={{0,16},{2,18},{4,20},{6,22},{8,24},{10,26},{12,28},{14,30},{16,0},... | collective-permute-start | bytes 344072 | tf_op jit(solution)/shard_map/ppermute | solution.py:369
  40.7 5.7 %collective-permute-start.10 = (f32[224,128]{1,0:T(8,128)S(1)}, f32[224,128]{1,0:T(8,128)S(1)}, u32[]{:S(2)}, u32[]{:S(2)}) collective-permute-start(f32[224,128]{1,0:T(8,128)S(1)} %add.61.m0), channel_id=1, source_target_pairs={{0,18},{2,16},{4,22},{6,20},{8,26},{10,24},{12,30},{14,28},{16,2},... | collective-permute-start | bytes 344072 | tf_op jit(solution)/shard_map/ppermute | solution.py:369
  40.7 5.7 %collective-permute-start.13 = (f32[224,128]{1,0:T(8,128)S(1)}, f32[224,128]{1,0:T(8,128)S(1)}, u32[]{:S(2)}, u32[]{:S(2)}) collective-permute-start(f32[224,128]{1,0:T(8,128)S(1)} %add.61.m0), channel_id=1, source_target_pairs={{0,1},{1,0},{2,3},{3,2},{4,5},{5,4},{6,7},{7,6},{8,9},{9,8},{10,11... | collective-permute-start | bytes 344072 | tf_op jit(solution)/shard_map/ppermute | solution.py:357
  41.1 5.4 %collective-permute-start.16 = (f32[224,128]{1,0:T(8,128)S(1)}, f32[224,128]{1,0:T(8,128)S(1)}, u32[]{:S(2)}, u32[]{:S(2)}) collective-permute-start(f32[224,128]{1,0:T(8,128)S(1)} %collective-permute-done.12.m3), channel_id=1, source_target_pairs={{0,1},{1,0},{2,3},{3,2},{4,5},{5,4},{6,7},{7,6},{8,9},{9,8},{10,11... | collective-permute-start | bytes 344072 | tf_op jit(solution)/shard_map/ppermute | solution.py:357
  44.3 2.1 %collective-permute-start.15 = (f32[224,128]{1,0:T(8,128)S(1)}, f32[224,128]{1,0:T(8,128)S(1)}, u32[]{:S(2)}, u32[]{:S(2)}) collective-permute-start(f32[224,128]{1,0:T(8,128)S(1)} %collective-permute-done.11.m2), channel_id=1, source_target_pairs={{0,1},{1,0},{2,3},{3,2},{4,5},{5,4},{6,7},{7,6},{8,9},{9,8},{10,11... | collective-permute-start | bytes 344072 | tf_op jit(solution)/shard_map/ppermute | solution.py:357
  46.4 1.3 %collective-permute-start.14 = (f32[224,128]{1,0:T(8,128)S(1)}, f32[224,128]{1,0:T(8,128)S(1)}, u32[]{:S(2)}, u32[]{:S(2)}) collective-permute-start(f32[224,128]{1,0:T(8,128)S(1)} %collective-permute-done.10.m1), channel_id=1, source_target_pairs={{0,1},{1,0},{2,3},{3,2},{4,5},{5,4},{6,7},{7,6},{8,9},{9,8},{10,11... | collective-permute-start | bytes 344072 | tf_op jit(solution)/shard_map/ppermute | solution.py:357
  51.9 10.7 %collective-permute-start.19 = (f32[8,1664]{1,0:T(8,128)S(1)}, f32[8,1664]{1,0:T(8,128)S(1)}, u32[]{:S(2)}, u32[]{:S(2)}) collective-permute-start(f32[8,1664]{1,0:T(8,128)S(1)} %get-tuple-element.30.own_ref), channel_id=1, source_target_pairs={{0,64},{64,128},{128,192},{192,0},{1,65},{65,129},{129,193},{193,1... | collective-permute-start | bytes 159752 | tf_op jit(solution)/shard_map/ppermute | solution.py:361
  53.5 9.1 %collective-permute-start.18 = (f32[8,1664]{1,0:T(8,128)S(1)}, f32[8,1664]{1,0:T(8,128)S(1)}, u32[]{:S(2)}, u32[]{:S(2)}) collective-permute-start(f32[8,1664]{1,0:T(8,128)S(1)} %get-tuple-element.30.own_ref), channel_id=1, source_target_pairs={{0,192},{64,0},{128,64},{192,128},{1,193},{65,1},{129,65},{193,129... | collective-permute-start | bytes 159752 | tf_op jit(solution)/shard_map/ppermute | solution.py:361
  55.2 7.4 %collective-permute-start.17 = (f32[8,1664]{1,0:T(8,128)S(1)}, f32[8,1664]{1,0:T(8,128)S(1)}, u32[]{:S(2)}, u32[]{:S(2)}) collective-permute-start(f32[8,1664]{1,0:T(8,128)S(1)} %get-tuple-element.30.own_ref), channel_id=1, source_target_pairs={{0,128},{64,192},{128,0},{192,64},{1,129},{65,193},{129,1},{193,65... | collective-permute-start | bytes 159752 | tf_op jit(solution)/shard_map/ppermute | solution.py:361
  (1 other events, 21.0 us)

commit v9 on v8

--- a/solution.py
+++ b/solution.py
@@ -216,7 +216,8 @@
     attentions, covs, mixers = [], [], []
     for window, span in enumerate(WINDOWS):
         same = masks(window)
-        cov = jnp.where(same, raw[window] * to_col(eye, q_inv[:, span]) * k_inv[:, span], 0.0)
+        cov = raw[window] * to_col(eye, q_inv[:, span]) * k_inv[:, span]
+        cov = jnp.where(same, jnp.clip(cov, -1.0, 1.0), 0.0)
         table = jnp.where(same, jnp.exp(sharp_col(sharp_ref, window) * cov), 0.0)
         total = jnp.sum(table, axis=1, keepdims=True)
         attention = table / jnp.where(total > 0.0, total, 1.0)

time: 63.3 us -> 63.3 us (level)
  no operation moved by 1% of the time
where the time goes in v9:
time: 63.3 us
  waiting for transfers between devices  24.4 us (39%)
  starting transfers between devices  23.6 us (37%)
  Pallas kernels  14.2 us (22%)
  between operations  0.82 us (1%)
    ppermute x9, waiting for transfers between devices, exchange(): return lax.ppermute(array, ('x', 'z'), pairs)  22.8 us
    ppermute x9, starting transfers between devices, exchange(): return lax.ppermute(array, ('x', 'z'), pairs)  17 us
    pallas_call x1, Pallas kernels, body(): call(output_kernel, [vmem] * 6, [hbm], [((tokens, D), f32)], [pltpu.VMEM(...  5.38 us
    ppermute x3, starting transfers between devices, shift(): lax.ppermute(array, axis, [(i, (i + by) % size) for i in range(size)])  5.3 us
    pallas_call x1, Pallas kernels, body(): call(solve_kernel, [smem, smem] + [vmem] * 10, [vmem] * 4, [((2, D, D), b...  4.13 us
    pallas_call x1, Pallas kernels, body(): call(gram_kernel, [smem, hbm, hbm], [vmem] * 2 * SQUARE, [quarter] * 2 *...  4.04 us
    ppermute x8, waiting for transfers between devices, swap(): return lax.ppermute(array, 'core', [(0, 1), (1, 0)])  1.62 us
    ppermute x8, starting transfers between devices, swap(): return lax.ppermute(array, 'core', [(0, 1), (1, 0)])  1.3 us
  transfers between devices with their start and end apart: 20, of which 10 were waited for; matrix products, arithmetic and copies ran while one was open for 0% of the time, Pallas kernels for 8%

profile of v9, /device:TPU:4, one launch (start us, length us, event | category | flops | bytes accessed | tf_op | source)
XLA Modules:
  0.0 63.3 jit_solution(16290209940303832072)
XLA Ops:
  0.7 4.0 %shard_map.84 = (f32[224,128]{1,0:T(8,128)S(1)}, f32[224,128]{1,0:T(8,128)S(1)}, f32[224,128]{1,0:T(8,128)S(1)}, f32[224,128]{1,0:T(8,128)S(1)}, f32[224,128]{1,...) custom-call(s32[3]{0:T(128)S(1)} %pad_add_fusion.place_ref, ...), custom_call_target="tpu_custom_call" | custom-call | flops 2038431744 | bytes 4194304 | tf_op jit(solution)/shard_map/pallas_call | solution.py:343
  4.9 0.5 collective-permute-start.3
  6.3 2.0 %collective-permute-start.2 = (f32[224,128]{1,0:T(8,128)S(1)}, f32[224,128]{1,0:T(8,128)S(1)}, u32[]{:S(2)}, u32[]{:S(2)}) collective-permute-start(f32[224,128]{1,0:T(8,128)S(1)} %add.53), channel_id=1, source_target_pairs={{0,2},{2,0},{4,6},{6,4},{8,10},{10,8},{12,14},{14,12},{16,18},{18,... | collective-permute-start | bytes 344072 | tf_op jit(solution)/shard_map/ppermute | solution.py:370
  8.3 1.3 %collective-permute-start.4 = (f32[224,128]{1,0:T(8,128)S(1)}, f32[224,128]{1,0:T(8,128)S(1)}, u32[]{:S(2)}, u32[]{:S(2)}) collective-permute-start(f32[224,128]{1,0:T(8,128)S(1)} %add.55), channel_id=1, source_target_pairs={{0,16},{2,18},{4,20},{6,22},{8,24},{10,26},{12,28},{14,30},{16,0},... | collective-permute-start | bytes 344072 | tf_op jit(solution)/shard_map/ppermute | solution.py:370
  9.6 0.5 collective-permute-start.6
  10.1 1.7 %collective-permute-done.2 = f32[224,128]{1,0:T(8,128)S(1)} collective-permute-done((f32[224,128]{1,0:T(8,128)S(1)}, f32[224,128]{1,0:T(8,128)S(1)}, u32[]{:S(2)}, u32[]{:S(2)}) %collective-permute-start.2) | collective-permute-done | bytes 114720 | tf_op jit(solution)/shard_map/ppermute | solution.py:370
  11.8 4.0 %collective-permute-done.4 = f32[224,128]{1,0:T(8,128)S(1)} collective-permute-done((f32[224,128]{1,0:T(8,128)S(1)}, f32[224,128]{1,0:T(8,128)S(1)}, u32[]{:S(2)}, u32[]{:S(2)}) %collective-permute-start.4) | collective-permute-done | bytes 114720 | tf_op jit(solution)/shard_map/ppermute | solution.py:370
  15.8 0.6 collective-permute-start.7
  16.4 4.3 %collective-permute-done.7 = f32[224,128]{1,0:T(8,128)S(1)} collective-permute-done((f32[224,128]{1,0:T(8,128)S(1)}, f32[224,128]{1,0:T(8,128)S(1)}, u32[]{:S(2)}, u32[]{:S(2)}) %collective-permute-start.7) | collective-permute-done | bytes 114720 | tf_op jit(solution)/shard_map/ppermute | solution.py:370
  20.7 5.5 %collective-permute-start.8 = (f32[224,128]{1,0:T(8,128)S(1)}, f32[224,128]{1,0:T(8,128)S(1)}, u32[]{:S(2)}, u32[]{:S(2)}) collective-permute-start(f32[224,128]{1,0:T(8,128)S(1)} %add.59), channel_id=1, source_target_pairs={{0,12},{2,14},{4,8},{6,10},{8,4},{10,6},{12,0},{14,2},{16,28},{18,... | collective-permute-start | bytes 344072 | tf_op jit(solution)/shard_map/ppermute | solution.py:370
  26.2 3.6 %collective-permute-done.8 = f32[224,128]{1,0:T(8,128)S(1)} collective-permute-done((f32[224,128]{1,0:T(8,128)S(1)}, f32[224,128]{1,0:T(8,128)S(1)}, u32[]{:S(2)}, u32[]{:S(2)}) %collective-permute-start.8) | collective-permute-done | bytes 114720 | tf_op jit(solution)/shard_map/ppermute | solution.py:370
  29.8 2.6 %collective-permute-start.9 = (f32[224,128]{1,0:T(8,128)S(1)}, f32[224,128]{1,0:T(8,128)S(1)}, u32[]{:S(2)}, u32[]{:S(2)}) collective-permute-start(f32[224,128]{1,0:T(8,128)S(1)} %add.60), channel_id=1, source_target_pairs={{0,4},{2,6},{4,0},{6,2},{8,12},{10,14},{12,8},{14,10},{16,20},{18,... | collective-permute-start | bytes 344072 | tf_op jit(solution)/shard_map/ppermute | solution.py:370
  32.3 3.8 %collective-permute-done.9 = f32[224,128]{1,0:T(8,128)S(1)} collective-permute-done((f32[224,128]{1,0:T(8,128)S(1)}, f32[224,128]{1,0:T(8,128)S(1)}, u32[]{:S(2)}, u32[]{:S(2)}) %collective-permute-start.9) | collective-permute-done | bytes 114720 | tf_op jit(solution)/shard_map/ppermute | solution.py:370
  36.2 2.0 %collective-permute-start.12 = (f32[224,128]{1,0:T(8,128)S(1)}, f32[224,128]{1,0:T(8,128)S(1)}, u32[]{:S(2)}, u32[]{:S(2)}) collective-permute-start(f32[224,128]{1,0:T(8,128)S(1)} %add.61.m0), channel_id=1, source_target_pairs={{0,2},{2,0},{4,6},{6,4},{8,10},{10,8},{12,14},{14,12},{16,18},{18,... | collective-permute-start | bytes 344072 | tf_op jit(solution)/shard_map/ppermute | solution.py:370
  38.1 2.6 %collective-permute-start.11 = (f32[224,128]{1,0:T(8,128)S(1)}, f32[224,128]{1,0:T(8,128)S(1)}, u32[]{:S(2)}, u32[]{:S(2)}) collective-permute-start(f32[224,128]{1,0:T(8,128)S(1)} %add.61.m0), channel_id=1, source_target_pairs={{0,16},{2,18},{4,20},{6,22},{8,24},{10,26},{12,28},{14,30},{16,0},... | collective-permute-start | bytes 344072 | tf_op jit(solution)/shard_map/ppermute | solution.py:370
  41.2 3.1 %collective-permute-done.11.m2 = f32[224,128]{1,0:T(8,128)S(1)} collective-permute-done((f32[224,128]{1,0:T(8,128)S(1)}, f32[224,128]{1,0:T(8,128)S(1)}, u32[]{:S(2)}, u32[]{:S(2)}) %collective-permute-start.11) | collective-permute-done | bytes 114720 | tf_op jit(solution)/shard_map/ppermute | solution.py:370
  44.3 2.1 %collective-permute-done.10.m1 = f32[224,128]{1,0:T(8,128)S(1)} collective-permute-done((f32[224,128]{1,0:T(8,128)S(1)}, f32[224,128]{1,0:T(8,128)S(1)}, u32[]{:S(2)}, u32[]{:S(2)}) %collective-permute-start.10) | collective-permute-done | bytes 114720 | tf_op jit(solution)/shard_map/ppermute | solution.py:370
  46.4 1.3 %collective-permute-done.14.o1 = f32[224,128]{1,0:T(8,128)S(1)} collective-permute-done((f32[224,128]{1,0:T(8,128)S(1)}, f32[224,128]{1,0:T(8,128)S(1)}, u32[]{:S(2)}, u32[]{:S(2)}) %collective-permute-start.14) | collective-permute-done | bytes 114720 | tf_op jit(solution)/shard_map/ppermute | solution.py:358
  47.8 4.1 %shard_map.85 = (bf16[2,384,384]{2,1,0:T(8,128)(2,1)S(1)}, bf16[2,2,256,256]{3,2,1,0:T(8,128)(2,1)S(1)}, f32[2,384]{1,0:T(2,128)S(1)}, f32[8,1664]{1,0:T(8,128)S(1)}) custom-call(s32[3]{0:T(128)S(1)} %pad_add_fusion.place_ref, f32[8]{0:T(128)S(1)} %copy-done.4, f32[384,1152]{1,0:T(8,128)S(1)} %copy-done, f32[384,384]{1,0:T(8,128)S(1)} %copy-done.3, ...), custom_call_target="tpu_custom_call" | custom-call | flops 2717908992 | bytes 4194304 | tf_op jit(solution)/shard_map/pallas_call | solution.py:383
  51.9 1.6 %collective-permute-start.19 = (f32[8,1664]{1,0:T(8,128)S(1)}, f32[8,1664]{1,0:T(8,128)S(1)}, u32[]{:S(2)}, u32[]{:S(2)}) collective-permute-start(f32[8,1664]{1,0:T(8,128)S(1)} %get-tuple-element.30.own_ref), channel_id=1, source_target_pairs={{0,64},{64,128},{128,192},{192,0},{1,65},{65,129},{129,193},{193,1... | collective-permute-start | bytes 159752 | tf_op jit(solution)/shard_map/ppermute | solution.py:362
  53.5 1.7 %collective-permute-start.18 = (f32[8,1664]{1,0:T(8,128)S(1)}, f32[8,1664]{1,0:T(8,128)S(1)}, u32[]{:S(2)}, u32[]{:S(2)}) collective-permute-start(f32[8,1664]{1,0:T(8,128)S(1)} %get-tuple-element.30.own_ref), channel_id=1, source_target_pairs={{0,192},{64,0},{128,64},{192,128},{1,193},{65,1},{129,65},{193,129... | collective-permute-start | bytes 159752 | tf_op jit(solution)/shard_map/ppermute | solution.py:362
  55.2 2.0 %collective-permute-start.17 = (f32[8,1664]{1,0:T(8,128)S(1)}, f32[8,1664]{1,0:T(8,128)S(1)}, u32[]{:S(2)}, u32[]{:S(2)}) collective-permute-start(f32[8,1664]{1,0:T(8,128)S(1)} %get-tuple-element.30.own_ref), channel_id=1, source_target_pairs={{0,128},{64,192},{128,0},{192,64},{1,129},{65,193},{129,1},{193,65... | collective-permute-start | bytes 159752 | tf_op jit(solution)/shard_map/ppermute | solution.py:362
  57.2 5.4 %shard_map.86 = f32[1024,384]{1,0:T(8,128)} custom-call(f32[1024,384]{1,0:T(8,128)S(1)} %bitcast.8, f32[1024,384]{1,0:T(8,128)S(1)} %bitcast.10, f32[384,1152]{1,0:T(8,128)S(1)} %copy-done, bf16[2,384,384]{2,1,0:T(8,128)(2,1)S(1)} %get-tuple-element.27.gv_ref, bf16[2,2,256,256]{3,2,1,0:T(8,128)(2,1)S(1)} %get-tuple-element.28.m_ref, ...), custom_call_target="tpu_custom_call" | custom-call | flops 4076863488 | bytes 4194304 | tf_op jit(solution)/shard_map/pallas_call | solution.py:400
  62.6 0.6 %shard_map.87 = (f32[6,1152]{1,0:T(8,128)}, f32[6,384]{1,0:T(8,128)}, f32[1,8]{1,0:T(1,128)}) custom-call(f32[8,1664]{1,0:T(8,128)S(1)} %get-tuple-element.30.own_ref, f32[8,1664]{1,0:T(8,128)S(1)} %collective-permute-done.17.two_ref, f32[8,1664]{1,0:T(8,128)S(1)} %collective-permute-done.18.three_ref, f32[8,1664]{1,0:T(8,128)S(1)} %collective-permute-done.19.one_ref), custom_call_target="tpu_custom_call" | custom-call | bytes 4194304 | tf_op jit(solution)/shard_map/pallas_call | solution.py:408
  (38 shorter events, 1.7 us)
Async XLA Ops:
  4.8 43.0 %copy-start = (f32[384,1152]{1,0:T(8,128)S(1)}, f32[384,1152]{1,0:T(8,128)}, u32[]{:S(2)}) copy-start(f32[384,1152]{1,0:T(8,128)} %w_ref.3) | copy-start | bytes 5308420
  4.8 42.9 %copy-start.3 = (f32[384,384]{1,0:T(8,128)S(1)}, f32[384,384]{1,0:T(8,128)}, u32[]{:S(2)}) copy-start(f32[384,384]{1,0:T(8,128)} %f_ref.1) | copy-start | bytes 1769476
  4.8 42.9 %copy-start.4 = (f32[8]{0:T(128)S(1)}, f32[8]{0:T(128)}, u32[]{:S(2)}) copy-start(f32[8]{0:T(128)} %sharp_ref.1) | copy-start | bytes 100
  4.8 1.4 %collective-permute-start.1 = (f32[224,128]{1,0:T(8,128)S(1)}, f32[224,128]{1,0:T(8,128)S(1)}, u32[]{:S(2)}, u32[]{:S(2)}) collective-permute-start(f32[224,128]{1,0:T(8,128)S(1)} %get-tuple-element.22), channel_id=1, source_target_pairs={{0,1},{1,0},{2,3},{3,2},{4,5},{5,4},{6,7},{7,6},{8,9},{9,8},{10,11... | collective-permute-start | bytes 344072 | tf_op jit(solution)/shard_map/ppermute | solution.py:358
  4.9 3.3 %collective-permute-start.3 = (f32[224,128]{1,0:T(8,128)S(1)}, f32[224,128]{1,0:T(8,128)S(1)}, u32[]{:S(2)}, u32[]{:S(2)}) collective-permute-start(f32[224,128]{1,0:T(8,128)S(1)} %get-tuple-element.24), channel_id=1, source_target_pairs={{0,1},{1,0},{2,3},{3,2},{4,5},{5,4},{6,7},{7,6},{8,9},{9,8},{10,11... | collective-permute-start | bytes 344072 | tf_op jit(solution)/shard_map/ppermute | solution.py:358
  5.4 4.2 %collective-permute-start.5 = (f32[224,128]{1,0:T(8,128)S(1)}, f32[224,128]{1,0:T(8,128)S(1)}, u32[]{:S(2)}, u32[]{:S(2)}) collective-permute-start(f32[224,128]{1,0:T(8,128)S(1)} %get-tuple-element.26), channel_id=1, source_target_pairs={{0,1},{1,0},{2,3},{3,2},{4,5},{5,4},{6,7},{7,6},{8,9},{9,8},{10,11... | collective-permute-start | bytes 344072 | tf_op jit(solution)/shard_map/ppermute | solution.py:358
  5.5 4.5 %collective-permute-start = (f32[224,128]{1,0:T(8,128)S(1)}, f32[224,128]{1,0:T(8,128)S(1)}, u32[]{:S(2)}, u32[]{:S(2)}) collective-permute-start(f32[224,128]{1,0:T(8,128)S(1)} %get-tuple-element.20), channel_id=1, source_target_pairs={{0,1},{1,0},{2,3},{3,2},{4,5},{5,4},{6,7},{7,6},{8,9},{9,8},{10,11... | collective-permute-start | bytes 344072 | tf_op jit(solution)/shard_map/ppermute | solution.py:358
  6.3 5.5 %collective-permute-start.2 = (f32[224,128]{1,0:T(8,128)S(1)}, f32[224,128]{1,0:T(8,128)S(1)}, u32[]{:S(2)}, u32[]{:S(2)}) collective-permute-start(f32[224,128]{1,0:T(8,128)S(1)} %add.53), channel_id=1, source_target_pairs={{0,2},{2,0},{4,6},{6,4},{8,10},{10,8},{12,14},{14,12},{16,18},{18,... | collective-permute-start | bytes 344072 | tf_op jit(solution)/shard_map/ppermute | solution.py:370
  8.3 7.5 %collective-permute-start.4 = (f32[224,128]{1,0:T(8,128)S(1)}, f32[224,128]{1,0:T(8,128)S(1)}, u32[]{:S(2)}, u32[]{:S(2)}) collective-permute-start(f32[224,128]{1,0:T(8,128)S(1)} %add.55), channel_id=1, source_target_pairs={{0,16},{2,18},{4,20},{6,22},{8,24},{10,26},{12,28},{14,30},{16,0},... | collective-permute-start | bytes 344072 | tf_op jit(solution)/shard_map/ppermute | solution.py:370
  9.6 6.2 %collective-permute-start.6 = (f32[224,128]{1,0:T(8,128)S(1)}, f32[224,128]{1,0:T(8,128)S(1)}, u32[]{:S(2)}, u32[]{:S(2)}) collective-permute-start(f32[224,128]{1,0:T(8,128)S(1)} %add.56), channel_id=1, source_target_pairs={{0,18},{2,16},{4,22},{6,20},{8,26},{10,24},{12,30},{14,28},{16,2},... | collective-permute-start | bytes 344072 | tf_op jit(solution)/shard_map/ppermute | solution.py:370
  15.8 4.9 %collective-permute-start.7 = (f32[224,128]{1,0:T(8,128)S(1)}, f32[224,128]{1,0:T(8,128)S(1)}, u32[]{:S(2)}, u32[]{:S(2)}) collective-permute-start(f32[224,128]{1,0:T(8,128)S(1)} %add_add_fusion), channel_id=1, source_target_pairs={{0,48},{2,50},{4,52},{6,54},{8,56},{10,58},{12,60},{14,62},{16,32}... | collective-permute-start | bytes 344072 | tf_op jit(solution)/shard_map/ppermute | solution.py:370
  20.7 9.1 %collective-permute-start.8 = (f32[224,128]{1,0:T(8,128)S(1)}, f32[224,128]{1,0:T(8,128)S(1)}, u32[]{:S(2)}, u32[]{:S(2)}) collective-permute-start(f32[224,128]{1,0:T(8,128)S(1)} %add.59), channel_id=1, source_target_pairs={{0,12},{2,14},{4,8},{6,10},{8,4},{10,6},{12,0},{14,2},{16,28},{18,... | collective-permute-start | bytes 344072 | tf_op jit(solution)/shard_map/ppermute | solution.py:370
  29.8 6.4 %collective-permute-start.9 = (f32[224,128]{1,0:T(8,128)S(1)}, f32[224,128]{1,0:T(8,128)S(1)}, u32[]{:S(2)}, u32[]{:S(2)}) collective-permute-start(f32[224,128]{1,0:T(8,128)S(1)} %add.60), channel_id=1, source_target_pairs={{0,4},{2,6},{4,0},{6,2},{8,12},{10,14},{12,8},{14,10},{16,20},{18,... | collective-permute-start | bytes 344072 | tf_op jit(solution)/shard_map/ppermute | solution.py:370
  36.1 21.0 %copy-start.1 = (f32[1,1024,384]{2,1,0:T(8,128)S(1)}, f32[1,1024,384]{2,1,0:T(8,128)}, u32[]{:S(2)}) copy-start(f32[1,1024,384]{2,1,0:T(8,128)} %param.5) | copy-start | bytes 4718596
  36.2 4.9 %collective-permute-start.12 = (f32[224,128]{1,0:T(8,128)S(1)}, f32[224,128]{1,0:T(8,128)S(1)}, u32[]{:S(2)}, u32[]{:S(2)}) collective-permute-start(f32[224,128]{1,0:T(8,128)S(1)} %add.61.m0), channel_id=1, source_target_pairs={{0,2},{2,0},{4,6},{6,4},{8,10},{10,8},{12,14},{14,12},{16,18},{18,... | collective-permute-start | bytes 344072 | tf_op jit(solution)/shard_map/ppermute | solution.py:370
  38.1 6.2 %collective-permute-start.11 = (f32[224,128]{1,0:T(8,128)S(1)}, f32[224,128]{1,0:T(8,128)S(1)}, u32[]{:S(2)}, u32[]{:S(2)}) collective-permute-start(f32[224,128]{1,0:T(8,128)S(1)} %add.61.m0), channel_id=1, source_target_pairs={{0,16},{2,18},{4,20},{6,22},{8,24},{10,26},{12,28},{14,30},{16,0},... | collective-permute-start | bytes 344072 | tf_op jit(solution)/shard_map/ppermute | solution.py:370
  40.7 5.7 %collective-permute-start.10 = (f32[224,128]{1,0:T(8,128)S(1)}, f32[224,128]{1,0:T(8,128)S(1)}, u32[]{:S(2)}, u32[]{:S(2)}) collective-permute-start(f32[224,128]{1,0:T(8,128)S(1)} %add.61.m0), channel_id=1, source_target_pairs={{0,18},{2,16},{4,22},{6,20},{8,26},{10,24},{12,30},{14,28},{16,2},... | collective-permute-start | bytes 344072 | tf_op jit(solution)/shard_map/ppermute | solution.py:370
  40.7 5.7 %collective-permute-start.13 = (f32[224,128]{1,0:T(8,128)S(1)}, f32[224,128]{1,0:T(8,128)S(1)}, u32[]{:S(2)}, u32[]{:S(2)}) collective-permute-start(f32[224,128]{1,0:T(8,128)S(1)} %add.61.m0), channel_id=1, source_target_pairs={{0,1},{1,0},{2,3},{3,2},{4,5},{5,4},{6,7},{7,6},{8,9},{9,8},{10,11... | collective-permute-start | bytes 344072 | tf_op jit(solution)/shard_map/ppermute | solution.py:358
  41.1 5.4 %collective-permute-start.16 = (f32[224,128]{1,0:T(8,128)S(1)}, f32[224,128]{1,0:T(8,128)S(1)}, u32[]{:S(2)}, u32[]{:S(2)}) collective-permute-start(f32[224,128]{1,0:T(8,128)S(1)} %collective-permute-done.12.m3), channel_id=1, source_target_pairs={{0,1},{1,0},{2,3},{3,2},{4,5},{5,4},{6,7},{7,6},{8,9},{9,8},{10,11... | collective-permute-start | bytes 344072 | tf_op jit(solution)/shard_map/ppermute | solution.py:358
  44.3 2.1 %collective-permute-start.15 = (f32[224,128]{1,0:T(8,128)S(1)}, f32[224,128]{1,0:T(8,128)S(1)}, u32[]{:S(2)}, u32[]{:S(2)}) collective-permute-start(f32[224,128]{1,0:T(8,128)S(1)} %collective-permute-done.11.m2), channel_id=1, source_target_pairs={{0,1},{1,0},{2,3},{3,2},{4,5},{5,4},{6,7},{7,6},{8,9},{9,8},{10,11... | collective-permute-start | bytes 344072 | tf_op jit(solution)/shard_map/ppermute | solution.py:358
  46.4 1.3 %collective-permute-start.14 = (f32[224,128]{1,0:T(8,128)S(1)}, f32[224,128]{1,0:T(8,128)S(1)}, u32[]{:S(2)}, u32[]{:S(2)}) collective-permute-start(f32[224,128]{1,0:T(8,128)S(1)} %collective-permute-done.10.m1), channel_id=1, source_target_pairs={{0,1},{1,0},{2,3},{3,2},{4,5},{5,4},{6,7},{7,6},{8,9},{9,8},{10,11... | collective-permute-start | bytes 344072 | tf_op jit(solution)/shard_map/ppermute | solution.py:358
  51.9 10.7 %collective-permute-start.19 = (f32[8,1664]{1,0:T(8,128)S(1)}, f32[8,1664]{1,0:T(8,128)S(1)}, u32[]{:S(2)}, u32[]{:S(2)}) collective-permute-start(f32[8,1664]{1,0:T(8,128)S(1)} %get-tuple-element.30.own_ref), channel_id=1, source_target_pairs={{0,64},{64,128},{128,192},{192,0},{1,65},{65,129},{129,193},{193,1... | collective-permute-start | bytes 159752 | tf_op jit(solution)/shard_map/ppermute | solution.py:362
  53.5 9.1 %collective-permute-start.18 = (f32[8,1664]{1,0:T(8,128)S(1)}, f32[8,1664]{1,0:T(8,128)S(1)}, u32[]{:S(2)}, u32[]{:S(2)}) collective-permute-start(f32[8,1664]{1,0:T(8,128)S(1)} %get-tuple-element.30.own_ref), channel_id=1, source_target_pairs={{0,192},{64,0},{128,64},{192,128},{1,193},{65,1},{129,65},{193,129... | collective-permute-start | bytes 159752 | tf_op jit(solution)/shard_map/ppermute | solution.py:362
  55.2 7.4 %collective-permute-start.17 = (f32[8,1664]{1,0:T(8,128)S(1)}, f32[8,1664]{1,0:T(8,128)S(1)}, u32[]{:S(2)}, u32[]{:S(2)}) collective-permute-start(f32[8,1664]{1,0:T(8,128)S(1)} %get-tuple-element.30.own_ref), channel_id=1, source_target_pairs={{0,128},{64,192},{128,0},{192,64},{1,129},{65,193},{129,1},{193,65... | collective-permute-start | bytes 159752 | tf_op jit(solution)/shard_map/ppermute | solution.py:362
  (1 other events, 21.0 us)
